TPU v7x, 32 devices: a whole 2x2x4 slice. The times are simulated.
32 devices in a mesh: seq: 16 (over z, y, x), wa: 2 (over core).
Axes of the slice: x: 2, y: 2, z: 4, core: 2. Of those that a mesh axis runs over, the one named last changes fastest.
Arguments:
- stream: bfloat16 [2, 49152, 800], P('wa', 'seq'), may hold values from -6 to 6
- doc_start: int32 [2, 49152], P('wa', 'seq'), may hold values from 0 to 49151, as said below
- doc_end: int32 [2, 49152], P('wa', 'seq'), may hold values from 1 to 49152, as said below
- cotangent: bfloat16 [2, 49152, 800], P('wa', 'seq'), may hold values from -6 to 6
- encoder_first_gain: bfloat16 [800], P('wa'), may hold values from 0.25 to 1.75
- encoder_first_bias: bfloat16 [800], P('wa'), may hold values from -3 to 3
- encoder_reduce_weight: bfloat16 [800, 400], P(None, 'wa'), may hold values from -0.21875 to 0.21875
- encoder_reduce_bias: bfloat16 [400], P('wa'), may hold values from -3 to 3
- encoder_middle_gain: bfloat16 [400], P('wa'), may hold values from 0.25 to 1.75
- encoder_middle_bias: bfloat16 [400], P('wa'), may hold values from -3 to 3
- encoder_conv_kernel: bfloat16 [5, 400, 400], P(None, 'wa'), may hold values from -0.125 to 0.125
- encoder_conv_bias: bfloat16 [400], P('wa'), may hold values from -3 to 3
- encoder_last_gain: bfloat16 [400], P('wa'), may hold values from 0.25 to 1.75
- encoder_last_bias: bfloat16 [400], P('wa'), may hold values from -3 to 3
- encoder_expand_weight: bfloat16 [400, 800], P('wa'), may hold values from -0.3125 to 0.3125
- encoder_expand_bias: bfloat16 [800], P('wa'), may hold values from -3 to 3
- decoder_first_gain: bfloat16 [800], P('wa'), may hold values from 0.25 to 1.75
- decoder_first_bias: bfloat16 [800], P('wa'), may hold values from -3 to 3
- decoder_reduce_weight: bfloat16 [800, 400], P(None, 'wa'), may hold values from -0.21875 to 0.21875
- decoder_reduce_bias: bfloat16 [400], P('wa'), may hold values from -3 to 3
- decoder_middle_gain: bfloat16 [400], P('wa'), may hold values from 0.25 to 1.75
- decoder_middle_bias: bfloat16 [400], P('wa'), may hold values from -3 to 3
- decoder_conv_kernel: bfloat16 [3, 400, 400], P(None, 'wa'), may hold values from -0.1875 to 0.1875
- decoder_conv_bias: bfloat16 [400], P('wa'), may hold values from -3 to 3
- decoder_last_gain: bfloat16 [400], P('wa'), may hold values from 0.25 to 1.75
- decoder_last_bias: bfloat16 [400], P('wa'), may hold values from -3 to 3
- decoder_expand_weight: bfloat16 [400, 800], P('wa'), may hold values from -0.3125 to 0.3125
- decoder_expand_bias: bfloat16 [800], P('wa'), may hold values from -3 to 3
Outputs:
- block_out: float32 [2, 49152, 800], P('wa', 'seq')
- stream_grad: float32 [2, 49152, 800], P('wa', 'seq')
- encoder_first_gain_grad: float32 [800], P('wa')
- encoder_first_bias_grad: float32 [800], P('wa')
- encoder_reduce_weight_grad: float32 [800, 400], P(None, 'wa')
- encoder_reduce_bias_grad: float32 [400], P('wa')
- encoder_middle_gain_grad: float32 [400], P('wa')
- encoder_middle_bias_grad: float32 [400], P('wa')
- encoder_conv_kernel_grad: float32 [5, 400, 400], P(None, 'wa')
- encoder_conv_bias_grad: float32 [400], P('wa')
- encoder_last_gain_grad: float32 [400], P('wa')
- encoder_last_bias_grad: float32 [400], P('wa')
- encoder_expand_weight_grad: float32 [400, 800], P('wa')
- encoder_expand_bias_grad: float32 [800], P('wa')
- decoder_first_gain_grad: float32 [800], P('wa')
- decoder_first_bias_grad: float32 [800], P('wa')
- decoder_reduce_weight_grad: float32 [800, 400], P(None, 'wa')
- decoder_reduce_bias_grad: float32 [400], P('wa')
- decoder_middle_gain_grad: float32 [400], P('wa')
- decoder_middle_bias_grad: float32 [400], P('wa')
- decoder_conv_kernel_grad: float32 [3, 400, 400], P(None, 'wa')
- decoder_conv_bias_grad: float32 [400], P('wa')
- decoder_last_gain_grad: float32 [400], P('wa')
- decoder_last_bias_grad: float32 [400], P('wa')
- decoder_expand_weight_grad: float32 [400, 800], P('wa')
- decoder_expand_bias_grad: float32 [800], P('wa')
Inputs may be any that keep to these rules, and one draw needn't show every extreme that they name: Documents are contiguous runs of positions within a stream; every position's doc_start is the first position of its run. Each stream holds two documents of exactly 4096 characters and otherwise short ones; positions 0 and 49151 are each a document of one character. doc_end is one past the last position of the same run as doc_start, so doc_start[p] <= p < doc_end[p].
All inputs are finite; a program needn't handle non-finite values.
Results may differ from a plain program's by a relative error of at most 0.014.
Values may be sent and summed in bfloat16 or wider, within the bound.
A program may use at most 256 MiB of HBM per device.

v0:
```python
import jax
import jax.numpy as jnp
from jax import lax
from jax.sharding import PartitionSpec as P

ENCODER_TAPS = 5
ENCODER_DILATION = 8
DECODER_TAPS = 3
DECODER_DILATION = 16


EPS = 1e-05


def extended(array, sides, width):
    for axis, dim in sides:
        size, length = (lax.axis_size(axis), array.shape[dim])
        up = [(i, (i + 1) % size) for i in range(size - 1)]
        down = [(j, i) for i, j in up]
        last = lax.slice_in_dim(array, length - width, length, axis=dim)
        initial = lax.slice_in_dim(array, 0, width, axis=dim)
        before = lax.ppermute(last, axis, up)
        after = lax.ppermute(initial, axis, down)
        array = jnp.concatenate([before, array, after], axis=dim)
    return array


def passed_along(array, axis, by):
    size = lax.axis_size(axis)
    pairs = [(i, i + by) for i in range(size) if 0 <= i + by < size]
    return lax.ppermute(array, axis, pairs)


def norm_act(value, gain, bias):
    centre = value - jnp.mean(value, axis=-1, keepdims=True)
    spread = jnp.mean(centre * centre, axis=-1, keepdims=True)
    return jax.nn.gelu(centre * lax.rsqrt(spread + EPS) * gain + bias)


def usable_rows(starts, ends, base, offset):
    source = base + jnp.arange(starts.shape[0], dtype=jnp.int32) + offset
    return (source >= starts) & (source < ends)


def contract_rows(left, right):
    return lax.dot_general(
        left, right, (((0,), (0,)), ((), ())), preferred_element_type=jnp.float32
    )


def contract_cols(left, right):
    return lax.dot_general(
        left, right, (((1,), (1,)), ((), ())), preferred_element_type=jnp.float32
    )


def tap_offsets(encoder):
    if encoder:
        return (
            [
                ENCODER_DILATION * (tap_index - ENCODER_TAPS // 2)
                for tap_index in range(ENCODER_TAPS)
            ],
            ENCODER_DILATION * (ENCODER_TAPS // 2),
        )
    return (
        [-DECODER_DILATION * (DECODER_TAPS - 1 - tap_index) for tap_index in range(DECODER_TAPS)],
        DECODER_DILATION * (DECODER_TAPS - 1),
    )


def forward_block(value, weights, starts, ends, base, encoder):
    (
        first_gain,
        first_bias,
        reduce_weight,
        reduce_bias,
        middle_gain,
        middle_bias,
        conv_kernel,
        conv_bias,
        last_gain,
        last_bias,
        expand_weight,
        expand_bias,
    ) = weights
    length = value.shape[0]
    first = norm_act(value, first_gain.astype(jnp.float32), first_bias.astype(jnp.float32)).astype(
        jnp.bfloat16
    )
    inner = jnp.dot(first, reduce_weight, preferred_element_type=jnp.float32) + reduce_bias.astype(
        jnp.float32
    )
    middle = norm_act(
        inner, middle_gain.astype(jnp.float32), middle_bias.astype(jnp.float32)
    ).astype(jnp.bfloat16)
    offsets, reach = tap_offsets(encoder)
    if encoder:
        padded = extended(middle, (("seq", 0),), reach)
    else:
        before = passed_along(middle[length - reach :], "seq", 1)
        padded = jnp.concatenate([before, middle], axis=0)
    pieces = []
    for offset in offsets:
        usable = usable_rows(starts, ends, base, offset)
        pieces.append(
            jnp.where(usable[:, None], padded[reach + offset : reach + offset + length], 0)
        )
    stacked = jnp.concatenate(pieces, axis=1)
    flat_kernel = conv_kernel.reshape(len(offsets) * conv_kernel.shape[1], conv_kernel.shape[2])
    mixed = jnp.dot(stacked, flat_kernel, preferred_element_type=jnp.float32) + conv_bias.astype(
        jnp.float32
    )
    last = norm_act(mixed, last_gain.astype(jnp.float32), last_bias.astype(jnp.float32)).astype(
        jnp.bfloat16
    )
    branch = jnp.dot(last, expand_weight, preferred_element_type=jnp.float32) + expand_bias.astype(
        jnp.float32
    )
    return (value + branch, (value, first, inner, stacked, mixed, last))


def backward_block(upstream, weights, kept, starts, ends, base, encoder):
    (
        first_gain,
        first_bias,
        reduce_weight,
        reduce_bias,
        middle_gain,
        middle_bias,
        conv_kernel,
        conv_bias,
        last_gain,
        last_bias,
        expand_weight,
        expand_bias,
    ) = weights
    value, first, inner, stacked, mixed, last = kept
    length = value.shape[0]
    branch_grad = upstream.astype(jnp.bfloat16)
    expand_weight_grad = contract_rows(last, branch_grad)
    expand_bias_grad = jnp.sum(branch_grad.astype(jnp.float32), axis=0)
    last_grad = contract_cols(branch_grad, expand_weight)
    unused, pull = jax.vjp(
        norm_act, mixed, last_gain.astype(jnp.float32), last_bias.astype(jnp.float32)
    )
    mixed_grad, last_gain_grad, last_bias_grad = pull(last_grad)
    mixed_low = mixed_grad.astype(jnp.bfloat16)
    conv_bias_grad = jnp.sum(mixed_low.astype(jnp.float32), axis=0)
    conv_kernel_grad = contract_rows(stacked, mixed_low).reshape(conv_kernel.shape)
    offsets, reach = tap_offsets(encoder)
    if encoder:
        padded = extended(mixed_low, (("seq", 0),), reach)
        lead = reach
    else:
        after = passed_along(mixed_low[:reach], "seq", -1)
        padded = jnp.concatenate([mixed_low, after], axis=0)
        lead = 0
    pieces = []
    for offset in offsets:
        usable = usable_rows(starts, ends, base, -offset)
        pieces.append(jnp.where(usable[:, None], padded[lead - offset : lead - offset + length], 0))
    back_stacked = jnp.concatenate(pieces, axis=1)
    turned = jnp.transpose(conv_kernel, (0, 2, 1)).reshape(
        len(offsets) * conv_kernel.shape[2], conv_kernel.shape[1]
    )
    middle_grad = jnp.dot(back_stacked, turned, preferred_element_type=jnp.float32)
    unused, pull = jax.vjp(
        norm_act, inner, middle_gain.astype(jnp.float32), middle_bias.astype(jnp.float32)
    )
    inner_grad, middle_gain_grad, middle_bias_grad = pull(middle_grad)
    inner_low = inner_grad.astype(jnp.bfloat16)
    reduce_bias_grad = jnp.sum(inner_low.astype(jnp.float32), axis=0)
    reduce_weight_grad = contract_rows(first, inner_low)
    first_grad = contract_cols(inner_low, reduce_weight)
    unused, pull = jax.vjp(
        norm_act, value, first_gain.astype(jnp.float32), first_bias.astype(jnp.float32)
    )
    value_grad, first_gain_grad, first_bias_grad = pull(first_grad)
    grads = (
        first_gain_grad,
        first_bias_grad,
        reduce_weight_grad,
        reduce_bias_grad,
        middle_gain_grad,
        middle_bias_grad,
        conv_kernel_grad,
        conv_bias_grad,
        last_gain_grad,
        last_bias_grad,
        expand_weight_grad,
        expand_bias_grad,
    )
    return (upstream + value_grad, grads)


def local(
    stream,
    doc_start,
    doc_end,
    cotangent,
    encoder_first_gain,
    encoder_first_bias,
    encoder_reduce_weight,
    encoder_reduce_bias,
    encoder_middle_gain,
    encoder_middle_bias,
    encoder_conv_kernel,
    encoder_conv_bias,
    encoder_last_gain,
    encoder_last_bias,
    encoder_expand_weight,
    encoder_expand_bias,
    decoder_first_gain,
    decoder_first_bias,
    decoder_reduce_weight,
    decoder_reduce_bias,
    decoder_middle_gain,
    decoder_middle_bias,
    decoder_conv_kernel,
    decoder_conv_bias,
    decoder_last_gain,
    decoder_last_bias,
    decoder_expand_weight,
    decoder_expand_bias,
):
    gathered = (
        lax.all_gather(encoder_first_gain, "wa", axis=0, tiled=True),
        lax.all_gather(encoder_first_bias, "wa", axis=0, tiled=True),
        lax.all_gather(encoder_reduce_weight, "wa", axis=1, tiled=True),
        lax.all_gather(encoder_reduce_bias, "wa", axis=0, tiled=True),
        lax.all_gather(encoder_middle_gain, "wa", axis=0, tiled=True),
        lax.all_gather(encoder_middle_bias, "wa", axis=0, tiled=True),
        lax.all_gather(encoder_conv_kernel, "wa", axis=1, tiled=True),
        lax.all_gather(encoder_conv_bias, "wa", axis=0, tiled=True),
        lax.all_gather(encoder_last_gain, "wa", axis=0, tiled=True),
        lax.all_gather(encoder_last_bias, "wa", axis=0, tiled=True),
        lax.all_gather(encoder_expand_weight, "wa", axis=0, tiled=True),
        lax.all_gather(encoder_expand_bias, "wa", axis=0, tiled=True),
        lax.all_gather(decoder_first_gain, "wa", axis=0, tiled=True),
        lax.all_gather(decoder_first_bias, "wa", axis=0, tiled=True),
        lax.all_gather(decoder_reduce_weight, "wa", axis=1, tiled=True),
        lax.all_gather(decoder_reduce_bias, "wa", axis=0, tiled=True),
        lax.all_gather(decoder_middle_gain, "wa", axis=0, tiled=True),
        lax.all_gather(decoder_middle_bias, "wa", axis=0, tiled=True),
        lax.all_gather(decoder_conv_kernel, "wa", axis=1, tiled=True),
        lax.all_gather(decoder_conv_bias, "wa", axis=0, tiled=True),
        lax.all_gather(decoder_last_gain, "wa", axis=0, tiled=True),
        lax.all_gather(decoder_last_bias, "wa", axis=0, tiled=True),
        lax.all_gather(decoder_expand_weight, "wa", axis=0, tiled=True),
        lax.all_gather(decoder_expand_bias, "wa", axis=0, tiled=True),
    )
    encoder_weights = gathered[:12]
    decoder_weights = gathered[12:]
    value = stream[0].astype(jnp.float32)
    starts = doc_start[0]
    ends = doc_end[0]
    base = lax.axis_index("seq") * value.shape[0]
    between, encoder_kept = forward_block(value, encoder_weights, starts, ends, base, True)
    result, decoder_kept = forward_block(between, decoder_weights, starts, ends, base, False)
    between_grad, decoder_grads = backward_block(
        cotangent[0].astype(jnp.float32), decoder_weights, decoder_kept, starts, ends, base, False
    )
    value_grad, encoder_grads = backward_block(
        between_grad, encoder_weights, encoder_kept, starts, ends, base, True
    )
    (
        grad_efg,
        grad_efb,
        grad_erw,
        grad_erb,
        grad_emg,
        grad_emb,
        grad_eck,
        grad_ecb,
        grad_elg,
        grad_elb,
        grad_eew,
        grad_eeb,
    ) = encoder_grads
    (
        grad_dfg,
        grad_dfb,
        grad_drw,
        grad_drb,
        grad_dmg,
        grad_dmb,
        grad_dck,
        grad_dcb,
        grad_dlg,
        grad_dlb,
        grad_dew,
        grad_deb,
    ) = decoder_grads
    summed = lax.psum(
        (
            grad_efg,
            grad_efb,
            grad_erw,
            grad_erb,
            grad_emg,
            grad_emb,
            grad_eck,
            grad_ecb,
            grad_elg,
            grad_elb,
            grad_eew,
            grad_eeb,
            grad_dfg,
            grad_dfb,
            grad_drw,
            grad_drb,
            grad_dmg,
            grad_dmb,
            grad_dck,
            grad_dcb,
            grad_dlg,
            grad_dlb,
            grad_dew,
            grad_deb,
        ),
        "seq",
    )
    (
        whole_efg,
        whole_efb,
        whole_erw,
        whole_erb,
        whole_emg,
        whole_emb,
        whole_eck,
        whole_ecb,
        whole_elg,
        whole_elb,
        whole_eew,
        whole_eeb,
        whole_dfg,
        whole_dfb,
        whole_drw,
        whole_drb,
        whole_dmg,
        whole_dmb,
        whole_dck,
        whole_dcb,
        whole_dlg,
        whole_dlb,
        whole_dew,
        whole_deb,
    ) = summed
    shares = (
        lax.psum_scatter(
            whole_efg.astype(jnp.bfloat16), "wa", scatter_dimension=0, tiled=True
        ).astype(jnp.float32),
        lax.psum_scatter(
            whole_efb.astype(jnp.bfloat16), "wa", scatter_dimension=0, tiled=True
        ).astype(jnp.float32),
        lax.psum_scatter(
            whole_erw.astype(jnp.bfloat16), "wa", scatter_dimension=1, tiled=True
        ).astype(jnp.float32),
        lax.psum_scatter(
            whole_erb.astype(jnp.bfloat16), "wa", scatter_dimension=0, tiled=True
        ).astype(jnp.float32),
        lax.psum_scatter(
            whole_emg.astype(jnp.bfloat16), "wa", scatter_dimension=0, tiled=True
        ).astype(jnp.float32),
        lax.psum_scatter(
            whole_emb.astype(jnp.bfloat16), "wa", scatter_dimension=0, tiled=True
        ).astype(jnp.float32),
        lax.psum_scatter(
            whole_eck.astype(jnp.bfloat16), "wa", scatter_dimension=1, tiled=True
        ).astype(jnp.float32),
        lax.psum_scatter(
            whole_ecb.astype(jnp.bfloat16), "wa", scatter_dimension=0, tiled=True
        ).astype(jnp.float32),
        lax.psum_scatter(
            whole_elg.astype(jnp.bfloat16), "wa", scatter_dimension=0, tiled=True
        ).astype(jnp.float32),
        lax.psum_scatter(
            whole_elb.astype(jnp.bfloat16), "wa", scatter_dimension=0, tiled=True
        ).astype(jnp.float32),
        lax.psum_scatter(
            whole_eew.astype(jnp.bfloat16), "wa", scatter_dimension=0, tiled=True
        ).astype(jnp.float32),
        lax.psum_scatter(
            whole_eeb.astype(jnp.bfloat16), "wa", scatter_dimension=0, tiled=True
        ).astype(jnp.float32),
        lax.psum_scatter(
            whole_dfg.astype(jnp.bfloat16), "wa", scatter_dimension=0, tiled=True
        ).astype(jnp.float32),
        lax.psum_scatter(
            whole_dfb.astype(jnp.bfloat16), "wa", scatter_dimension=0, tiled=True
        ).astype(jnp.float32),
        lax.psum_scatter(
            whole_drw.astype(jnp.bfloat16), "wa", scatter_dimension=1, tiled=True
        ).astype(jnp.float32),
        lax.psum_scatter(
            whole_drb.astype(jnp.bfloat16), "wa", scatter_dimension=0, tiled=True
        ).astype(jnp.float32),
        lax.psum_scatter(
            whole_dmg.astype(jnp.bfloat16), "wa", scatter_dimension=0, tiled=True
        ).astype(jnp.float32),
        lax.psum_scatter(
            whole_dmb.astype(jnp.bfloat16), "wa", scatter_dimension=0, tiled=True
        ).astype(jnp.float32),
        lax.psum_scatter(
            whole_dck.astype(jnp.bfloat16), "wa", scatter_dimension=1, tiled=True
        ).astype(jnp.float32),
        lax.psum_scatter(
            whole_dcb.astype(jnp.bfloat16), "wa", scatter_dimension=0, tiled=True
        ).astype(jnp.float32),
        lax.psum_scatter(
            whole_dlg.astype(jnp.bfloat16), "wa", scatter_dimension=0, tiled=True
        ).astype(jnp.float32),
        lax.psum_scatter(
            whole_dlb.astype(jnp.bfloat16), "wa", scatter_dimension=0, tiled=True
        ).astype(jnp.float32),
        lax.psum_scatter(
            whole_dew.astype(jnp.bfloat16), "wa", scatter_dimension=0, tiled=True
        ).astype(jnp.float32),
        lax.psum_scatter(
            whole_deb.astype(jnp.bfloat16), "wa", scatter_dimension=0, tiled=True
        ).astype(jnp.float32),
    )
    return (result[None], value_grad[None], *shares)


def solution(mesh):
    in_specs = (
        P("wa", "seq", None),
        P("wa", "seq"),
        P("wa", "seq"),
        P("wa", "seq", None),
        P("wa"),
        P("wa"),
        P(None, "wa"),
        P("wa"),
        P("wa"),
        P("wa"),
        P(None, "wa", None),
        P("wa"),
        P("wa"),
        P("wa"),
        P("wa", None),
        P("wa"),
        P("wa"),
        P("wa"),
        P(None, "wa"),
        P("wa"),
        P("wa"),
        P("wa"),
        P(None, "wa", None),
        P("wa"),
        P("wa"),
        P("wa"),
        P("wa", None),
        P("wa"),
    )
    out_specs = (
        P("wa", "seq", None),
        P("wa", "seq", None),
        P("wa"),
        P("wa"),
        P(None, "wa"),
        P("wa"),
        P("wa"),
        P("wa"),
        P(None, "wa", None),
        P("wa"),
        P("wa"),
        P("wa"),
        P("wa", None),
        P("wa"),
        P("wa"),
        P("wa"),
        P(None, "wa"),
        P("wa"),
        P("wa"),
        P("wa"),
        P(None, "wa", None),
        P("wa"),
        P("wa"),
        P("wa"),
        P("wa", None),
        P("wa"),
    )
    return jax.shard_map(local, mesh=mesh, in_specs=in_specs, out_specs=out_specs, check_vma=False)
```

profile of v0, /device:TPU:0, one launch (start us, length us, event | category | flops | bytes accessed | tf_op | source)
XLA Modules:
  0.0 943.6 jit_solution(16776876127185316949)
XLA Ops:
  25.1 4.3 all-reduce.42
  29.5 3.4 convert_reduce_fusion.1
  37.9 5.6 fusion.14
  52.2 5.2 collective-permute-start
  59.9 5.4 all_gather.90
  66.6 4.9 all_gather.86
  84.8 4.1 select_dynamic-update-slice_fusion.1
  88.8 2.9 fusion.82
  91.8 2.9 fusion.93
  94.7 9.3 add_reduce_fusion.2
  105.0 5.0 fusion.150
  113.9 5.2 multiply_convert_fusion
  122.9 4.3 broadcast_select_fusion.1
  127.3 4.8 collective-permute-start.2
  137.1 4.1 copy.61
  143.3 3.7 add_reduce_fusion
  147.9 5.4 fusion.60
  153.3 7.5 fusion.139
  160.8 2.9 multiply_reduce_fusion.3
  163.8 3.5 convert_reduce_fusion.3
  168.9 5.5 fusion.66
  174.4 3.4 fusion.77
  177.8 8.6 fusion.140
  186.5 2.9 multiply_reduce_fusion.4
  192.1 14.7 %multiply_reduce_fusion = (f32[800]{0:T(1024)S(1)}, f32[3072]{0:T(1024)S(1)}, f32[800]{0:T(1024)S(1)}, f32[3072,800]{0,1:T(8,128)}) fusion(f32[3072,800]{0,1:T(8,128)S(1)} %bitcast.142, f32[3072]{0:T(1024)S(1)} %fusion.127, f32[3072]{0:T(1024)S(1)} %broadcast_multiply_fusion.4, f32[800]{0:T(1024)S(1)} %copy-done.61, f32[800]{0:T(1024)S(1)} %copy-done.82, ...), kind=kOutput, calls=%fused_computation.39 | convolution fusion | flops 2037345792 | bytes 22808064 | tf_op jit(solution)/shard_map/dot_general | solution.py:52
  206.8 14.2 %fusion.146 = (f32[3072]{0:T(1024)S(1)}, f32[3072,800]{0,1:T(8,128)}) fusion(f32[3072]{0:T(1024)S(1)} %multiply_multiply_fusion.15, f32[3072,800]{0,1:T(8,128)} %copy-done.2, f32[3072]{0:T(1024)S(1)} %broadcast_multiply_fusion.4, f32[3072]{0:T(1024)S(1)} %fusion.127, f32[3072,800]{0,1:T(8,128)} %get-tuple-element.157, f32[800]{0:T(1024)S(1)} %copy-done.61), kind=kLoop, calls=%fused_computation.275 | loop fusion | flops 17200128 | bytes 29543552 | tf_op jit(solution)/shard_map/transpose(jvp())/reduce_sum | solution.py:35
  221.0 7.4 convert_reduce_fusion.2
  228.5 7.8 fusion.137
  236.3 6.6 fusion.141
  247.4 10.9 %fusion.152 = f32[2000,400]{1,0:T(8,128)} fusion(bf16[3072,2000]{0,1:T(8,128)(2,1)} %fusion.93, bf16[3072,400]{0,1:T(8,128)(2,1)S(1)} %get-tuple-element.116), kind=kOutput, calls=%fused_computation.281 | convolution fusion | flops 4915200000 | bytes 17945600 | tf_op jit(solution)/shard_map/dot_general | solution.py:46
  259.8 3.8 fusion.153
  263.6 5.5 collective-permute-start.5
  275.2 4.5 copy-done.26
  279.7 12.6 %fusion.142 = (f32[400]{0:T(512)S(1)}, f32[3072]{0:T(1024)S(1)}, f32[3072,400]{0,1:T(8,128)S(1)}) fusion(f32[400]{0:T(512)S(1)} %copy-done.54, f32[3072]{0:T(1024)S(1)} %copy-done.28, f32[3072,400]{0,1:T(8,128)S(1)} %bitcast.134, f32[400]{0:T(512)S(1)} %copy-done.48, f32[400]{0:T(512)S(1)} %copy-done.78, f32[3072]{0:T(1024)S(1)} %copy-done.34, ...), kind=kOutput, calls=%fused_computation.274 | convolution fusion | flops 4949602816 | bytes 23761664 | tf_op jit(solution)/shard_map/dot_general | solution.py:167
  297.2 3.9 fusion.151
  301.2 11.7 %fusion.138 = (f32[800]{0:T(1024)S(1)}, f32[3072]{0:T(1024)S(1)}, f32[3072,800]{0,1:T(8,128)S(1)}) fusion(f32[800]{0:T(1024)S(1)} %copy-done.50, f32[3072]{0:T(1024)S(1)} %copy-done.32, bf16[1,3072,800]{1,2,0:T(8,128)(2,1)S(1)} %bitcast.138, f32[800]{0:T(1024)S(1)} %copy-done.80, f32[3072]{0:T(1024)S(1)} %copy-done.36, ...), kind=kOutput, calls=%fused_computation.270 | convolution fusion | flops 2034888960 | bytes 17889664 | tf_op jit(solution)/shard_map/dot_general | solution.py:52
  312.9 4.1 fusion.17
  317.2 9.3 add_bitcast_fusion
  326.5 510.7 %all-reduce.44 = (bf16[800]{0:T(1024)(128)(2,1)S(1)}, bf16[800]{0:T(1024)(128)(2,1)S(1)}, bf16[800,400]{0,1:T(8,128)(2,1)}, bf16[400]{0:T(512)(128)(2,1)S(1)}, b...) all-reduce(f32[800]{0:T(1024)S(1)} %get-tuple-element.28, ...), channel_id=1, replica_groups=mesh['seq'=16,'wa'=2] {'seq'}, use_global_device_ids=true, to_apply=%region_25.26 | all-reduce | flops 2569600 | bytes 15417600 | tf_op jit(solution)/shard_map/psum | solution.py:295
  846.8 4.8 reshape.464
  853.2 3.4 all-reduce.41
  862.5 13.8 %add_bitcast_fusion.1 = f32[1,3072,800]{1,2,0:T(8,128)} fusion(f32[3072,800]{0,1:T(8,128)} %copy-done.2, bf16[400,800]{1,0:T(8,128)(2,1)} %copy-done.19, f32[800]{0:T(1024)S(1)} %convert_element_type.311, f32[400]{0:T(512)S(1)} %copy-done.96, f32[400]{0:T(512)S(1)} %copy-done.73, f32[3072]{0:T(1024)S(1)} %copy-done.40, f32[3072,400]{0,1:T(8,128)} %copy-done.4, ...), kind=kOutput, calls=%fused_computation.43 | convolution fusion | flops 1988198400 | bytes 25248576 | tf_op jit(solution)/shard_map/dot_general | solution.py:117
  878.2 3.8 reduce-scatter.31.cloned.1.call-done
  883.9 10.0 %reduce-scatter.29.cloned.1.call-done = bf16[200,800]{1,0:T(8,128)(2,1)} async-done(((bf16[400,800]{1,0:T(8,128)(2,1)}), bf16[200,800]{1,0:T(8,128)(2,1)}) %reduce-scatter.29.cloned.1.call-update) | async-done | bytes 320016
  895.8 10.1 %reduce-scatter.27.cloned.1.call-done = bf16[800,200]{0,1:T(8,128)(2,1)} async-done(((bf16[800,400]{0,1:T(8,128)(2,1)}), bf16[800,200]{0,1:T(8,128)(2,1)}) %reduce-scatter.27.cloned.1.call-update) | async-done | bytes 320016
  907.8 10.5 %reduce-scatter.25.cloned.1.call-done = bf16[200,1200]{1,0:T(8,128)(2,1)} async-done(((bf16[400,1200]{1,0:T(8,128)(2,1)}), bf16[200,1200]{1,0:T(8,128)(2,1)}) %reduce-scatter.25.cloned.1.call-update) | async-done | bytes 480016
  922.1 9.4 reduce-scatter.23.cloned.1.call-done
  931.5 3.4 reshape.465
  (418 shorter events, 112.9 us)
Async XLA Ops:
  7.2 87.5 %all-gather.2.cloned.1.call-start = ((), (), s32[]{:S(2)}) async-start(), calls=%async_computation.6 | async-start | bytes 3072000 | tf_op jit(solution)/shard_map/all_gather | solution.py:234
  7.9 868.4 %reduce-scatter.33.cloned.1.call-start = ((), (), s32[]{:S(2)}) async-start(), calls=%async_computation.12 | async-start | bytes 1075200
  29.5 55.3 %copy-start.47 = (f32[400]{0:T(512)}, f32[400]{0:T(512)S(1)}, u32[]{:S(2)}) copy-start(f32[400]{0:T(512)S(1)} %convert_element_type.291) | copy-start | bytes 4804
  29.5 55.2 %copy-start.53 = (f32[400]{0:T(512)}, f32[400]{0:T(512)S(1)}, u32[]{:S(2)}) copy-start(f32[400]{0:T(512)S(1)} %convert_element_type.292) | copy-start | bytes 4804
  29.5 17.7 %copy-start.76 = (f32[400]{0:T(512)}, f32[400]{0:T(512)S(1)}, u32[]{:S(2)}) copy-start(f32[400]{0:T(512)S(1)} %convert_element_type.293) | copy-start | bytes 4804
  46.3 38.4 %copy-start.27 = (f32[3072]{0:T(1024)}, f32[3072]{0:T(1024)S(1)}, u32[]{:S(2)}) copy-start(f32[3072]{0:T(1024)S(1)} %broadcast_multiply_fusion.3) | copy-start | bytes 36868
  47.2 37.5 %copy-start.33 = (f32[3072]{0:T(1024)}, f32[3072]{0:T(1024)S(1)}, u32[]{:S(2)}) copy-start(f32[3072]{0:T(1024)S(1)} %fusion.125) | copy-start | bytes 36868
  47.2 18.1 %copy-start.85 = (s32[1,3072]{1,0:T(1,128)S(1)}, s32[1,3072]{1,0:T(1,128)}, u32[]{:S(2)}) copy-start(s32[1,3072]{1,0:T(1,128)} %param.29) | copy-start | bytes 36868
  50.9 38.0 %collective-permute-start.1 = (bf16[16,400]{0,1:T(8,128)(2,1)S(1)}, bf16[16,400]{0,1:T(8,128)(2,1)S(1)}, u32[]{:S(2)}, u32[]{:S(2)}) collective-permute-start(bf16[16,400]{0,1:T(8,128)(2,1)S(1)} %get-tuple-element.134), channel_id=1, source_target_pairs={{2,0},{4,2},{6,4},{8,6},{10,8},{12,10},{14,12},{16,14},{18,16},{20... | collective-permute-start | bytes 38408 | tf_op jit(solution)/shard_map/ppermute | solution.py:23
  52.2 27.2 %collective-permute-start = (bf16[16,400]{0,1:T(8,128)(2,1)}, bf16[16,400]{0,1:T(8,128)(2,1)S(1)}, u32[]{:S(2)}, u32[]{:S(2)}) collective-permute-start(bf16[16,400]{0,1:T(8,128)(2,1)} %get-tuple-element.135), channel_id=1, source_target_pairs={{0,2},{2,4},{4,6},{6,8},{8,10},{10,12},{12,14},{14,16},{16,18},{18... | collective-permute-start | bytes 38408 | tf_op jit(solution)/shard_map/ppermute | solution.py:22
  59.9 45.1 %copy-start.22 = (bf16[400,800]{1,0:T(8,128)(2,1)}, bf16[400,800]{1,0:T(8,128)(2,1)S(1)}, u32[]{:S(2)}) copy-start(bf16[400,800]{1,0:T(8,128)(2,1)S(1)} %all_gather.82) | copy-start | bytes 1920004
  66.6 18.1 %copy-start.55 = (pred[3072]{0:T(1024)(128)(4,1)}, pred[3072]{0:T(1024)(128)(4,1)S(1)}, u32[]{:S(2)}) copy-start(pred[3072]{0:T(1024)(128)(4,1)S(1)} %get-tuple-element.142) | copy-start | bytes 9220
  66.6 18.1 %copy-start.68 = (pred[3072]{0:T(1024)(128)(4,1)}, pred[3072]{0:T(1024)(128)(4,1)S(1)}, u32[]{:S(2)}) copy-start(pred[3072]{0:T(1024)(128)(4,1)S(1)} %get-tuple-element.141) | copy-start | bytes 9220
  66.6 22.2 %copy-start.70 = (pred[3072]{0:T(1024)(128)(4,1)}, pred[3072]{0:T(1024)(128)(4,1)S(1)}, u32[]{:S(2)}) copy-start(pred[3072]{0:T(1024)(128)(4,1)S(1)} %get-tuple-element.139) | copy-start | bytes 9220
  66.6 25.1 %copy-start.58 = (pred[3072]{0:T(1024)(128)(4,1)}, pred[3072]{0:T(1024)(128)(4,1)S(1)}, u32[]{:S(2)}) copy-start(pred[3072]{0:T(1024)(128)(4,1)S(1)} %get-tuple-element.138) | copy-start | bytes 9220
  66.6 18.1 %slice-start = ((s8[4915200]{0:T(1024)(128)(4,1)}), s8[4194304]{0:T(1024)(128)(4,1)S(1)}, s32[]{:S(2)}) async-start(s8[4915200]{0:T(1024)(128)(4,1)} %bitcast.131), calls=%async_computation.13 | async-start | bytes 8388608
  72.2 32.7 %copy-start.64 = (f32[400]{0:T(512)}, f32[400]{0:T(512)S(1)}, u32[]{:S(2)}) copy-start(f32[400]{0:T(512)S(1)} %convert_element_type.295) | copy-start | bytes 4804
  72.2 50.6 %copy-start.51 = (f32[400]{0:T(512)}, f32[400]{0:T(512)S(1)}, u32[]{:S(2)}) copy-start(f32[400]{0:T(512)S(1)} %convert_element_type.303) | copy-start | bytes 4804
  72.9 32.1 %copy-start.74 = (f32[400]{0:T(512)}, f32[400]{0:T(512)S(1)}, u32[]{:S(2)}) copy-start(f32[400]{0:T(512)S(1)} %convert_element_type.296) | copy-start | bytes 4804
  73.6 49.3 %copy-start.66 = (f32[400]{0:T(512)}, f32[400]{0:T(512)S(1)}, u32[]{:S(2)}) copy-start(f32[400]{0:T(512)S(1)} %convert_element_type.304) | copy-start | bytes 4804
  78.1 33.1 %copy-start.60 = (f32[800]{0:T(1024)}, f32[800]{0:T(1024)S(1)}, u32[]{:S(2)}) copy-start(f32[800]{0:T(1024)S(1)} %convert_element_type.300) | copy-start | bytes 9604
  127.3 13.9 %collective-permute-start.2 = (bf16[32,400]{0,1:T(8,128)(2,1)S(1)}, bf16[32,400]{0,1:T(8,128)(2,1)S(1)}, u32[]{:S(2)}, u32[]{:S(2)}) collective-permute-start(bf16[32,400]{0,1:T(8,128)(2,1)S(1)} %slice.86), channel_id=1, source_target_pairs={{0,2},{2,4},{4,6},{6,8},{8,10},{10,12},{12,14},{14,16},{16,18},{18... | collective-permute-start | bytes 76808 | tf_op jit(solution)/shard_map/ppermute | solution.py:31
  134.5 18.8 %copy-start.19 = (bf16[400,800]{1,0:T(8,128)(2,1)}, bf16[400,800]{1,0:T(8,128)(2,1)S(1)}, u32[]{:S(2)}) copy-start(bf16[400,800]{1,0:T(8,128)(2,1)S(1)} %all_gather.94) | copy-start | bytes 1920004
  134.5 26.4 %copy-start.62 = (f32[400]{0:T(512)}, f32[400]{0:T(512)S(1)}, u32[]{:S(2)}) copy-start(f32[400]{0:T(512)S(1)} %convert_element_type.307) | copy-start | bytes 4804
  134.5 26.3 %copy-start.72 = (f32[400]{0:T(512)}, f32[400]{0:T(512)S(1)}, u32[]{:S(2)}) copy-start(f32[400]{0:T(512)S(1)} %convert_element_type.308) | copy-start | bytes 4804
  134.5 18.8 %copy-start.95 = (f32[400]{0:T(512)}, f32[400]{0:T(512)S(1)}, u32[]{:S(2)}) copy-start(f32[400]{0:T(512)S(1)} %convert_element_type.309) | copy-start | bytes 4804
  147.0 16.8 %copy-start.4 = (f32[3072,400]{0,1:T(8,128)}, f32[3072,400]{0,1:T(8,128)S(1)}, u32[]{:S(2)}) copy-start(f32[3072,400]{0,1:T(8,128)S(1)} %get-tuple-element.154) | copy-start | bytes 14745604
  147.0 16.8 %copy-start.37 = (f32[3072]{0:T(1024)}, f32[3072]{0:T(1024)S(1)}, u32[]{:S(2)}) copy-start(f32[3072]{0:T(1024)S(1)} %broadcast_multiply_fusion) | copy-start | bytes 36868
  147.9 15.9 %copy-start.39 = (f32[3072]{0:T(1024)}, f32[3072]{0:T(1024)S(1)}, u32[]{:S(2)}) copy-start(f32[3072]{0:T(1024)S(1)} %fusion.129) | copy-start | bytes 36868
  167.4 6.9 collective-permute-start.3
  192.0 14.8 %copy-start.15 = (bf16[3072,400]{0,1:T(8,128)(2,1)}, bf16[3072,400]{0,1:T(8,128)(2,1)S(1)}, u32[]{:S(2)}) copy-start(bf16[3072,400]{0,1:T(8,128)(2,1)S(1)} %get-tuple-element.112) | copy-start | bytes 7372804
  221.0 15.3 %slice-start.16 = ((s8[4915200]{0:T(1024)(128)(4,1)}), s8[720896]{0:T(1024)(128)(4,1)S(1)}, s32[]{:S(2)}) async-start(s8[4915200]{0:T(1024)(128)(4,1)} %bitcast.145), calls=%async_computation.29 | async-start | bytes 1441792
  245.3 14.4 %slice-start.20 = ((s8[4915200]{0:T(1024)(128)(4,1)}), s8[720896]{0:T(1024)(128)(4,1)S(1)}, s32[]{:S(2)}) async-start(s8[4915200]{0:T(1024)(128)(4,1)} %bitcast.152), calls=%async_computation.33 | async-start | bytes 1441792
  258.4 10.7 %collective-permute-start.4 = (bf16[16,400]{0,1:T(8,128)(2,1)S(1)}, bf16[16,400]{0,1:T(8,128)(2,1)S(1)}, u32[]{:S(2)}, u32[]{:S(2)}) collective-permute-start(bf16[16,400]{0,1:T(8,128)(2,1)S(1)} %get-tuple-element.132), channel_id=1, source_target_pairs={{2,0},{4,2},{6,4},{8,6},{10,8},{12,10},{14,12},{16,14},{18,16},{20... | collective-permute-start | bytes 38408 | tf_op jit(solution)/shard_map/ppermute | solution.py:23
  263.6 8.8 collective-permute-start.5
  297.2 19.9 %slice-start.8 = ((s8[9830400]{0:T(1024)(128)(4,1)}), s8[4194304]{0:T(1024)(128)(4,1)S(1)}, s32[]{:S(2)}) async-start(s8[9830400]{0:T(1024)(128)(4,1)} %bitcast.139), calls=%async_computation.21 | async-start | bytes 8388608
  301.2 15.9 %slice-start.9 = ((s8[9830400]{0:T(1024)(128)(4,1)}), s8[4194304]{0:T(1024)(128)(4,1)S(1)}, s32[]{:S(2)}) async-start(s8[9830400]{0:T(1024)(128)(4,1)} %bitcast.139), calls=%async_computation.22 | async-start | bytes 8388608
  301.2 15.9 %slice-start.10 = ((s8[9830400]{0:T(1024)(128)(4,1)}), s8[1441792]{0:T(1024)(128)(4,1)S(1)}, s32[]{:S(2)}) async-start(s8[9830400]{0:T(1024)(128)(4,1)} %bitcast.139), calls=%async_computation.23 | async-start | bytes 2883584
  837.3 44.8 %reduce-scatter.31.cloned.1.call-start = ((), (), s32[]{:S(2)}) async-start(), calls=%async_computation.11 | async-start | bytes 1075200
  838.0 55.9 %reduce-scatter.29.cloned.1.call-start = ((), (), s32[]{:S(2)}) async-start(), calls=%async_computation.10 | async-start | bytes 1075200
  838.6 67.3 %reduce-scatter.27.cloned.1.call-start = ((), (), s32[]{:S(2)}) async-start(), calls=%async_computation.9 | async-start | bytes 1075200
  839.2 79.2 %reduce-scatter.25.cloned.1.call-start = ((), (), s32[]{:S(2)}) async-start(), calls=%async_computation.8 | async-start | bytes 1536000
  843.6 87.9 %reduce-scatter.23.cloned.1.call-start = ((), (), s32[]{:S(2)}) async-start(), calls=%async_computation.7 | async-start | bytes 2457600
  843.9 18.6 %copy-start.38 = (f32[3072]{0:T(1024)S(1)}, f32[3072]{0:T(1024)}, u32[]{:S(2)}) copy-start(f32[3072]{0:T(1024)} %copy-done.37) | copy-start | bytes 36868
  843.9 18.6 %copy-start.40 = (f32[3072]{0:T(1024)S(1)}, f32[3072]{0:T(1024)}, u32[]{:S(2)}) copy-start(f32[3072]{0:T(1024)} %copy-done.39) | copy-start | bytes 36868
  843.9 18.6 %copy-start.63 = (f32[400]{0:T(512)S(1)}, f32[400]{0:T(512)}, u32[]{:S(2)}) copy-start(f32[400]{0:T(512)} %copy-done.62) | copy-start | bytes 4804
  843.9 18.6 %copy-start.73 = (f32[400]{0:T(512)S(1)}, f32[400]{0:T(512)}, u32[]{:S(2)}) copy-start(f32[400]{0:T(512)} %copy-done.72) | copy-start | bytes 4804
  843.9 18.6 %copy-start.96 = (f32[400]{0:T(512)S(1)}, f32[400]{0:T(512)}, u32[]{:S(2)}) copy-start(f32[400]{0:T(512)} %copy-done.95) | copy-start | bytes 4804
  (92 other events, 578.6 us)
Sparse Core Ops, SparseCore 0:
  9.6 13.1 all-gather.1
  837.4 32.4 reduce-scatter.32
  872.8 9.1 reduce-scatter.30
  884.7 9.1 reduce-scatter.28
  896.7 9.1 reduce-scatter.26
  908.6 9.6 reduce-scatter.24
  921.2 10.2 reduce-scatter.22
where the time goes:
time: 950 us; the launch traced here: 944 us
  blocking collectives  536 us (56%)
  matrix products  136 us (14%)
  other arithmetic  135 us (14%)
  local copies, waits for them, and re-layouts  50.5 us (5%)
  waiting for transfers between devices  46.3 us (5%)
  starting transfers between devices  20 us (2%)
  between operations  19 us (2%)
    psum x1, blocking collectives, local(): lax.psum((grad_efg, grad_efb, grad_erw, grad_erb, grad_emg, grad_emb, gra...  511 us
    unnamed x13, waiting for transfers between devices  46.3 us
    unnamed x297, local copies, waits for them, and re-layouts  42.9 us
    dot_general x4, matrix products, contract_cols(): lax.dot_general(left, right, (((1,), (1,)), ((), ())), preferred_element_...  40.5 us
    dot_general x6, matrix products, contract_rows(): lax.dot_general(left, right, (((0,), (0,)), ((), ())), preferred_element_...  37.3 us
    dot_general x2, matrix products, backward_block(): jnp.dot(back_stacked, turned, preferred_element_type=jnp.float32)  21.2 us
  transfers between devices with their start and end apart: 13, of which 5 were waited for; matrix products, arithmetic and copies ran while one was open for 13% of the time, Pallas kernels for 0%

commit v1 on v0

v1 whole, which is shorter than its diff:
```python
import functools

import jax
import jax.numpy as jnp
from jax import lax
from jax.experimental import pallas as pl
from jax.experimental.pallas import tpu as pltpu
from jax.sharding import PartitionSpec as P

ENCODER_TAPS = 5
ENCODER_DILATION = 8
DECODER_TAPS = 3
DECODER_DILATION = 16
EPS = 1e-05

MESH = pl.DeviceIdType.MESH
BF = jnp.bfloat16
F32 = jnp.float32
LANES = 128
TILE = 512
HALF = 256
AUG = 16
VMEM_LIMIT = 56 * 1024 * 1024
GELU_1 = 2.0 * 0.7978845608028654
GELU_3 = 8.0 * 0.7978845608028654 * 0.044715

ENCODER_SHIFTS = tuple(ENCODER_DILATION * (j - ENCODER_TAPS // 2) for j in range(ENCODER_TAPS))
DECODER_SHIFTS = tuple(-DECODER_DILATION * (DECODER_TAPS - 1 - j) for j in range(DECODER_TAPS))


def params(collective=None):
    if collective is None:
        return pltpu.CompilerParams(vmem_limit_bytes=VMEM_LIMIT)
    return pltpu.CompilerParams(
        vmem_limit_bytes=VMEM_LIMIT, collective_id=collective, has_side_effects=True
    )


def whole(shape):
    return pl.BlockSpec(shape, lambda *_: (0,) * len(shape))


def nt_dot(left, right):
    return lax.dot_general(left, right, (((1,), (1,)), ((), ())), preferred_element_type=F32)


def nn_dot(left, right):
    return jnp.dot(left, right, preferred_element_type=F32)


def lanes_of(column, width):
    return jnp.concatenate([column] * (width // LANES), axis=1)


def fold(value):
    total = value[:, :LANES]
    for at in range(LANES, value.shape[1], LANES):
        total = total + value[:, at : at + LANES]
    return total


def weights_kernel(dims, *refs):
    d, inner, taps = dims
    n_in = 24
    ins, refs = refs[:n_in], refs[n_in:]
    outs, refs = refs[:24], refs[24:]
    (small_own, small_got, k_own0, k_own1, e_own0, e_own1, r_own0, r_own1, *rest) = refs
    (r_got0, r_got1, k_got0, k_got1, e_got0, e_got1, send, recv) = rest
    me = lax.axis_index("wa")
    other = 1 - me
    barrier = pltpu.get_barrier_semaphore()
    pl.semaphore_signal(barrier, inc=1, device_id={"wa": other}, device_id_type=MESH)
    pl.semaphore_wait(barrier, 1)

    half = inner // 2
    pad = k_own0.shape[1]
    small_own[...] = jnp.zeros_like(small_own)
    small_at = []
    for side in range(2):
        for at in (0, 1, 3, 4, 5, 7, 8, 9, 11):
            small_at.append(12 * side + at)
    for row, at in enumerate(small_at):
        n = ins[at].shape[0]
        small_own[row : row + 1, 0:n] = ins[at][...].astype(F32).reshape(1, n)
    owns, gots = [], []
    for side, (k_own, e_own, r_own) in enumerate(((k_own0, e_own0, r_own0), (k_own1, e_own1, r_own1))):
        base = 12 * side
        k_own[:, half - 8 : pad, :] = jnp.zeros((taps[side], pad - half + 8, inner), BF)
        k_own[:, 0:half, :] = ins[base + 6][...]
        e_own[half - 8 : pad, :] = jnp.zeros((pad - half + 8, d), BF)
        e_own[0:half, :] = ins[base + 10][...]
        r_own[half - 8 : pad, :] = jnp.zeros((pad - half + 8, d), BF)
        r_own[0:half, :] = ins[base + 2][...]
        owns += [r_own, k_own, e_own]
    owns.append(small_own)
    gots = [r_got0, k_got0, e_got0, r_got1, k_got1, e_got1, small_got]
    copies = []
    for at, (own, got) in enumerate(zip(owns, gots)):
        copies.append(
            pltpu.make_async_remote_copy(
                src_ref=own,
                dst_ref=got,
                send_sem=send.at[at],
                recv_sem=recv.at[at],
                device_id={"wa": other},
                device_id_type=MESH,
            )
        )
        copies[-1].start()
    for copy in copies:
        copy.wait()

    first_core = me == 0

    def ordered(own, got):
        own, got = own.astype(F32), got.astype(F32)
        return jnp.where(first_core, own, got), jnp.where(first_core, got, own)

    small0, small1 = ordered(small_own[...], small_got[...])

    def column(row, n):
        line = jnp.concatenate([small0[row : row + 1, 0 : n // 2], small1[row : row + 1, 0 : n // 2]], axis=1)
        return jnp.broadcast_to(line, (LANES, n)).T

    def bias_columns(value):
        where = lax.broadcasted_iota(jnp.int32, (value.shape[0], AUG), 1) == 0
        return jnp.where(where, value[:, :AUG], 0.0).astype(BF)

    for side in range(2):
        o = outs[12 * side : 12 * side + 12]
        wrt, kt, wet, we, kb, wr, g1, b1, g2, b2, g3, b3 = o
        base = 9 * side
        g1[...] = column(base + 0, d)
        b1[...] = column(base + 1, d)
        g2[...] = column(base + 3, inner)
        b2[...] = column(base + 4, inner)
        g3[...] = column(base + 6, inner)
        b3[...] = column(base + 7, inner)
        n = taps[side]
        r0, r1 = ordered(owns[3 * side][0:half, :], gots[3 * side][0:half, :])
        r = jnp.concatenate([r0, r1], axis=0)
        wr[...] = r.T.astype(BF)
        wrt[:, 0:d] = r.astype(BF)
        wrt[:, d : d + AUG] = bias_columns(column(base + 2, inner))
        e0, e1 = ordered(owns[3 * side + 2][0:half, :], gots[3 * side + 2][0:half, :])
        e = jnp.concatenate([e0, e1], axis=0)
        we[...] = e.astype(BF)
        wet[:, 0:inner] = e.T.astype(BF)
        wet[:, inner : inner + AUG] = bias_columns(column(base + 8, d))
        for j in range(n):
            k0, k1 = ordered(owns[3 * side + 1][j, 0:half, :], gots[3 * side + 1][j, 0:half, :])
            k = jnp.concatenate([k0, k1], axis=0)
            kb[:, j * inner : (j + 1) * inner] = k.astype(BF)
            kt[:, j * inner : (j + 1) * inner] = k.T.astype(BF)
        kt[:, n * inner : n * inner + AUG] = bias_columns(column(base + 5, inner))


def gather_weights(args, d, inner):
    taps = (ENCODER_TAPS, DECODER_TAPS)
    half = inner // 2
    pad = -(-half // 16) * 16
    shapes = []
    for n in taps:
        shapes += [
            ((inner, d + AUG), BF),
            ((inner, n * inner + AUG), BF),
            ((d, inner + AUG), BF),
            ((inner, d), BF),
            ((inner, n * inner), BF),
            ((d, inner), BF),
            ((d, LANES), F32),
            ((d, LANES), F32),
            ((inner, LANES), F32),
            ((inner, LANES), F32),
            ((inner, LANES), F32),
            ((inner, LANES), F32),
        ]
    vm = pl.BlockSpec(memory_space=pltpu.VMEM)
    small = pltpu.VMEM((24, 512), F32)
    kk = [pltpu.VMEM((n, pad, inner), BF) for n in taps]
    ee = [pltpu.VMEM((pad, d), BF)] * 2
    outs = pl.pallas_call(
        functools.partial(weights_kernel, (d, inner, taps)),
        out_shape=[jax.ShapeDtypeStruct(*s) for s in shapes],
        in_specs=[vm] * 24,
        out_specs=[vm] * 24,
        scratch_shapes=[small, small, *kk, *ee, *ee, *ee, *kk, *ee]
        + [pltpu.SemaphoreType.DMA((7,)), pltpu.SemaphoreType.DMA((7,))],
        compiler_params=params(0),
        name="gather_weights",
    )(*args)
    return outs[:12], outs[12:]


def statistics(src, lanes, channels):
    width = lanes.stop - lanes.start
    total = [jnp.zeros((8, width), F32) for _ in range(4)]
    for g in range(channels // 8):
        total[g % 4] = total[g % 4] + src[8 * g : 8 * g + 8, lanes]
    mean = jnp.sum((total[0] + total[1]) + (total[2] + total[3]), axis=0, keepdims=True) * (1.0 / channels)
    wide = jnp.broadcast_to(mean, (8, width))
    total = [jnp.zeros((8, width), F32) for _ in range(4)]
    for g in range(channels // 8):
        centre = src[8 * g : 8 * g + 8, lanes] - wide
        total[g % 4] = total[g % 4] + centre * centre
    spread = jnp.sum((total[0] + total[1]) + (total[2] + total[3]), axis=0, keepdims=True) * (1.0 / channels)
    return mean, lax.rsqrt(spread + EPS)


def norm_forward(src, lanes, channels, gain, bias, h_out, z_out, d_out, r_out):
    width = lanes.stop - lanes.start
    mean, r = statistics(src, lanes, channels)
    if r_out is not None:
        r_out[:, lanes] = jnp.broadcast_to(r, (8, width))
    rw = jnp.broadcast_to(r, (16, width))
    mw = jnp.broadcast_to(mean * r, (16, width))
    for c in range(0, channels, 16):
        rows = slice(c, c + 16)
        z = src[rows, lanes] * rw - mw
        half = z * lanes_of(gain[rows, :] * 0.5, width) + lanes_of(bias[rows, :] * 0.5, width)
        sq = half * half
        t = jnp.tanh(half * (sq * GELU_3 + GELU_1))
        h_out[rows, lanes] = (half + half * t).astype(BF)
        slope = (1.0 + t) * (0.5 + (half * (sq * (1.5 * GELU_3) + 0.5 * GELU_1)) * (1.0 - t))
        z_out[rows, lanes] = z.astype(BF)
        d_out[rows, lanes] = slope.astype(BF)


def norm_backward(grad, lanes, channels, gain, z_in, d_in, r_in, gain_sum, bias_sum, emit):
    width = lanes.stop - lanes.start
    one = [jnp.zeros((8, width), F32) for _ in range(2)]
    two = [jnp.zeros((8, width), F32) for _ in range(2)]
    for c in range(0, channels, 16):
        rows = slice(c, c + 16)
        da = grad[rows, lanes] * d_in[rows, lanes].astype(F32)
        p = da * z_in[rows, lanes].astype(F32)
        bias_sum[rows, :] += fold(da)
        gain_sum[rows, :] += fold(p)
        wide = lanes_of(gain[rows, :], width)
        dz = da * wide
        q = p * wide
        grad[rows, lanes] = dz
        for at in range(2):
            one[at] = one[at] + dz[8 * at : 8 * at + 8]
            two[at] = two[at] + q[8 * at : 8 * at + 8]
    r = r_in[0:1, lanes]
    scale = r * (1.0 / channels)
    m1 = jnp.broadcast_to(jnp.sum(one[0] + one[1], axis=0, keepdims=True) * scale, (16, width))
    m2 = jnp.broadcast_to(jnp.sum(two[0] + two[1], axis=0, keepdims=True) * scale, (16, width))
    rw = jnp.broadcast_to(r, (16, width))
    for c in range(0, channels, 16):
        rows = slice(c, c + 16)
        emit(rows, grad[rows, lanes] * rw - m1 - z_in[rows, lanes].astype(F32) * m2)


def tap_mask(starts, ends, first, shift):
    place = first + shift + lax.broadcasted_iota(jnp.int32, (8, TILE), 1)
    usable = (place >= jnp.broadcast_to(starts[...], (8, TILE))) & (place < jnp.broadcast_to(ends[...], (8, TILE)))
    one = jnp.where(usable, 1.0, 0.0)
    return jnp.concatenate([one, one], axis=0).astype(BF)


def stack_taps(stack, shifts, before, main, after, starts, ends, first, inner):
    for j, shift in enumerate(shifts):
        if not shift:
            stack[j * inner : (j + 1) * inner, :] = main[0:inner, :]
            continue
        mask = tap_mask(starts, ends, first, shift)
        for c in range(0, inner, 16):
            rows = slice(c, c + 16)
            if shift < 0:
                span = jnp.concatenate([before[rows, :], main[rows, :]], axis=1)
                span = pltpu.roll(span, -shift, 1)[:, LANES:]
            else:
                span = jnp.concatenate([main[rows, :], after[rows, :]], axis=1)
                span = pltpu.roll(span, TILE + LANES - shift, 1)[:, :TILE]
            stack[j * inner + c : j * inner + c + 16, :] = span * mask


def ones_rows(width):
    where = lax.broadcasted_iota(jnp.int32, (AUG, width), 0) == 0
    return jnp.where(where, 1.0, 0.0).astype(BF)


def neighbours():
    me = lax.axis_index("seq")
    n = lax.axis_size("seq")
    return lax.rem(me + n - 1, n), lax.rem(me + 1, n)


def greet(left, right):
    barrier = pltpu.get_barrier_semaphore()
    for device in (left, right):
        pl.semaphore_signal(barrier, inc=1, device_id={"seq": device}, device_id_type=MESH)
    pl.semaphore_wait(barrier, 2)


def send_copy(src, dst, sems, device):
    return pltpu.make_async_remote_copy(
        src_ref=src,
        dst_ref=dst,
        send_sem=sems.at[0],
        recv_sem=sems.at[1],
        device_id={"seq": device},
        device_id_type=MESH,
    )


def share_edges(kind, step, steps, inner, source, edges, scratch):
    left, right = neighbours()
    own_r = got_r = own_l = got_l = None
    if kind == "both":
        own_r, got_r, sem_r, own_l, got_l, sem_l = scratch
    elif kind == "right":
        own_r, got_r, sem_r = scratch
    else:
        own_l, got_l, sem_l = scratch

    @pl.when(step == 0)
    def _():
        greet(left, right)
        if own_r is not None:
            own_r[...] = source[0:inner, TILE - LANES : TILE]
            send_copy(own_r, got_r, sem_r, right).start()

    if own_l is not None:

        @pl.when(step == 1)
        def _():
            own_l[...] = source[0:inner, 0:LANES]
            send_copy(own_l, got_l, sem_l, left).start()

    @pl.when(step == steps - 1)
    def _():
        at = 0
        if own_r is not None:
            send_copy(own_r, got_r, sem_r, right).wait()
            edges[at][...] = got_r[...]
            at += 1
        if own_l is not None:
            send_copy(own_l, got_l, sem_l, left).wait()
            edges[at][...] = got_l[...]


def edge_scratch(kind, inner):
    one = [pltpu.VMEM((inner, LANES), BF), pltpu.VMEM((inner, LANES), BF), pltpu.SemaphoreType.DMA((2,))]
    return one * 2 if kind == "both" else one


def first_place(step, steps):
    return lax.axis_index("seq") * (steps * TILE) + lax.rem(step + steps - 1, steps) * TILE


CHAINS = (slice(0, HALF), slice(HALF, TILE))


def enc_in_kernel(steps, x, wrt, g1, b1, g2, b2, h1, z1, d1, r1, h2, z2, d2, r2, e_l, e_r, xt, u, *edge):
    step = pl.program_id(0)
    d, inner = x.shape[0], wrt.shape[0]
    h1[d : d + AUG, :] = ones_rows(TILE)
    h2[inner : inner + AUG, :] = ones_rows(TILE)
    for lanes in CHAINS:
        xt[:, lanes] = x[:, lanes].astype(F32)
        norm_forward(xt, lanes, d, g1, b1, h1, z1, d1, r1)
    for lanes in CHAINS:
        u[:, lanes] = nn_dot(wrt[...], h1[:, lanes])
    for lanes in CHAINS:
        norm_forward(u, lanes, inner, g2, b2, h2, z2, d2, r2)
    share_edges("both", step, steps, inner, h2, (e_l, e_r), edge)


def enc_out_kernel(
    steps, starts, ends, before, main, after, e_l, e_r, xt, kt, wet, wrt, g3, b3, g1, b1, g2, b2,
    h3, z3, d3, r3, x1, h1, z1, d1, r1, h2, z2, d2, r2, edge_o,
    stack, win_b, win_a, v, y, u, *edge,
):
    step = pl.program_id(0)
    d, inner = xt.shape[0], v.shape[0]
    win_b[...] = jnp.where(step == 1, e_l[...], before[0:inner, :])
    win_a[...] = jnp.where(step == 0, e_r[...], after[0:inner, :])
    stack_taps(stack, ENCODER_SHIFTS, win_b, main, win_a, starts, ends, first_place(step, steps), inner)
    stack[len(ENCODER_SHIFTS) * inner :, :] = ones_rows(TILE)
    h3[inner : inner + AUG, :] = ones_rows(TILE)
    h1[d : d + AUG, :] = ones_rows(TILE)
    h2[inner : inner + AUG, :] = ones_rows(TILE)
    for lanes in CHAINS:
        v[:, lanes] = nn_dot(kt[...], stack[:, lanes])
    for lanes in CHAINS:
        norm_forward(v, lanes, inner, g3, b3, h3, z3, d3, r3)
    for lanes in CHAINS:
        y[:, lanes] = nn_dot(wet[...], h3[:, lanes])
    for lanes in CHAINS:
        for c in range(0, d, 16):
            rows = slice(c, c + 16)
            total = y[rows, lanes] + xt[rows, lanes].astype(F32)
            y[rows, lanes] = total
            x1[rows, lanes] = total.astype(BF)
        norm_forward(y, lanes, d, g1, b1, h1, z1, d1, r1)
    for lanes in CHAINS:
        u[:, lanes] = nn_dot(wrt[...], h1[:, lanes])
    for lanes in CHAINS:
        norm_forward(u, lanes, inner, g2, b2, h2, z2, d2, r2)
    share_edges("right", step, steps, inner, h2, (edge_o,), edge)


def dec_out_kernel(
    steps, starts, ends, before, main, e_l, cot_t, kt, we, g3, b3,
    h3, evr, edge_o, dwe, dg3, db3,
    stack, win_b, v, z3, d3, r3, g, *edge,
):
    step = pl.program_id(0)
    inner = v.shape[0]

    @pl.when(step == 0)
    def _():
        dwe[...] = jnp.zeros_like(dwe)
        dg3[...] = jnp.zeros_like(dg3)
        db3[...] = jnp.zeros_like(db3)

    win_b[...] = jnp.where(step == 1, e_l[...], before[0:inner, :])
    stack_taps(stack, DECODER_SHIFTS, win_b, main, None, starts, ends, first_place(step, steps), inner)
    stack[len(DECODER_SHIFTS) * inner :, :] = ones_rows(TILE)
    h3[inner : inner + AUG, :] = ones_rows(TILE)
    for lanes in CHAINS:
        v[:, lanes] = nn_dot(kt[...], stack[:, lanes])
    for lanes in CHAINS:
        g[:, lanes] = nn_dot(we[...], cot_t[:, lanes])
    for lanes in CHAINS:
        norm_forward(v, lanes, inner, g3, b3, h3, z3, d3, r3)
    dwe[...] += nt_dot(h3[...], cot_t[...])

    for lanes in CHAINS:

        def emit(rows, value):
            evr[rows, lanes] = value.astype(BF)

        norm_backward(g, lanes, inner, g3, z3, d3, r3, dg3, db3, emit)
    share_edges("left", step, steps, inner, evr, (edge_o,), edge)


def dec_back_kernel(
    steps, starts, ends, main, after, e_r, kb, wr, we, g2, g1, g3,
    h2, z2, d2, r2, h1, z1, d1, r1, cot_t, h3, z3, d3, r3,
    ey, evr, e_l2, e_r2, dk, dwrt, dwe, dg2, db2, dg1, db1, dg3, db3,
    stack, win_a, g, big, eur, *edge,
):
    step = pl.program_id(0)
    d, inner = cot_t.shape[0], g.shape[0]

    @pl.when(step == 0)
    def _():
        for ref in (dk, dwrt, dwe, dg2, db2, dg1, db1, dg3, db3):
            ref[...] = jnp.zeros_like(ref)

    win_a[...] = jnp.where(step == 0, e_r[...], after[0:inner, :])
    back = tuple(-s for s in DECODER_SHIFTS)
    stack_taps(stack, back, None, main, win_a, starts, ends, first_place(step, steps), inner)
    for lanes in CHAINS:
        g[:, lanes] = nn_dot(kb[...], stack[:, lanes])
    dk[...] += nt_dot(h2[...], stack[...])
    for lanes in CHAINS:

        def emit_u(rows, value):
            eur[rows, lanes] = value.astype(BF)

        norm_backward(g, lanes, inner, g2, z2, d2, r2, dg2, db2, emit_u)
    for lanes in CHAINS:
        big[:, lanes] = nn_dot(wr[...], eur[:, lanes])
    dwrt[...] += nt_dot(eur[...], h1[...])
    for lanes in CHAINS:

        def emit_x(rows, value):
            ey[rows, lanes] = (value + cot_t[rows, lanes].astype(F32)).astype(BF)

        norm_backward(big, lanes, d, g1, z1, d1, r1, dg1, db1, emit_x)
    for lanes in CHAINS:
        g[:, lanes] = nn_dot(we[...], ey[:, lanes])
    dwe[...] += nt_dot(h3[...], ey[...])
    for lanes in CHAINS:

        def emit_v(rows, value):
            evr[rows, lanes] = value.astype(BF)

        norm_backward(g, lanes, inner, g3, z3, d3, r3, dg3, db3, emit_v)
    share_edges("both", step, steps, inner, evr, (e_l2, e_r2), edge)


def enc_back_kernel(
    steps, starts, ends, before, main, after, e_l, e_r, kb, wr, wet, g2, g1,
    h2, z2, d2, r2, h1, z1, d1, r1, ey, x1, h3,
    out, grad, dk, dwrt, dg2, db2, dg1, db1,
    stack, win_b, win_a, g, big, eur,
):
    step = pl.program_id(0)
    d, inner = ey.shape[0], g.shape[0]

    @pl.when(step == 0)
    def _():
        for ref in (dk, dwrt, dg2, db2, dg1, db1):
            ref[...] = jnp.zeros_like(ref)

    win_b[...] = jnp.where(step == 1, e_l[...], before[0:inner, :])
    win_a[...] = jnp.where(step == 0, e_r[...], after[0:inner, :])
    back = tuple(-s for s in ENCODER_SHIFTS)
    stack_taps(stack, back, win_b, main, win_a, starts, ends, first_place(step, steps), inner)
    for lanes in CHAINS:
        g[:, lanes] = nn_dot(kb[...], stack[:, lanes])
    for lanes in CHAINS:
        out[:, lanes] = nn_dot(wet[...], h3[:, lanes]) + x1[:, lanes].astype(F32)
    dk[...] += nt_dot(h2[...], stack[...])
    for lanes in CHAINS:

        def emit_u(rows, value):
            eur[rows, lanes] = value.astype(BF)

        norm_backward(g, lanes, inner, g2, z2, d2, r2, dg2, db2, emit_u)
    for lanes in CHAINS:
        big[:, lanes] = nn_dot(wr[...], eur[:, lanes])
    dwrt[...] += nt_dot(eur[...], h1[...])
    for lanes in CHAINS:

        def emit_x(rows, value):
            grad[rows, lanes] = value + ey[rows, lanes].astype(F32)

        norm_backward(big, lanes, d, g1, z1, d1, r1, dg1, db1, emit_x)


def sections(d, inner):
    return (
        ("e_we", d),
        ("e_k", ENCODER_TAPS * inner),
        ("e_wr", d + AUG),
        ("d_we", d),
        ("d_k", DECODER_TAPS * inner),
        ("d_wr", d + AUG),
    )


def section_blocks(d, inner):
    starts, at = {}, 0
    for name, used in sections(d, inner):
        starts[name] = at
        at += -(-used // LANES)
    starts["vec"] = at
    return starts, at + 1


def reduce_kernel(plan, *refs):
    d, inner, n, streams, per = plan
    half = inner // 2
    starts, blocks = section_blocks(d, inner)
    mats, vecs, refs = refs[:6], refs[6:18], refs[18:]
    out, pack, got, rs_got, wa_sem, rs_send, rs_recv, ag_send, ag_recv = refs
    me = lax.axis_index("wa")
    seq = lax.axis_index("seq")
    bits = []
    bit = 1
    while bit < n:
        bits.append(bit)
        bit *= 2

    barrier = pltpu.get_barrier_semaphore()
    pl.semaphore_signal(barrier, inc=1, device_id={"wa": 1 - me}, device_id_type=MESH)
    partners = []
    for b in bits:
        low = lax.rem(lax.div(seq, b), 2)
        partners.append(seq + b - 2 * b * low)
        pl.semaphore_signal(barrier, inc=1, device_id={"seq": partners[-1]}, device_id_type=MESH)
    pl.semaphore_wait(barrier, 1 + len(bits))

    rows_of = 13

    def put(w, tile, value):
        pack[w, tile] = value.astype(BF)

    def rows16(ref, w, r, lanes):
        base = half * w
        if r < rows_of - 1:
            return ref[base + 16 * r : base + 16 * r + 16, lanes]
        top = ref[base + 16 * r : base + 16 * r + 8, lanes]
        if ref.shape[0] > inner:
            return jnp.concatenate([top, ref[inner : inner + 8, lanes]], axis=0)
        return jnp.concatenate([top, jnp.zeros_like(top)], axis=0)

    for w in range(2):
        for (name, used), ref in zip(sections(d, inner), mats):
            count = -(-used // LANES)
            for b in range(count):
                stop = min(used, LANES * (b + 1))
                width = stop - LANES * b
                for r in range(rows_of):
                    value = rows16(ref, w, r, slice(LANES * b, stop))
                    if width < LANES:
                        value = jnp.concatenate([value, jnp.zeros((16, LANES - width), F32)], axis=1)
                    put(w, (starts[name] + b) * rows_of + r, value)
        columns = []
        for ref in vecs:
            total = jnp.sum(ref[...], axis=1, keepdims=True)
            if ref.shape[0] == d:
                columns.append(total[half * 2 * w : half * (2 * w + 1)])
                columns.append(total[half * (2 * w + 1) : half * (2 * w + 2)])
            else:
                columns.append(total[half * w : half * (w + 1)])
        lane = lax.broadcasted_iota(jnp.int32, (half, LANES), 1)
        value = jnp.zeros((half, LANES), F32)
        for at, column in enumerate(columns):
            value = jnp.where(lane == at, column, value)
        value = jnp.concatenate([value, jnp.zeros((rows_of * 16 - half, LANES), F32)], axis=0)
        for r in range(rows_of):
            put(w, starts["vec"] * rows_of + r, value[16 * r : 16 * r + 16])
        filled = blocks * rows_of
        if streams * per > filled:
            pack[w, filled : streams * per] = jnp.zeros((streams * per - filled, 16, LANES), BF)

    exchange = pltpu.make_async_remote_copy(
        src_ref=pack.at[1 - me],
        dst_ref=got,
        send_sem=wa_sem.at[0],
        recv_sem=wa_sem.at[1],
        device_id={"wa": 1 - me},
        device_id_type=MESH,
    )
    exchange.start()
    exchange.wait()

    chunk = 8

    def add_into(dst, dst_at, src, src_at, count):
        def body(i, _):
            total = dst[pl.ds(dst_at + i * chunk, chunk)].astype(F32) + src[pl.ds(src_at + i * chunk, chunk)].astype(F32)
            dst[pl.ds(dst_at + i * chunk, chunk)] = total.astype(BF)
            return 0

        whole_chunks = count // chunk
        if whole_chunks:
            lax.fori_loop(0, whole_chunks, body, 0)
        for i in range(whole_chunks * chunk, count):
            total = dst[pl.ds(dst_at + i, 1)].astype(F32) + src[pl.ds(src_at + i, 1)].astype(F32)
            dst[pl.ds(dst_at + i, 1)] = total.astype(BF)

    mine = pack.at[me]
    add_into(mine, 0, got, 0, streams * per)

    orders = [[(s + k) % len(bits) for k in range(len(bits))] for s in range(streams)]
    offsets = [s * per for s in range(streams)]
    sizes = [per] * streams
    landing = [s * per for s in range(streams)]
    trail = []
    for k in range(len(bits)):
        flights = []
        for s in range(streams):
            which = orders[s][k]
            partner = partners[which]
            size = sizes[s] // 2
            high = lax.rem(lax.div(seq, bits[which]), 2)
            keep = offsets[s] + high * size
            give = offsets[s] + (1 - high) * size
            copy = pltpu.make_async_remote_copy(
                src_ref=mine.at[pl.ds(give, size)],
                dst_ref=rs_got.at[pl.ds(landing[s], size)],
                send_sem=rs_send.at[k, s],
                recv_sem=rs_recv.at[k, s],
                device_id={"seq": partner},
                device_id_type=MESH,
            )
            copy.start()
            flights.append((copy, keep, size, landing[s]))
            landing[s] += size
            offsets[s], sizes[s] = keep, size
        trail.append([(orders[s][k], offsets[s], sizes[s]) for s in range(streams)])
        for copy, keep, size, land in flights:
            copy.wait()
            add_into(mine, keep, rs_got, land, size)
    for s in range(streams):
        size = sizes[s]

        def keep_own(i, _, s=s):
            out[pl.ds(offsets[s] + i, 1)] = mine[pl.ds(offsets[s] + i, 1)]
            return 0

        lax.fori_loop(0, size, keep_own, 0)
    for k in reversed(range(len(bits))):
        flights = []
        for s in range(streams):
            which, at, size = trail[k][s]
            copy = pltpu.make_async_remote_copy(
                src_ref=out.at[pl.ds(at, size)],
                dst_ref=out.at[pl.ds(at, size)],
                send_sem=ag_send.at[k, s],
                recv_sem=ag_recv.at[k, s],
                device_id={"seq": partners[which]},
                device_id_type=MESH,
            )
            copy.start()
            flights.append(copy)
        for copy in flights:
            copy.wait()


def unpack_kernel(plan, packed, *outs):
    d, inner = plan
    half = inner // 2
    starts, _ = section_blocks(d, inner)
    rows_of = 13
    me = lax.axis_index("wa")

    def block(at):
        return packed[at * rows_of : (at + 1) * rows_of].reshape(rows_of * 16, LANES).astype(F32)

    def matrix(name, used):
        parts = [block(starts[name] + b) for b in range(-(-used // LANES))]
        return jnp.concatenate(parts, axis=1)

    def my_half(line, size):
        return jnp.where(me == 0, line[:, 0:size], line[:, size : 2 * size])

    vec = block(starts["vec"])[0:half]
    turned = vec.T

    def write(ref, pieces):
        ref[...] = jnp.concatenate(pieces, axis=1).reshape(ref.shape)

    for side, taps in enumerate((ENCODER_TAPS, DECODER_TAPS)):
        tag = "ed"[side]
        first_g, first_b, red_w, red_b, mid_g, mid_b, ker, ker_b, last_g, last_b, exp_w, exp_b = outs[12 * side : 12 * side + 12]
        at = 8 * side
        write(first_g, [turned[at : at + 1], turned[at + 1 : at + 2]])
        write(first_b, [turned[at + 2 : at + 3], turned[at + 3 : at + 4]])
        write(mid_g, [turned[at + 4 : at + 5]])
        write(mid_b, [turned[at + 5 : at + 6]])
        write(last_g, [turned[at + 6 : at + 7]])
        write(last_b, [turned[at + 7 : at + 8]])
        value = matrix(tag + "_we", d)
        exp_w[...] = value[0:half, 0:d]
        write(exp_b, [my_half(value[half : half + 1, 0:d], d // 2)])
        value = matrix(tag + "_k", taps * inner)
        for j in range(taps):
            ker[j] = value[0:half, j * inner : (j + 1) * inner]
        centre = (ENCODER_SHIFTS if side == 0 else DECODER_SHIFTS).index(0)
        write(ker_b, [my_half(value[half : half + 1, centre * inner : (centre + 1) * inner], half)])
        value = matrix(tag + "_wr", d + AUG)[0:half]
        red_w[...] = value[:, 0:d]
        write(red_b, [value[:, d:].T[0:1]])


def reduce_gradients(mats, vecs, d, inner, n, half_shapes):
    _, blocks = section_blocks(d, inner)
    streams = 3
    total = blocks * 13
    per = -(-total // (streams * n)) * n
    steps = max(1, n.bit_length() - 1)
    vm = pl.BlockSpec(memory_space=pltpu.VMEM)
    count = streams * per
    sem = pltpu.SemaphoreType.DMA
    packed = pl.pallas_call(
        functools.partial(reduce_kernel, (d, inner, n, streams, per)),
        out_shape=jax.ShapeDtypeStruct((count, 16, LANES), BF),
        in_specs=[vm] * 18,
        out_specs=vm,
        scratch_shapes=[
            pltpu.VMEM((2, count, 16, LANES), BF),
            pltpu.VMEM((count, 16, LANES), BF),
            pltpu.VMEM((count, 16, LANES), BF),
            sem((2,)),
            sem((steps, streams)),
            sem((steps, streams)),
            sem((steps, streams)),
            sem((steps, streams)),
        ],
        compiler_params=params(5),
        name="reduce_gradients",
    )(*mats, *vecs)
    return pl.pallas_call(
        functools.partial(unpack_kernel, (d, inner)),
        out_shape=[jax.ShapeDtypeStruct(s, F32) for s in half_shapes],
        in_specs=[vm],
        out_specs=[vm] * 24,
        compiler_params=params(),
        name="unpack_gradients",
    )(packed)


def local(n, stream, doc_start, doc_end, cotangent, *weights):
    rows, d = stream.shape[1], stream.shape[2]
    inner = weights[6].shape[1] * 2
    steps = rows // TILE
    x, cot = stream[0].T, cotangent[0].T
    starts, ends = doc_start, doc_end
    weights = [w.T if at % 12 == 2 else w for at, w in enumerate(weights)]
    enc, dec = gather_weights(weights, d, inner)
    wrt_e, kt_e, wet_e, we_e, kb_e, wr_e, g1_e, b1_e, g2_e, b2_e, g3_e, b3_e = enc
    wrt_d, kt_d, wet_d, we_d, kb_d, wr_d, g1_d, b1_d, g2_d, b2_d, g3_d, b3_d = dec

    def tile(i):
        return (i + steps - 1) % steps

    def cols(channels):
        return pl.BlockSpec((channels, TILE), lambda i: (0, tile(i)))

    per = TILE // LANES

    def block_before(channels):
        return pl.BlockSpec((channels, LANES), lambda i: (0, (per * tile(i) + per * steps - 1) % (per * steps)))

    def block_after(channels):
        return pl.BlockSpec((channels, LANES), lambda i: (0, (per * tile(i) + per) % (per * steps)))

    def spec(a):
        return whole(a.shape)

    def wide(channels, dtype=BF):
        return jax.ShapeDtypeStruct((channels, rows), dtype)

    def fixed(shape, dtype=F32):
        return jax.ShapeDtypeStruct(shape, dtype)

    d1, i1 = d + AUG, inner + AUG
    norm_wide = [(d1, BF), (d, BF), (d, BF), (8, F32)]
    norm_in = [(i1, BF), (inner, BF), (inner, BF), (8, F32)]

    def outs_of(items):
        return [wide(c, t) for c, t in items], [cols(c) for c, _ in items]

    shapes, specs = outs_of(norm_wide + norm_in)
    edge = fixed((inner, LANES), BF)
    ins = [wrt_e, g1_e, b1_e, g2_e, b2_e]
    h1e, z1e, d1e, r1e, h2e, z2e, d2e, r2e, el, er = pl.pallas_call(
        functools.partial(enc_in_kernel, steps),
        grid=(steps,),
        out_shape=shapes + [edge, edge],
        in_specs=[cols(d)] + [spec(a) for a in ins],
        out_specs=specs + [whole(edge.shape)] * 2,
        scratch_shapes=[
            pltpu.VMEM((d, TILE), F32),
            pltpu.VMEM((inner, TILE), F32),
        ]
        + edge_scratch("both", inner),
        compiler_params=params(1),
        name="encoder_in",
    )(x, *ins)

    shapes, specs = outs_of(norm_in + [(d, BF)] + norm_wide + norm_in)
    ins = [kt_e, wet_e, wrt_d, g3_e, b3_e, g1_d, b1_d, g2_d, b2_d]
    h3e, z3e, d3e, r3e, x1, h1d, z1d, d1d, r1d, h2d, z2d, d2d, r2d, eld = pl.pallas_call(
        functools.partial(enc_out_kernel, steps),
        grid=(steps,),
        out_shape=shapes + [edge],
        in_specs=[cols(1), cols(1), block_before(i1), cols(i1), block_after(i1), spec(el), spec(er), cols(d)]
        + [spec(a) for a in ins],
        out_specs=specs + [whole(edge.shape)],
        scratch_shapes=[
            pltpu.VMEM((ENCODER_TAPS * inner + AUG, TILE), BF),
            pltpu.VMEM((inner, LANES), BF),
            pltpu.VMEM((inner, LANES), BF),
            pltpu.VMEM((inner, TILE), F32),
            pltpu.VMEM((d, TILE), F32),
            pltpu.VMEM((inner, TILE), F32),
        ]
        + edge_scratch("right", inner),
        compiler_params=params(2),
        name="encoder_out",
    )(starts, ends, h2e, h2e, h2e, el, er, x, *ins)

    shapes, specs = outs_of([(i1, BF), (inner, BF)])
    sums = [fixed((i1, d)), fixed((inner, LANES)), fixed((inner, LANES))]
    ins = [kt_d, we_d, g3_d, b3_d]
    h3d, evr_d, erd, dwe_d, dg3_d, db3_d = pl.pallas_call(
        functools.partial(dec_out_kernel, steps),
        grid=(steps,),
        out_shape=shapes + [edge] + sums,
        in_specs=[cols(1), cols(1), block_before(i1), cols(i1), spec(eld), cols(d)] + [spec(a) for a in ins],
        out_specs=specs + [whole(edge.shape)] + [whole(s.shape) for s in sums],
        scratch_shapes=[
            pltpu.VMEM((DECODER_TAPS * inner + AUG, TILE), BF),
            pltpu.VMEM((inner, LANES), BF),
            pltpu.VMEM((inner, TILE), F32),
            pltpu.VMEM((inner, TILE), BF),
            pltpu.VMEM((inner, TILE), BF),
            pltpu.VMEM((8, TILE), F32),
            pltpu.VMEM((inner, TILE), F32),
        ]
        + edge_scratch("left", inner),
        compiler_params=params(3),
        name="decoder_out",
    )(starts, ends, h2d, h2d, eld, cot, *ins)

    shapes, specs = outs_of([(d, BF), (inner, BF)])
    small, large = fixed((inner, LANES)), fixed((d, LANES))
    sums = [fixed((i1, DECODER_TAPS * inner)), fixed((inner, d1)), fixed((i1, d))]
    sums += [small, small, large, large, small, small]
    ins = [kb_d, wr_d, we_e, g2_d, g1_d, g3_e]
    stash = [h2d, z2d, d2d, r2d, h1d, z1d, d1d, r1d, cot, h3e, z3e, d3e, r3e]
    ey, evr_e, el2, er2, dk_d, dwr_d, dwe_e, dg2_d, db2_d, dg1_d, db1_d, dg3_e, db3_e = pl.pallas_call(
        functools.partial(dec_back_kernel, steps),
        grid=(steps,),
        out_shape=shapes + [edge, edge] + sums,
        in_specs=[cols(1), cols(1), cols(inner), block_after(inner), spec(erd)]
        + [spec(a) for a in ins]
        + [cols(a.shape[0]) for a in stash],
        out_specs=specs + [whole(edge.shape)] * 2 + [whole(s.shape) for s in sums],
        scratch_shapes=[
            pltpu.VMEM((DECODER_TAPS * inner, TILE), BF),
            pltpu.VMEM((inner, LANES), BF),
            pltpu.VMEM((inner, TILE), F32),
            pltpu.VMEM((d, TILE), F32),
            pltpu.VMEM((inner, TILE), BF),
        ]
        + edge_scratch("both", inner),
        compiler_params=params(4),
        name="decoder_back",
    )(starts, ends, evr_d, evr_d, erd, *ins, *stash)

    sums = [fixed((i1, ENCODER_TAPS * inner)), fixed((inner, d1)), small, small, large, large]
    ins = [kb_e, wr_e, wet_d, g2_e, g1_e]
    stash = [h2e, z2e, d2e, r2e, h1e, z1e, d1e, r1e, ey, x1, h3d]
    full = wide(d, F32)
    out, grad, dk_e, dwr_e, dg2_e, db2_e, dg1_e, db1_e = pl.pallas_call(
        functools.partial(enc_back_kernel, steps),
        grid=(steps,),
        out_shape=[full, full] + sums,
        in_specs=[cols(1), cols(1), block_before(inner), cols(inner), block_after(inner), spec(el2), spec(er2)]
        + [spec(a) for a in ins]
        + [cols(a.shape[0]) for a in stash],
        out_specs=[cols(d), cols(d)] + [whole(s.shape) for s in sums],
        scratch_shapes=[
            pltpu.VMEM((ENCODER_TAPS * inner, TILE), BF),
            pltpu.VMEM((inner, LANES), BF),
            pltpu.VMEM((inner, LANES), BF),
            pltpu.VMEM((inner, TILE), F32),
            pltpu.VMEM((d, TILE), F32),
            pltpu.VMEM((inner, TILE), BF),
        ],
        compiler_params=params(),
        name="encoder_back",
    )(starts, ends, evr_e, evr_e, evr_e, el2, er2, *ins, *stash)

    mats = [dwe_e, dk_e, dwr_e, dwe_d, dk_d, dwr_d]
    vecs = [dg1_e, db1_e, dg2_e, db2_e, dg3_e, db3_e, dg1_d, db1_d, dg2_d, db2_d, dg3_d, db3_d]
    shares = reduce_gradients(mats, vecs, d, inner, n, [w.shape for w in weights])
    shares = [w.T if at % 12 == 2 else w for at, w in enumerate(shares)]
    return (out.T[None], grad.T[None], *shares)


def solution(mesh):
    rows = P("wa", "seq", None)
    block = (
        P("wa"), P("wa"), P(None, "wa"), P("wa"), P("wa"), P("wa"),
        P(None, "wa", None), P("wa"), P("wa"), P("wa"), P("wa", None), P("wa"),
    )
    return jax.shard_map(
        functools.partial(local, mesh.shape["seq"]),
        mesh=mesh,
        in_specs=(rows, P("wa", "seq"), P("wa", "seq"), rows, *block, *block),
        out_specs=(rows, rows, *block, *block),
        check_vma=False,
    )
```

time: 950 us -> 271 us (0.29)
  blocking collectives: 536 us -> 0 us
  Pallas kernels: 0 us -> 270 us
  matrix products: 136 us -> 0 us
  other arithmetic: 135 us -> 0 us
  local copies, waits for them, and re-layouts: 50.5 us -> 0 us
  waiting for transfers between devices: 46.3 us -> 0 us
  starting transfers between devices: 20 us -> 0 us
  between operations: 19 us -> 0.85 us
    psum x1 -> x0, blocking collectives: 511 us -> none  [local(): lax.psum((grad_efg, grad_efb, grad_erw, grad_erb, grad_emg, grad_emb, gra...]
    pallas_call x0 -> x8, Pallas kernels: none -> 270 us  [the longest x1 86 us: reduce_gradients(): pl.pallas_call(functools.partial(reduce_kernel, (d, inner, n, streams, pe...]
    dot_general x18 -> x0, matrix products: 136 us -> none  [the longest x4 40.5 us: contract_cols(): lax.dot_general(left, right, (((1,), (1,)), ((), ())), preferred_element_...]
    reduce_sum x18 -> x0, other arithmetic: 55.9 us -> none  [the longest x2 17.5 us: norm_act(): centre = value - jnp.mean(value, axis=-1, keepdims=True)]
    unnamed x13 -> x0, waiting for transfers between devices: 46.3 us -> none
    unnamed x297 -> x0, local copies, waits for them, and re-layouts: 42.9 us -> none
    convert_element_type x36 -> x0, other arithmetic: 37.8 us -> none  [the longest x15 16.3 us: local(): shares = (lax.psum_scatter(whole_efg.astype(jnp.bfloat16), 'wa', scatter_...]
    ppermute x6 -> x0, starting transfers between devices: 19.5 us -> none  [the longest x2 10.7 us: extended(): before = lax.ppermute(last, axis, up)]
  transfers between devices with their start and end apart: 13 -> 0, of which waited for: 5 -> 0; matrix products, arithmetic and copies ran while one was open for 13% -> 0% of each run, Pallas kernels for 0% -> 0%
where the time goes in v1:
time: 271 us
  Pallas kernels  270 us (100%)
    pallas_call x1, Pallas kernels, reduce_gradients(): pl.pallas_call(functools.partial(reduce_kernel, (d, inner, n, streams, pe...  86 us
    pallas_call x1, Pallas kernels, local(): pl.pallas_call(functools.partial(enc_out_kernel, steps), grid=(steps,), o...  39.3 us
    pallas_call x1, Pallas kernels, local(): pl.pallas_call(functools.partial(dec_back_kernel, steps), grid=(steps,),...  35.8 us
    pallas_call x1, Pallas kernels, local(): pl.pallas_call(functools.partial(enc_back_kernel, steps), grid=(steps,),...  34.8 us
    pallas_call x1, Pallas kernels, local(): pl.pallas_call(functools.partial(enc_in_kernel, steps), grid=(steps,), ou...  27.4 us
    pallas_call x1, Pallas kernels, local(): pl.pallas_call(functools.partial(dec_out_kernel, steps), grid=(steps,), o...  25.5 us
    pallas_call x1, Pallas kernels, gather_weights(): pl.pallas_call(functools.partial(weights_kernel, (d, inner, taps)), out_s...  16.3 us

profile of v1, /device:TPU:0, one launch (start us, length us, event | category | flops | bytes accessed | tf_op | source)
XLA Modules:
  0.0 270.9 jit_solution(10562985460821086014)
XLA Ops:
  0.7 16.3 %gather_weights.1 = (bf16[400,816]{1,0:T(8,128)(2,1)}, bf16[400,2016]{1,0:T(8,128)(2,1)}, bf16[800,416]{1,0:T(8,128)(2,1)}, bf16[400,800]{1,0:T(8,128)(2,1)}, bf...) custom-call(bf16[400]{0:T(512)(128)(2,1)} %refs_0_.1, ...), custom_call_target="tpu_custom_call" | custom-call | tf_op jit(solution)/shard_map/gather_weights/pallas_call | solution.py:182
  17.0 27.4 %encoder_in.1 = (bf16[816,3072]{1,0:T(8,128)(2,1)}, bf16[800,3072]{1,0:T(8,128)(2,1)}, bf16[800,3072]{1,0:T(8,128)(2,1)}, f32[8,3072]{1,0:T(8,128)}, bf16[416,30...) custom-call(bf16[800,3072]{1,0:T(8,128)(2,1)} %bitcast.18, ...), custom_call_target="tpu_custom_call" | custom-call | tf_op jit(solution)/shard_map/encoder_in/pallas_call | solution.py:827
  44.3 39.3 %encoder_out.1 = (bf16[416,3072]{1,0:T(8,128)(2,1)}, bf16[400,3072]{1,0:T(8,128)(2,1)}, bf16[400,3072]{1,0:T(8,128)(2,1)}, f32[8,3072]{1,0:T(8,128)}, bf16[800,3...) custom-call(s32[1,3072]{1,0:T(1,128)} %starts.7, ...), custom_call_target="tpu_custom_call" | custom-call | tf_op jit(solution)/shard_map/encoder_out/pallas_call | solution.py:844
  83.7 25.5 %decoder_out.1 = (bf16[416,3072]{1,0:T(8,128)(2,1)}, bf16[400,3072]{1,0:T(8,128)(2,1)}, bf16[400,128]{1,0:T(8,128)(2,1)}, f32[416,800]{1,0:T(8,128)}, f32[400,128]{1,0:T(8,128)}, /*index=5*/f32[400,128]{1,0:T(8,128)}) custom-call(s32[1,3072]{1,0:T(1,128)} %starts.7, s32[1,3072]{1,0:T(1,128)} %ends.7, bf16[416,3072]{1,0:T(8,128)(2,1)} %get-tuple-element.142.before.main.h2, ...), custom_call_target="tpu_custom_call" | custom-call | tf_op jit(solution)/shard_map/decoder_out/pallas_call | solution.py:867
  109.2 35.8 %decoder_back.1 = (bf16[800,3072]{1,0:T(8,128)(2,1)}, bf16[400,3072]{1,0:T(8,128)(2,1)}, bf16[400,128]{1,0:T(8,128)(2,1)}, bf16[400,128]{1,0:T(8,128)(2,1)}, f32...) custom-call(s32[1,3072]{1,0:T(1,128)} %starts.7, ...), custom_call_target="tpu_custom_call" | custom-call | tf_op jit(solution)/shard_map/decoder_back/pallas_call | solution.py:893
  145.0 34.8 %encoder_back.1 = (f32[800,3072]{1,0:T(8,128)}, f32[800,3072]{1,0:T(8,128)}, f32[416,2000]{1,0:T(8,128)}, f32[400,816]{1,0:T(8,128)}, f32[400,128]{1,0:T(8,128)}...) custom-call(s32[1,3072]{1,0:T(1,128)} %starts.7, s32[1,3072]{1,0:T(1,128)} %ends.7, ...), custom_call_target="tpu_custom_call" | custom-call | tf_op jit(solution)/shard_map/encoder_back/pallas_call | solution.py:917
  179.7 86.0 %reduce_gradients.1.packed = bf16[720,16,128]{2,1,0:T(8,128)(2,1)} custom-call(f32[416,800]{1,0:T(8,128)} %get-tuple-element.182.refs_0_, f32[416,2000]{1,0:T(8,128)} %get-tuple-element.183.refs_1_, f32[400,816]{1,0:T(8,128)} %get-tuple-element.184.refs_2_, f32[416,800]{1,0:T(8,128)} %get-tuple-element.185.refs_3_, f32[416,1200]{1,0:T(8,128)} %get-tuple-element.186.refs_4_, ...), custom_call_target="tpu_custom_call" | custom-call | tf_op jit(solution)/shard_map/reduce_gradients/pallas_call | solution.py:755
  265.7 5.1 %unpack_gradients.1 = (f32[400]{0:T(512)}, f32[400]{0:T(512)}, f32[200,800]{1,0:T(8,128)}, f32[200]{0:T(256)}, f32[200]{0:T(256)}, /*index=5*/f32[200]{0:T(256)}...) custom-call(bf16[720,16,128]{2,1,0:T(8,128)(2,1)} %reduce_gradients., ...), custom_call_target="tpu_custom_call" | custom-call | tf_op jit(solution)/shard_map/unpack_gradients/pallas_call | solution.py:773

commit v2 on v1

v2 whole, which is shorter than its diff:
```python
import functools

import jax
import jax.numpy as jnp
from jax import lax
from jax.experimental import pallas as pl
from jax.experimental.pallas import tpu as pltpu
from jax.sharding import PartitionSpec as P

ENCODER_TAPS = 5
ENCODER_DILATION = 8
DECODER_TAPS = 3
DECODER_DILATION = 16
EPS = 1e-05

MESH = pl.DeviceIdType.MESH
BF = jnp.bfloat16
F32 = jnp.float32
LANES = 128
TILE = 512
HALF = 256
AUG = 16
VMEM_LIMIT = 56 * 1024 * 1024
GELU_1 = 2.0 * 0.7978845608028654
GELU_3 = 8.0 * 0.7978845608028654 * 0.044715

ENCODER_SHIFTS = tuple(ENCODER_DILATION * (j - ENCODER_TAPS // 2) for j in range(ENCODER_TAPS))
DECODER_SHIFTS = tuple(-DECODER_DILATION * (DECODER_TAPS - 1 - j) for j in range(DECODER_TAPS))


def params(collective=None):
    if collective is None:
        return pltpu.CompilerParams(vmem_limit_bytes=VMEM_LIMIT)
    return pltpu.CompilerParams(
        vmem_limit_bytes=VMEM_LIMIT, collective_id=collective, has_side_effects=True
    )


def whole(shape):
    return pl.BlockSpec(shape, lambda *_: (0,) * len(shape))


def nt_dot(left, right):
    return lax.dot_general(left, right, (((1,), (1,)), ((), ())), preferred_element_type=F32)


def nn_dot(left, right):
    return jnp.dot(left, right, preferred_element_type=F32)


def lanes_of(column, width):
    return jnp.concatenate([column] * (width // LANES), axis=1)


def fold(value):
    total = value[:, :LANES]
    for at in range(LANES, value.shape[1], LANES):
        total = total + value[:, at : at + LANES]
    return total


def weights_kernel(dims, *refs):
    d, inner, taps = dims
    n_in = 24
    ins, refs = refs[:n_in], refs[n_in:]
    outs, refs = refs[:30], refs[30:]
    (small_own, small_got, k_own0, k_own1, e_own0, e_own1, r_own0, r_own1, *rest) = refs
    (r_got0, r_got1, k_got0, k_got1, e_got0, e_got1, send, recv) = rest
    me = lax.axis_index("wa")
    other = 1 - me
    barrier = pltpu.get_barrier_semaphore()
    pl.semaphore_signal(barrier, inc=1, device_id={"wa": other}, device_id_type=MESH)
    pl.semaphore_wait(barrier, 1)

    half = inner // 2
    pad = k_own0.shape[1]
    small_own[...] = jnp.zeros_like(small_own)
    small_at = []
    for side in range(2):
        for at in (0, 1, 3, 4, 5, 7, 8, 9, 11):
            small_at.append(12 * side + at)
    for row, at in enumerate(small_at):
        n = ins[at].shape[0]
        small_own[row : row + 1, 0:n] = ins[at][...].astype(F32).reshape(1, n)
    owns, gots = [], []
    for side, (k_own, e_own, r_own) in enumerate(((k_own0, e_own0, r_own0), (k_own1, e_own1, r_own1))):
        base = 12 * side
        k_own[:, half - 8 : pad, :] = jnp.zeros((taps[side], pad - half + 8, inner), BF)
        k_own[:, 0:half, :] = ins[base + 6][...]
        e_own[half - 8 : pad, :] = jnp.zeros((pad - half + 8, d), BF)
        e_own[0:half, :] = ins[base + 10][...]
        r_own[half - 8 : pad, :] = jnp.zeros((pad - half + 8, d), BF)
        r_own[0:half, :] = ins[base + 2][...]
        owns += [r_own, k_own, e_own]
    owns.append(small_own)
    gots = [r_got0, k_got0, e_got0, r_got1, k_got1, e_got1, small_got]
    copies = []
    for at, (own, got) in enumerate(zip(owns, gots)):
        copies.append(
            pltpu.make_async_remote_copy(
                src_ref=own,
                dst_ref=got,
                send_sem=send.at[at],
                recv_sem=recv.at[at],
                device_id={"wa": other},
                device_id_type=MESH,
            )
        )
        copies[-1].start()
    for copy in copies:
        copy.wait()

    first_core = me == 0

    def ordered(own, got):
        own, got = own.astype(F32), got.astype(F32)
        return jnp.where(first_core, own, got), jnp.where(first_core, got, own)

    small0, small1 = ordered(small_own[...], small_got[...])

    def column(row, n):
        line = jnp.concatenate([small0[row : row + 1, 0 : n // 2], small1[row : row + 1, 0 : n // 2]], axis=1)
        return jnp.broadcast_to(line, (LANES, n)).T

    def bias_columns(value):
        where = lax.broadcasted_iota(jnp.int32, (value.shape[0], AUG), 1) == 0
        return jnp.where(where, value[:, :AUG], 0.0).astype(BF)

    for side in range(2):
        o = outs[15 * side : 15 * side + 15]
        wrt, kt, wet, we, kb, wr, *vectors = o
        base = 9 * side
        for at, (row, n) in enumerate(((0, d), (3, inner), (6, inner))):
            gain, half_gain, half_bias = vectors[3 * at : 3 * at + 3]
            gain[...] = column(base + row, n)
            half_gain[...] = gain[...] * 0.5
            half_bias[...] = column(base + row + 1, n) * 0.5
        n = taps[side]
        r0, r1 = ordered(owns[3 * side][0:half, :], gots[3 * side][0:half, :])
        r = jnp.concatenate([r0, r1], axis=0)
        wr[...] = r.T.astype(BF)
        wrt[:, 0:d] = r.astype(BF)
        wrt[:, d : d + AUG] = bias_columns(column(base + 2, inner))
        e0, e1 = ordered(owns[3 * side + 2][0:half, :], gots[3 * side + 2][0:half, :])
        e = jnp.concatenate([e0, e1], axis=0)
        we[...] = e.astype(BF)
        wet[:, 0:inner] = e.T.astype(BF)
        wet[:, inner : inner + AUG] = bias_columns(column(base + 8, d))
        for j in range(n):
            k0, k1 = ordered(owns[3 * side + 1][j, 0:half, :], gots[3 * side + 1][j, 0:half, :])
            k = jnp.concatenate([k0, k1], axis=0)
            kb[:, j * inner : (j + 1) * inner] = k.astype(BF)
            kt[:, j * inner : (j + 1) * inner] = k.T.astype(BF)
        kt[:, n * inner : n * inner + AUG] = bias_columns(column(base + 5, inner))


def gather_weights(args, d, inner):
    taps = (ENCODER_TAPS, DECODER_TAPS)
    half = inner // 2
    pad = -(-half // 16) * 16
    shapes = []
    for n in taps:
        shapes += [
            ((inner, d + AUG), BF),
            ((inner, n * inner + AUG), BF),
            ((d, inner + AUG), BF),
            ((inner, d), BF),
            ((inner, n * inner), BF),
            ((d, inner), BF),
        ]
        for c in (d, inner, inner):
            shapes += [((c, LANES), F32)] * 3
    vm = pl.BlockSpec(memory_space=pltpu.VMEM)
    small = pltpu.VMEM((24, 512), F32)
    kk = [pltpu.VMEM((n, pad, inner), BF) for n in taps]
    ee = [pltpu.VMEM((pad, d), BF)] * 2
    outs = pl.pallas_call(
        functools.partial(weights_kernel, (d, inner, taps)),
        out_shape=[jax.ShapeDtypeStruct(*s) for s in shapes],
        in_specs=[vm] * 24,
        out_specs=[vm] * 30,
        scratch_shapes=[small, small, *kk, *ee, *ee, *ee, *kk, *ee]
        + [pltpu.SemaphoreType.DMA((7,)), pltpu.SemaphoreType.DMA((7,))],
        compiler_params=params(0),
        name="gather_weights",
    )(*args)
    return outs[:15], outs[15:]


def pacing(thunks, slots):
    state = [0, 0]
    thunks = list(thunks)

    def between():
        while state[1] < len(thunks) and state[0] * len(thunks) >= state[1] * slots:
            thunks[state[1]]()
            state[1] += 1
        state[0] += 1

    return between


def add_product(total, left, right):
    def piece(at, stop):
        total[:, at:stop] += nt_dot(left[...], right[at:stop, :])

    columns = right.shape[0]
    return [functools.partial(piece, at, min(at + HALF, columns)) for at in range(0, columns, HALF)]


def norm_forward(src, lanes, channels, gain, bias, h_out, z_out, d_out, r_out, keep=None, fill=()):
    width = lanes.stop - lanes.start
    between = pacing(fill, 3 * (channels // 16))
    total = [jnp.zeros((8, width), F32) for _ in range(4)]
    for c in range(0, channels, 16):
        between()
        x = src[c : c + 16, lanes].astype(F32)
        if keep is not None:
            keep[c : c + 16, lanes] = x
        at = (c // 8) % 4
        total[at] = total[at] + x[0:8]
        total[at + 1] = total[at + 1] + x[8:16]
    mean = jnp.sum((total[0] + total[1]) + (total[2] + total[3]), axis=0, keepdims=True) * (1.0 / channels)
    wide = jnp.broadcast_to(mean, (16, width))
    values = src if keep is None else keep
    total = [jnp.zeros((8, width), F32) for _ in range(4)]
    for c in range(0, channels, 16):
        between()
        centre = values[c : c + 16, lanes] - wide
        square = centre * centre
        at = (c // 8) % 4
        total[at] = total[at] + square[0:8]
        total[at + 1] = total[at + 1] + square[8:16]
    spread = jnp.sum((total[0] + total[1]) + (total[2] + total[3]), axis=0, keepdims=True) * (1.0 / channels)
    r = lax.rsqrt(spread + EPS)
    if r_out is not None:
        r_out[:, lanes] = jnp.broadcast_to(r, (8, width))
    rw = jnp.broadcast_to(r, (16, width))
    mw = jnp.broadcast_to(mean * r, (16, width))
    one, point = BF(1.0), BF(0.5)
    for c in range(0, channels, 16):
        between()
        rows = slice(c, c + 16)
        z = values[rows, lanes] * rw - mw
        half = (z * lanes_of(gain[rows, :], width) + lanes_of(bias[rows, :], width)).astype(BF)
        sq = half * half
        t = jnp.tanh(half * (sq * BF(GELU_3) + BF(GELU_1)))
        up = one + t
        h_out[rows, lanes] = half * up
        d_out[rows, lanes] = up * (point + half * (sq * BF(1.5 * GELU_3) + BF(0.5 * GELU_1)) * (one - t))
        z_out[rows, lanes] = z.astype(BF)


def norm_backward(grad, lanes, channels, gain, z_in, d_in, r_in, gain_sum, bias_sum, keep, emit, fill=()):
    width = lanes.stop - lanes.start
    between = pacing(fill, 2 * (channels // 16))
    one = [jnp.zeros((8, width), F32) for _ in range(2)]
    two = [jnp.zeros((8, width), F32) for _ in range(2)]
    r = r_in[0:1, lanes]
    rw = jnp.broadcast_to(r, (16, width))
    for c in range(0, channels, 16):
        between()
        rows = slice(c, c + 16)
        da = grad[rows, lanes] * d_in[rows, lanes].astype(F32)
        p = da * z_in[rows, lanes].astype(F32)
        bias_sum[rows, :] += fold(da)
        gain_sum[rows, :] += fold(p)
        wide = lanes_of(gain[rows, :], width)
        dz = da * wide
        q = p * wide
        keep[rows, lanes] = (dz * rw).astype(BF)
        for at in range(2):
            one[at] = one[at] + dz[8 * at : 8 * at + 8]
            two[at] = two[at] + q[8 * at : 8 * at + 8]
    scale = r * (1.0 / channels)
    m1 = jnp.broadcast_to(jnp.sum(one[0] + one[1], axis=0, keepdims=True) * scale, (16, width)).astype(BF)
    m2 = jnp.broadcast_to(jnp.sum(two[0] + two[1], axis=0, keepdims=True) * scale, (16, width)).astype(BF)
    for c in range(0, channels, 16):
        between()
        rows = slice(c, c + 16)
        emit(rows, keep[rows, lanes] - (z_in[rows, lanes] * m2 + m1))


def tap_mask(starts, ends, first, shift):
    place = first + shift + lax.broadcasted_iota(jnp.int32, (8, TILE), 1)
    usable = (place >= jnp.broadcast_to(starts[...], (8, TILE))) & (place < jnp.broadcast_to(ends[...], (8, TILE)))
    one = jnp.where(usable, 1.0, 0.0)
    return jnp.concatenate([one, one], axis=0).astype(BF)


def stack_taps(stack, shifts, before, main, after, starts, ends, first, inner):
    for j, shift in enumerate(shifts):
        if not shift:
            stack[j * inner : (j + 1) * inner, :] = main[0:inner, :]
            continue
        mask = tap_mask(starts, ends, first, shift)
        for c in range(0, inner, 16):
            rows = slice(c, c + 16)
            if shift < 0:
                span = jnp.concatenate([before[rows, :], main[rows, :]], axis=1)
                span = pltpu.roll(span, -shift, 1)[:, LANES:]
            else:
                span = jnp.concatenate([main[rows, :], after[rows, :]], axis=1)
                span = pltpu.roll(span, TILE + LANES - shift, 1)[:, :TILE]
            stack[j * inner + c : j * inner + c + 16, :] = span * mask


def ones_rows(width):
    where = lax.broadcasted_iota(jnp.int32, (AUG, width), 0) == 0
    return jnp.where(where, 1.0, 0.0).astype(BF)


def neighbours():
    me = lax.axis_index("seq")
    n = lax.axis_size("seq")
    return lax.rem(me + n - 1, n), lax.rem(me + 1, n)


def greet(others):
    barrier = pltpu.get_barrier_semaphore()
    for device in others:
        pl.semaphore_signal(barrier, inc=1, device_id=device, device_id_type=MESH)
    pl.semaphore_wait(barrier, len(others))


def send_copy(src, dst, send_sem, recv_sem, device):
    return pltpu.make_async_remote_copy(
        src_ref=src, dst_ref=dst, send_sem=send_sem, recv_sem=recv_sem, device_id=device, device_id_type=MESH
    )


def later_tile(step, steps):
    return lax.rem(step + 1, steps)


def first_place(tile, steps):
    return lax.axis_index("seq") * (steps * TILE) + tile * TILE


CHAINS = (slice(0, HALF), slice(HALF, TILE))


def enc_in_kernel(x, wrt, g1, b1, g2, b2, h1, z1, d1, r1, h2, z2, d2, r2, xt, u):
    d, inner = x.shape[0], wrt.shape[0]
    h1[d : d + AUG, :] = ones_rows(TILE)
    h2[inner : inner + AUG, :] = ones_rows(TILE)
    one, two = CHAINS

    def make_u(lanes):
        u[:, lanes] = nn_dot(wrt[...], h1[:, lanes])

    norm_forward(x, one, d, g1, b1, h1, z1, d1, r1, xt)
    norm_forward(x, two, d, g1, b1, h1, z1, d1, r1, xt, [lambda: make_u(one)])
    norm_forward(u, one, inner, g2, b2, h2, z2, d2, r2, None, [lambda: make_u(two)])
    norm_forward(u, two, inner, g2, b2, h2, z2, d2, r2)


def choose_edge(window, block, edge, at_end):
    window[...] = block[0 : window.shape[0], :]

    @pl.when(at_end)
    def _():
        window[...] = edge[0 : window.shape[0], :]


def trade_edges(step, steps, head, tail, got_l, got_r, send, recv, others=()):
    left, right = neighbours()
    to_left = send_copy(head, got_r, send.at[0], recv.at[0], {"seq": left})
    to_right = send_copy(tail, got_l, send.at[1], recv.at[1], {"seq": right})

    @pl.when(step == 0)
    def _():
        greet([{"seq": left}, {"seq": right}, *others])
        to_left.start()
        to_right.start()

    @pl.when(step == steps - 2)
    def _():
        to_left.wait()
        to_right.wait()


def enc_out_kernel(
    steps, starts, ends, before, main, after, head, tail, xt, kt, wet, wrt, g3, b3, g1, b1, g2, b2,
    h3, z3, d3, r3, x1, h1, z1, d1, r1, h2, z2, d2, r2, edge_o,
    stack, win_b, win_a, v, y, u, got_l, got_r, own, got, send, recv,
):
    step = pl.program_id(0)
    d, inner = xt.shape[0], v.shape[0]
    trade_edges(step, steps, head, tail, got_l, got_r, send, recv)
    choose_edge(win_b, before, got_l, step == steps - 1)
    choose_edge(win_a, after, got_r, step == steps - 2)
    stack_taps(stack, ENCODER_SHIFTS, win_b, main, win_a, starts, ends, first_place(later_tile(step, steps), steps), inner)
    stack[len(ENCODER_SHIFTS) * inner :, :] = ones_rows(TILE)
    h3[inner : inner + AUG, :] = ones_rows(TILE)
    h1[d : d + AUG, :] = ones_rows(TILE)
    h2[inner : inner + AUG, :] = ones_rows(TILE)
    one, two = CHAINS

    def make_v(lanes):
        v[:, lanes] = nn_dot(kt[...], stack[:, lanes])

    def make_y(lanes):
        y[:, lanes] = nn_dot(wet[...], h3[:, lanes]) + xt[:, lanes].astype(F32)

    def make_u(lanes):
        u[:, lanes] = nn_dot(wrt[...], h1[:, lanes])

    def norm_last(lanes, fill):
        norm_forward(v, lanes, inner, g3, b3, h3, z3, d3, r3, None, fill)

    def norm_first(lanes, fill):
        for c in range(0, d, 16):
            x1[c : c + 16, lanes] = y[c : c + 16, lanes].astype(BF)
        norm_forward(y, lanes, d, g1, b1, h1, z1, d1, r1, None, fill)

    make_v(one)
    norm_last(one, [lambda: make_v(two)])
    norm_last(two, [lambda: make_y(one)])
    norm_first(one, [lambda: make_y(two)])
    norm_first(two, [lambda: make_u(one)])
    norm_forward(u, one, inner, g2, b2, h2, z2, d2, r2, None, [lambda: make_u(two)])
    norm_forward(u, two, inner, g2, b2, h2, z2, d2, r2)

    def give():
        return send_copy(own, got, send.at[2], recv.at[2], {"seq": neighbours()[1]})

    @pl.when(step == steps - 2)
    def _():
        own[...] = h2[:, TILE - LANES : TILE]
        give().start()

    @pl.when(step == steps - 1)
    def _():
        give().wait()
        edge_o[...] = got[...]


def dec_out_kernel(
    steps, starts, ends, before, main, e_l, cot_t, x1, kt, we, wet, f3, b3, g3,
    out, evr, dwe, dg3, db3,
    stack, win_b, v, h3, z3, d3, r3, g, kept,
):
    step = pl.program_id(0)
    inner = v.shape[0]

    @pl.when(step == 0)
    def _():
        dwe[...] = jnp.zeros_like(dwe)
        dg3[...] = jnp.zeros_like(dg3)
        db3[...] = jnp.zeros_like(db3)

    choose_edge(win_b, before, e_l, step == 0)
    stack_taps(stack, DECODER_SHIFTS, win_b, main, None, starts, ends, first_place(step, steps), inner)
    stack[len(DECODER_SHIFTS) * inner :, :] = ones_rows(TILE)
    h3[inner : inner + AUG, :] = ones_rows(TILE)
    one, two = CHAINS

    def make_v(lanes):
        v[:, lanes] = nn_dot(kt[...], stack[:, lanes])

    def make_g(lanes):
        g[:, lanes] = nn_dot(we[...], cot_t[:, lanes])

    def back(lanes, fill):
        def emit(rows, value):
            evr[rows, lanes] = value

        norm_backward(g, lanes, inner, g3, z3, d3, r3, dg3, db3, kept, emit, fill)

    def make_out(lanes):
        out[:, lanes] = nn_dot(wet[...], h3[:, lanes]) + x1[:, lanes].astype(F32)

    make_g(one)
    make_g(two)
    make_v(one)
    norm_forward(v, one, inner, f3, b3, h3, z3, d3, r3, None, [lambda: make_v(two)])
    norm_forward(v, two, inner, f3, b3, h3, z3, d3, r3)
    products = add_product(dwe, h3, cot_t)
    back(one, [lambda: make_out(one), *products[:2]])
    back(two, [lambda: make_out(two), *products[2:]])


def dec_back_kernel(
    plan, starts, ends, main, after, head, kb, wr, we, g2, g1, g3,
    h2, z2, d2, r2, h1, z1, d1, r1, cot_t, h3, z3, d3, r3, dwe_d,
    ey, evr, packed, dg2, db2, dg1, db1, dg3, db3,
    dk, dwrt, dwe, stack, win_a, g, big, eur, kept, got, send, recv,
):
    steps = plan.steps
    step = pl.program_id(0)
    d, inner = cot_t.shape[0], g.shape[0]

    @pl.when(step == 0)
    def _():
        for ref in (dk, dwrt, dwe, dg2, db2, dg1, db1, dg3, db3):
            ref[...] = jnp.zeros_like(ref)

    left, right = neighbours()
    to_left = send_copy(head, got, send.at[0], recv.at[0], {"seq": left})

    @pl.when(step == 0)
    def _():
        greet([{"seq": left}, {"seq": right}])
        to_left.start()

    @pl.when(step == steps - 1)
    def _():
        to_left.wait()

    choose_edge(win_a, after, got, step == steps - 1)
    back = tuple(-s for s in DECODER_SHIFTS)
    stack_taps(stack, back, None, main, win_a, starts, ends, first_place(step, steps), inner)
    one, two = CHAINS

    def make_g2(lanes):
        g[:, lanes] = nn_dot(kb[...], stack[:, lanes])

    def make_g1(lanes):
        big[:, lanes] = nn_dot(wr[...], eur[:, lanes])

    def make_g3(lanes):
        g[:, lanes] = nn_dot(we[...], ey[:, lanes])

    def back2(lanes, fill):
        def emit(rows, value):
            eur[rows, lanes] = value

        norm_backward(g, lanes, inner, g2, z2, d2, r2, dg2, db2, kept, emit, fill)

    def back1(lanes, fill):
        def emit(rows, value):
            ey[rows, lanes] = value + cot_t[rows, lanes]

        norm_backward(big, lanes, d, g1, z1, d1, r1, dg1, db1, kept, emit, fill)

    def back3(lanes, fill):
        def emit(rows, value):
            evr[rows, lanes] = value

        norm_backward(g, lanes, inner, g3, z3, d3, r3, dg3, db3, kept, emit, fill)

    make_g2(one)
    by_k = add_product(dk, h2, stack)
    back2(one, [lambda: make_g2(two)])
    back2(two, [lambda: make_g1(one)])
    by_r = add_product(dwrt, eur, h1)
    back1(one, [lambda: make_g1(two), *by_k[:3]])
    back1(two, [lambda: make_g3(one), *by_k[3:], *by_r[:2]])
    make_g3(two)
    by_e = add_product(dwe, h3, ey)
    back3(one, [*by_r[2:], *by_e[:1]])
    back3(two, by_e[1:])

    @pl.when(step == steps - 1)
    def _():
        pack_gradients(packed, plan, ((dwe_d, d), (dk, dk.shape[1]), (dwrt, d + AUG), (dwe, d)), ())


def enc_back_kernel(
    plan, starts, ends, before, main, after, head, tail, kb, wr, g2, g1,
    h2, z2, d2, r2, h1, z1, d1, r1, ey, given, *rest,
):
    vecs, rest = rest[:8], rest[8:]
    (
        grad, packed, summed,
        dk, dwrt, dg2, db2, dg1, db1,
        stack, win_b, win_a, g, big, eur, kept, got_l, got_r, send, recv,
    ), traffic = rest[:20], rest[20:]
    steps = plan.steps
    step = pl.program_id(0)
    d, inner = ey.shape[0], g.shape[0]

    @pl.when(step == 0)
    def _():
        for ref in (dk, dwrt, dg2, db2, dg1, db1):
            ref[...] = jnp.zeros_like(ref)

    sum_over = Summing(plan.early, given, summed, traffic)
    trade_edges(step, steps, head, tail, got_l, got_r, send, recv, sum_over.partners())

    stage_count = sum_over.steps + 2
    due = [0, 2] + [6 + 6 * i // max(1, stage_count - 3) for i in range(stage_count - 2)]

    def hook(at):
        for stage, place in enumerate(due):
            where = (place // 2, place % 2) if place < 2 * steps else (steps - 1, 2)
            if where[1] == at:

                @pl.when(step == where[0])
                def _(stage=stage):
                    sum_over.reduce_stage(stage)

    hook(0)
    choose_edge(win_b, before, got_l, step == steps - 1)
    choose_edge(win_a, after, got_r, step == steps - 2)
    back = tuple(-s for s in ENCODER_SHIFTS)
    stack_taps(stack, back, win_b, main, win_a, starts, ends, first_place(later_tile(step, steps), steps), inner)
    one, two = CHAINS

    def make_g2(lanes):
        g[:, lanes] = nn_dot(kb[...], stack[:, lanes])

    def make_g1(lanes):
        big[:, lanes] = nn_dot(wr[...], eur[:, lanes])

    def back2(lanes, fill):
        def emit(rows, value):
            eur[rows, lanes] = value

        norm_backward(g, lanes, inner, g2, z2, d2, r2, dg2, db2, kept, emit, fill)

    def back1(lanes, fill):
        def emit(rows, value):
            grad[rows, lanes] = value + ey[rows, lanes]

        norm_backward(big, lanes, d, g1, z1, d1, r1, dg1, db1, kept, emit, fill)

    make_g2(one)
    by_k = add_product(dk, h2, stack)
    back2(one, [lambda: make_g2(two)])
    back2(two, [lambda: make_g1(one), *by_k[:1]])
    hook(1)
    by_r = add_product(dwrt, eur, h1)
    back1(one, [lambda: make_g1(two), *by_k[1:5]])
    back1(two, [*by_k[5:], *by_r])

    @pl.when(step == steps - 1)
    def _():
        sums = (dg1, db1, dg2, db2, *vecs)
        pack_gradients(packed, plan, ((dk, dk.shape[1]), (dwrt, d + AUG)), sums)

    hook(2)


ROWS_OF = 13


def blocks_of(used):
    return -(-used // LANES)


class Part:
    def __init__(self, sections, vectors, streams, n):
        self.starts, at = {}, 0
        for name, used in sections:
            self.starts[name] = (at, used)
            at += blocks_of(used)
        if vectors:
            self.starts["vec"] = (at, LANES)
            at += 1
        self.filled = at * ROWS_OF
        self.streams = streams
        self.per = -(-self.filled // (streams * n)) * n
        self.pieces = streams * self.per
        self.n = n
        self.bits = []
        while 1 << len(self.bits) < n:
            self.bits.append(1 << len(self.bits))


class Plan:
    def __init__(self, d, inner, steps, n):
        self.d, self.inner, self.steps, self.n = d, inner, steps, n
        early = (("d_we", d), ("d_k", DECODER_TAPS * inner), ("d_wr", d + AUG), ("e_we", d))
        self.early = Part(early, False, 2, n)
        self.late = Part((("e_k", ENCODER_TAPS * inner), ("e_wr", d + AUG)), True, 4, n)


def pack_gradients(packed, plan, mats, vecs):
    d, inner = plan.d, plan.inner
    half = inner // 2
    for w in range(2):
        at = 0
        for ref, used in mats:
            for b in range(blocks_of(used)):
                stop = min(used, LANES * (b + 1))
                lanes = slice(LANES * b, stop)
                for r in range(ROWS_OF):
                    base = half * w + 16 * r
                    if r < ROWS_OF - 1:
                        value = ref[base : base + 16, lanes]
                    else:
                        value = ref[base : base + 8, lanes]
                        low = ref[inner : inner + 8, lanes] if ref.shape[0] > inner else jnp.zeros_like(value)
                        value = jnp.concatenate([value, low], axis=0)
                    if stop - LANES * b < LANES:
                        blank = jnp.zeros((16, LANES * (b + 1) - stop), F32)
                        value = jnp.concatenate([value, blank], axis=1)
                    packed[w, at] = value.astype(BF)
                    at += 1
        if vecs:
            columns = []
            for ref in vecs:
                total = jnp.sum(ref[...], axis=1, keepdims=True)
                if ref.shape[0] == d:
                    columns.append(total[2 * half * w : 2 * half * w + half])
                    columns.append(total[2 * half * w + half : 2 * half * w + 2 * half])
                else:
                    columns.append(total[half * w : half * (w + 1)])
            lane = lax.broadcasted_iota(jnp.int32, (half, LANES), 1)
            value = jnp.zeros((half, LANES), F32)
            for lane_at, column in enumerate(columns):
                value = jnp.where(lane == lane_at, column, value)
            value = jnp.concatenate([value, jnp.zeros((ROWS_OF * 16 - half, LANES), F32)], axis=0)
            for r in range(ROWS_OF):
                packed[w, at] = value[16 * r : 16 * r + 16].astype(BF)
                at += 1
        left = packed.shape[1] - at
        if left:
            packed[w, at : packed.shape[1]] = jnp.zeros((left, 16, LANES), BF)


def in_chunks(count, body):
    size = max(c for c in range(1, 17) if count % c == 0)

    def step(i, _):
        body(i * size, size)
        return 0

    lax.fori_loop(0, count // size, step, 0)


def copy_pieces(dst, src, at, count):
    dst[pl.ds(at, count)] = src[pl.ds(at, count)]


class Summing:
    def __init__(self, part, given, out, traffic):
        self.part, self.given, self.out = part, given, out
        self.got, self.total, self.leave, self.landed, self.core, self.down, *up = traffic
        self.up = up[0] if up else None
        self.me = lax.axis_index("wa")
        self.seq = lax.axis_index("seq")
        self.steps = len(part.bits)
        self.orders = []
        for s in range(part.streams):
            order = list(range(self.steps))
            if s % 2 and self.steps > 1:
                order[0], order[1] = order[1], order[0]
            self.orders.append(order)

    @staticmethod
    def scratch(part):
        sem = pltpu.SemaphoreType.DMA
        steps = max(1, len(part.bits))
        pieces = (part.pieces, 16, LANES)
        return [
            pltpu.VMEM(pieces, BF),
            pltpu.VMEM(pieces, F32),
            pltpu.VMEM(pieces, BF),
            pltpu.VMEM(pieces, BF),
            sem((2,)),
            sem((2, steps, part.streams)),
        ]

    @staticmethod
    def spread_scratch(part):
        return [pltpu.SemaphoreType.DMA((2, max(1, len(part.bits)), part.streams))]

    def high(self, which):
        return lax.rem(lax.div(self.seq, self.part.bits[which]), 2)

    def partner(self, which):
        bit = self.part.bits[which]
        return {"seq": self.seq + bit - 2 * bit * self.high(which)}

    def partners(self):
        return [{"wa": 1 - self.me}] + [self.partner(k) for k in range(self.steps)]

    def range_at(self, s, k):
        start, size, land = s * self.part.per, self.part.per, s * self.part.per
        for i in range(k):
            size //= 2
            start = start + self.high(self.orders[s][i]) * size
            if i < k - 1:
                land += size
        return start, size, land

    def core_copy(self):
        return send_copy(
            self.given.at[1 - self.me], self.got, self.core.at[0], self.core.at[1], {"wa": 1 - self.me}
        )

    def down_copy(self, s, k):
        start, size, _ = self.range_at(s, k)
        _, half, land = self.range_at(s, k + 1)
        which = self.orders[s][k]
        give = start + (1 - self.high(which)) * half
        return send_copy(
            self.leave.at[pl.ds(give, half)],
            self.landed.at[pl.ds(land, half)],
            self.down.at[0, k, s],
            self.down.at[1, k, s],
            self.partner(which),
        )

    def up_copy(self, s, k):
        start, size, _ = self.range_at(s, k + 1)
        ref = self.out.at[pl.ds(start, size)]
        return send_copy(ref, ref, self.up.at[0, k, s], self.up.at[1, k, s], self.partner(self.orders[s][k]))

    def add(self, s, k):
        start, size, land = self.range_at(s, k)
        last = k == self.steps

        def summed(at, count):
            if k == 0:
                own = self.given[self.me, pl.ds(start + at, count)].astype(F32)
                return own + self.got[pl.ds(start + at, count)].astype(F32)
            return self.total[pl.ds(start + at, count)] + self.landed[pl.ds(land + at, count)].astype(F32)

        if last:

            def finish(at, count):
                self.out[pl.ds(start + at, count)] = summed(at, count).astype(BF)

            in_chunks(size, finish)
            return
        half = size // 2
        high = self.high(self.orders[s][k])
        give, keep = (1 - high) * half, high * half

        def to_leave(at, count):
            self.leave[pl.ds(start + give + at, count)] = summed(give + at, count).astype(BF)

        def to_keep(at, count):
            self.total[pl.ds(start + keep + at, count)] = summed(keep + at, count)

        in_chunks(half, to_leave)
        self.down_copy(s, k).start()
        in_chunks(half, to_keep)

    def reduce_stage(self, at):
        if at == 0:
            self.core_copy().start()
            return
        if at == 1:
            self.core_copy().wait()
        for s in range(self.part.streams):
            if at > 1:
                self.down_copy(s, at - 2).wait()
            self.add(s, at - 1)

    def spread_stage(self, at):
        for s in range(self.part.streams):
            if at > 0:
                self.up_copy(s, self.steps - at).wait()
            if at < self.steps:
                self.up_copy(s, self.steps - at - 1).start()

    def take_share(self, source):
        for s in range(self.part.streams):
            start, size, _ = self.range_at(s, self.steps)
            in_chunks(size, lambda at, count, start=start: copy_pieces(self.out, source, start + at, count))


def sum_kernel(plan, late_given, early_share, early_out, late_out, *traffic):
    late = Summing(plan.late, late_given, late_out, traffic[:7])
    early = Summing(plan.early, None, early_out, (None,) * 6 + traffic[7:])
    steps = late.steps
    greet(late.partners())
    late.reduce_stage(0)
    early.take_share(early_share)
    early.spread_stage(0)
    late.reduce_stage(1)
    for at in range(steps):
        early.spread_stage(at + 1)
        late.reduce_stage(at + 2)
    for at in range(steps + 1):
        late.spread_stage(at)


def finish_kernel(plan, grad_low, early, late, grad, *outs):
    d, inner = plan.d, plan.inner
    half = inner // 2
    grad[...] = grad_low[...].astype(F32)

    @pl.when(pl.program_id(0) == 0)
    def _():
        me = lax.axis_index("wa")

        def matrix(name):
            part, ref = (plan.early, early) if name in plan.early.starts else (plan.late, late)
            first, used = part.starts[name]
            parts = []
            for b in range(first, first + blocks_of(used)):
                value = ref[b * ROWS_OF : (b + 1) * ROWS_OF].reshape(ROWS_OF * 16, LANES)
                parts.append(value.astype(F32))
            return jnp.concatenate(parts, axis=1)

        def my_half(line, size):
            return jnp.where(me == 0, line[:, 0:size], line[:, size : 2 * size])

        turned = matrix("vec")[0:half].T

        def write(ref, pieces):
            ref[...] = jnp.concatenate(pieces, axis=1).reshape(ref.shape)

        for side, taps in enumerate((ENCODER_TAPS, DECODER_TAPS)):
            tag = "ed"[side]
            first_g, first_b, red_w, red_b, mid_g, mid_b, ker, ker_b, last_g, last_b, exp_w, exp_b = outs[
                12 * side : 12 * side + 12
            ]
            at = 8 * side
            write(first_g, [turned[at : at + 1], turned[at + 1 : at + 2]])
            write(first_b, [turned[at + 2 : at + 3], turned[at + 3 : at + 4]])
            write(mid_g, [turned[at + 4 : at + 5]])
            write(mid_b, [turned[at + 5 : at + 6]])
            write(last_g, [turned[at + 6 : at + 7]])
            write(last_b, [turned[at + 7 : at + 8]])
            value = matrix(tag + "_we")
            exp_w[...] = value[0:half, 0:d]
            write(exp_b, [my_half(value[half : half + 1, 0:d], d // 2)])
            value = matrix(tag + "_k")
            for j in range(taps):
                ker[j] = value[0:half, j * inner : (j + 1) * inner]
            centre = (ENCODER_SHIFTS if side == 0 else DECODER_SHIFTS).index(0)
            write(ker_b, [my_half(value[half : half + 1, centre * inner : (centre + 1) * inner], half)])
            value = matrix(tag + "_wr")[0:half]
            red_w[...] = value[:, 0:d]
            write(red_b, [value[:, d:].T[0:1]])


def local(n, stream, doc_start, doc_end, cotangent, *weights):
    rows, d = stream.shape[1], stream.shape[2]
    inner = weights[6].shape[1] * 2
    steps = rows // TILE
    x, cot = stream[0].T, cotangent[0].T
    starts, ends = doc_start, doc_end
    weights = [w.T if at % 12 == 2 else w for at, w in enumerate(weights)]
    enc, dec = gather_weights(weights, d, inner)
    wrt_e, kt_e, wet_e, we_e, kb_e, wr_e, g1_e, f1_e, b1_e, g2_e, f2_e, b2_e, g3_e, f3_e, b3_e = enc
    wrt_d, kt_d, wet_d, we_d, kb_d, wr_d, g1_d, f1_d, b1_d, g2_d, f2_d, b2_d, g3_d, f3_d, b3_d = dec

    plan = Plan(d, inner, steps, n)
    blocks = rows // LANES
    per = TILE // LANES

    def spec(a):
        return whole(a.shape)

    def wide(channels, dtype=BF):
        return jax.ShapeDtypeStruct((channels, rows), dtype)

    def fixed(shape, dtype=F32):
        return jax.ShapeDtypeStruct(shape, dtype)

    class Order:
        def __init__(self, first):
            self.tile = lambda i: (i + first) % steps

        def cols(self, channels):
            return pl.BlockSpec((channels, TILE), lambda i: (0, self.tile(i)))

        def before(self, channels):
            return pl.BlockSpec((channels, LANES), lambda i: (0, (per * self.tile(i) + blocks - 1) % blocks))

        def after(self, channels):
            return pl.BlockSpec((channels, LANES), lambda i: (0, (per * self.tile(i) + per) % blocks))

    def head(channels):
        return pl.BlockSpec((channels, LANES), lambda i: (0, 0))

    def tail(channels):
        return pl.BlockSpec((channels, LANES), lambda i: (0, blocks - 1))

    plain, later = Order(0), Order(1)
    d1, i1 = d + AUG, inner + AUG
    norm_wide = [(d1, BF), (d, BF), (d, BF), (8, F32)]
    norm_in = [(i1, BF), (inner, BF), (inner, BF), (8, F32)]
    sem = pltpu.SemaphoreType.DMA
    vmem = pltpu.VMEM

    def outs_of(order, items):
        return [wide(c, t) for c, t in items], [order.cols(c) for c, _ in items]

    shapes, specs = outs_of(plain, norm_wide + norm_in)
    ins = [wrt_e, f1_e, b1_e, f2_e, b2_e]
    h1e, z1e, d1e, r1e, h2e, z2e, d2e, r2e = pl.pallas_call(
        enc_in_kernel,
        grid=(steps,),
        out_shape=shapes,
        in_specs=[plain.cols(d)] + [spec(a) for a in ins],
        out_specs=specs,
        scratch_shapes=[vmem((d, TILE), F32), vmem((inner, TILE), F32)],
        compiler_params=params(),
        name="encoder_in",
    )(x, *ins)

    shapes, specs = outs_of(later, norm_in + [(d, BF)] + norm_wide + norm_in)
    ins = [kt_e, wet_e, wrt_d, f3_e, b3_e, f1_d, b1_d, f2_d, b2_d]
    h3e, z3e, d3e, r3e, x1, h1d, z1d, d1d, r1d, h2d, z2d, d2d, r2d, edge_d = pl.pallas_call(
        functools.partial(enc_out_kernel, steps),
        grid=(steps,),
        out_shape=shapes + [fixed((i1, LANES), BF)],
        in_specs=[later.cols(1), later.cols(1), later.before(i1), later.cols(i1), later.after(i1)]
        + [head(i1), tail(i1), later.cols(d)]
        + [spec(a) for a in ins],
        out_specs=specs + [whole((i1, LANES))],
        scratch_shapes=[
            vmem((ENCODER_TAPS * inner + AUG, TILE), BF),
            vmem((inner, LANES), BF),
            vmem((inner, LANES), BF),
            vmem((inner, TILE), F32),
            vmem((d, TILE), F32),
            vmem((inner, TILE), F32),
        ]
        + [vmem((i1, LANES), BF)] * 4
        + [sem((3,)), sem((3,))],
        compiler_params=params(1),
        name="encoder_out",
    )(starts, ends, h2e, h2e, h2e, h2e, h2e, x, *ins)

    small, large = fixed((inner, LANES)), fixed((d, LANES))
    sums = [fixed((i1, d)), small, small]
    ins = [kt_d, we_d, wet_d, f3_d, b3_d, g3_d]
    out, evr_d, dwe_d, dg3_d, db3_d = pl.pallas_call(
        functools.partial(dec_out_kernel, steps),
        grid=(steps,),
        out_shape=[wide(d, F32), wide(inner)] + sums,
        in_specs=[plain.cols(1), plain.cols(1), plain.before(i1), plain.cols(i1), spec(edge_d)]
        + [plain.cols(d), plain.cols(d)]
        + [spec(a) for a in ins],
        out_specs=[plain.cols(d), plain.cols(inner)] + [whole(s.shape) for s in sums],
        scratch_shapes=[
            vmem((DECODER_TAPS * inner + AUG, TILE), BF),
            vmem((inner, LANES), BF),
            vmem((inner, TILE), F32),
            vmem((i1, TILE), BF),
            vmem((inner, TILE), BF),
            vmem((inner, TILE), BF),
            vmem((8, TILE), F32),
            vmem((inner, TILE), F32),
            vmem((inner, TILE), BF),
        ],
        compiler_params=params(),
        name="decoder_out",
    )(starts, ends, h2d, h2d, edge_d, cot, x1, *ins)

    shapes, specs = outs_of(plain, [(d, BF), (inner, BF)])
    early = fixed((2, plan.early.pieces, 16, LANES), BF)
    sums = [small, small, large, large, small, small]
    ins = [kb_d, wr_d, we_e, g2_d, g1_d, g3_e]
    stash = [h2d, z2d, d2d, r2d, h1d, z1d, d1d, r1d, cot, h3e, z3e, d3e, r3e]
    ey, evr_e, packed, dg2_d, db2_d, dg1_d, db1_d, dg3_e, db3_e = pl.pallas_call(
        functools.partial(dec_back_kernel, plan),
        grid=(steps,),
        out_shape=shapes + [early] + sums,
        in_specs=[plain.cols(1), plain.cols(1), plain.cols(inner), plain.after(inner), head(inner)]
        + [spec(a) for a in ins]
        + [plain.cols(a.shape[0]) for a in stash]
        + [spec(dwe_d)],
        out_specs=specs + [whole(early.shape)] + [whole(s.shape) for s in sums],
        scratch_shapes=[
            vmem((i1, DECODER_TAPS * inner), F32),
            vmem((inner, d1), F32),
            vmem((i1, d), F32),
            vmem((DECODER_TAPS * inner, TILE), BF),
            vmem((inner, LANES), BF),
            vmem((inner, TILE), F32),
            vmem((d, TILE), F32),
            vmem((inner, TILE), BF),
            vmem((d, TILE), BF),
            vmem((inner, LANES), BF),
            sem((1,)),
            sem((1,)),
        ],
        compiler_params=params(2),
        name="decoder_back",
    )(starts, ends, evr_d, evr_d, evr_d, *ins, *stash, dwe_d)

    late = fixed((2, plan.late.pieces, 16, LANES), BF)
    early_sum = fixed((plan.early.pieces, 16, LANES), BF)
    ins = [kb_e, wr_e, g2_e, g1_e]
    stash = [h2e, z2e, d2e, r2e, h1e, z1e, d1e, r1e, ey]
    vecs = [dg3_e, db3_e, dg1_d, db1_d, dg2_d, db2_d, dg3_d, db3_d]
    grad_low, packed_late, summed = pl.pallas_call(
        functools.partial(enc_back_kernel, plan),
        grid=(steps,),
        out_shape=[wide(d), late, early_sum],
        in_specs=[later.cols(1), later.cols(1), later.before(inner), later.cols(inner), later.after(inner)]
        + [head(inner), tail(inner)]
        + [spec(a) for a in ins]
        + [later.cols(a.shape[0]) for a in stash]
        + [whole(early.shape)]
        + [spec(a) for a in vecs],
        out_specs=[later.cols(d), whole(late.shape), whole(early_sum.shape)],
        scratch_shapes=[
            vmem((i1, ENCODER_TAPS * inner), F32),
            vmem((inner, d1), F32),
            vmem((inner, LANES), F32),
            vmem((inner, LANES), F32),
            vmem((d, LANES), F32),
            vmem((d, LANES), F32),
            vmem((ENCODER_TAPS * inner, TILE), BF),
            vmem((inner, LANES), BF),
            vmem((inner, LANES), BF),
            vmem((inner, TILE), F32),
            vmem((d, TILE), F32),
            vmem((inner, TILE), BF),
            vmem((d, TILE), BF),
            vmem((inner, LANES), BF),
            vmem((inner, LANES), BF),
            sem((2,)),
            sem((2,)),
        ]
        + Summing.scratch(plan.early),
        compiler_params=params(3),
        name="encoder_back",
    )(starts, ends, evr_e, evr_e, evr_e, evr_e, evr_e, *ins, *stash, packed, *vecs)

    vm = pl.BlockSpec(memory_space=pltpu.VMEM)
    early_whole, late_whole = pl.pallas_call(
        functools.partial(sum_kernel, plan),
        out_shape=[early_sum, fixed((plan.late.pieces, 16, LANES), BF)],
        in_specs=[vm, vm],
        out_specs=[vm, vm],
        scratch_shapes=Summing.scratch(plan.late)
        + Summing.spread_scratch(plan.late)
        + Summing.spread_scratch(plan.early),
        compiler_params=params(4),
        name="sum_gradients",
    )(packed_late, summed)

    grad, *shares = pl.pallas_call(
        functools.partial(finish_kernel, plan),
        grid=(steps,),
        out_shape=[wide(d, F32)] + [fixed(w.shape) for w in weights],
        in_specs=[plain.cols(d), whole(early_whole.shape), whole(late_whole.shape)],
        out_specs=[plain.cols(d)] + [whole(w.shape) for w in weights],
        compiler_params=params(),
        name="finish",
    )(grad_low, early_whole, late_whole)
    shares = [w.T if at % 12 == 2 else w for at, w in enumerate(shares)]
    return (out.T[None], grad.T[None], *shares)


def solution(mesh):
    rows = P("wa", "seq", None)
    block = (
        P("wa"), P("wa"), P(None, "wa"), P("wa"), P("wa"), P("wa"),
        P(None, "wa", None), P("wa"), P("wa"), P("wa"), P("wa", None), P("wa"),
    )
    return jax.shard_map(
        functools.partial(local, mesh.shape["seq"]),
        mesh=mesh,
        in_specs=(rows, P("wa", "seq"), P("wa", "seq"), rows, *block, *block),
        out_specs=(rows, rows, *block, *block),
        check_vma=False,
    )
```

time: 271 us -> 243 us (0.90)
  Pallas kernels: 270 us -> 241 us
    pallas_call x5, Pallas kernels: 189 us -> 160 us  [the longest x1 54.6 us: local(): pl.pallas_call(functools.partial(sum_kernel, plan), out_shape=[early_sum,...]
where the time goes in v2:
time: 243 us; the launch traced here: 242 us
  Pallas kernels  241 us (99%)
    pallas_call x1, Pallas kernels, local(): pl.pallas_call(functools.partial(sum_kernel, plan), out_shape=[early_sum,...  54.6 us
    pallas_call x1, Pallas kernels, local(): pl.pallas_call(functools.partial(enc_back_kernel, plan), grid=(steps,), o...  43.1 us
    pallas_call x1, Pallas kernels, local(): pl.pallas_call(functools.partial(enc_out_kernel, steps), grid=(steps,), o...  40.9 us
    pallas_call x1, Pallas kernels, local(): pl.pallas_call(functools.partial(dec_back_kernel, plan), grid=(steps,), o...  35.5 us
    pallas_call x1, Pallas kernels, local(): pl.pallas_call(functools.partial(dec_out_kernel, steps), grid=(steps,), o...  22.9 us
    pallas_call x1, Pallas kernels, gather_weights(): pl.pallas_call(functools.partial(weights_kernel, (d, inner, taps)), out_s...  17.7 us
    pallas_call x1, Pallas kernels, local(): pl.pallas_call(enc_in_kernel, grid=(steps,), out_shape=shapes, in_specs=[...  15.8 us
    pallas_call x1, Pallas kernels, local(): pl.pallas_call(functools.partial(finish_kernel, plan), grid=(steps,), out...  10.9 us

profile of v2, /device:TPU:0, one launch (start us, length us, event | category | flops | bytes accessed | tf_op | source)
XLA Modules:
  0.0 242.3 jit_solution(5990064854192374139)
XLA Ops:
  0.7 17.7 %gather_weights.1 = (bf16[400,816]{1,0:T(8,128)(2,1)}, bf16[400,2016]{1,0:T(8,128)(2,1)}, bf16[800,416]{1,0:T(8,128)(2,1)}, bf16[400,800]{1,0:T(8,128)(2,1)}, bf...) custom-call(bf16[400]{0:T(512)(128)(2,1)} %refs_0_.1, ...), custom_call_target="tpu_custom_call" | custom-call | tf_op jit(solution)/shard_map/gather_weights/pallas_call | solution.py:177
  18.4 15.8 %encoder_in.1 = (bf16[816,3072]{1,0:T(8,128)(2,1)}, bf16[800,3072]{1,0:T(8,128)(2,1)}, bf16[800,3072]{1,0:T(8,128)(2,1)}, f32[8,3072]{1,0:T(8,128)}, bf16[416,30...) custom-call(bf16[800,3072]{1,0:T(8,128)(2,1)} %bitcast.16, ...), custom_call_target="tpu_custom_call" | custom-call | tf_op jit(solution)/shard_map/encoder_in/pallas_call | solution.py:980
  34.2 40.9 %encoder_out.1 = (bf16[416,3072]{1,0:T(8,128)(2,1)}, bf16[400,3072]{1,0:T(8,128)(2,1)}, bf16[400,3072]{1,0:T(8,128)(2,1)}, f32[8,3072]{1,0:T(8,128)}, bf16[800,3...) custom-call(s32[1,3072]{1,0:T(1,128)} %starts.7, ...), custom_call_target="tpu_custom_call" | custom-call | tf_op jit(solution)/shard_map/encoder_out/pallas_call | solution.py:993
  75.1 22.9 %decoder_out.1 = (f32[800,3072]{1,0:T(8,128)}, bf16[400,3072]{1,0:T(8,128)(2,1)}, f32[416,800]{1,0:T(8,128)}, f32[400,128]{1,0:T(8,128)}, f32[400,128]{1,0:T(8,128)}) custom-call(s32[1,3072]{1,0:T(1,128)} %starts.7, s32[1,3072]{1,0:T(1,128)} %ends.7, bf16[416,3072]{1,0:T(8,128)(2,1)} %get-tuple-element.137.before.main.h2, ...), custom_call_target="tpu_custom_call" | custom-call | tf_op jit(solution)/shard_map/decoder_out/pallas_call | solution.py:1018
  98.0 35.5 %decoder_back.1 = (bf16[800,3072]{1,0:T(8,128)(2,1)}, bf16[400,3072]{1,0:T(8,128)(2,1)}, bf16[2,416,16,128]{3,2,1,0:T(8,128)(2,1)}, f32[400,128]{1,0:T(8,128)}, ...) custom-call(s32[1,3072]{1,0:T(1,128)} %starts.7, ...), custom_call_target="tpu_custom_call" | custom-call | tf_op jit(solution)/shard_map/decoder_back/pallas_call | solution.py:1046
  133.5 43.1 %encoder_back.1 = (bf16[800,3072]{1,0:T(8,128)(2,1)}, bf16[2,320,16,128]{3,2,1,0:T(8,128)(2,1)}, bf16[416,16,128]{2,1,0:T(8,128)(2,1)}) custom-call(s32[1,3072]{1,0:T(1,128)} %starts.7, s32[1,3072]{1,0:T(1,128)} %ends.7, bf16[400,3072]{1,0:T(8,128)(2,1)} %get-tuple-element.166.before.main.after.head.tail, ...), custom_call_target="tpu_custom_call" | custom-call | tf_op jit(solution)/shard_map/encoder_back/pallas_call | solution.py:1078
  176.6 54.6 %sum_gradients.1 = (bf16[416,16,128]{2,1,0:T(8,128)(2,1)}, bf16[320,16,128]{2,1,0:T(8,128)(2,1)}) custom-call(bf16[2,320,16,128]{3,2,1,0:T(8,128)(2,1)} %get-tuple-element.189.late_given, bf16[416,16,128]{2,1,0:T(8,128)(2,1)} %get-tuple-element.190.early_share), custom_call_target="tpu_custom_call" | custom-call | tf_op jit(solution)/shard_map/sum_gradients/pallas_call | solution.py:1114
  231.2 10.9 %finish.1 = (f32[800,3072]{1,0:T(8,128)}, f32[400]{0:T(512)}, f32[400]{0:T(512)}, f32[200,800]{1,0:T(8,128)}, f32[200]{0:T(256)}, /*index=5*/f32[200]{0:T(256)},...) custom-call(bf16[800,3072]{1,0:T(8,128)(2,1)} %get-tuple-element.188, ...), custom_call_target="tpu_custom_call" | custom-call | tf_op jit(solution)/shard_map/finish/pallas_call | solution.py:1126

commit v3 on v2

--- a/solution.py
+++ b/solution.py
@@ -63,9 +63,10 @@
     d, inner, taps = dims
     n_in = 24
     ins, refs = refs[:n_in], refs[n_in:]
+    results, refs = refs[:30], refs[30:]
     outs, refs = refs[:30], refs[30:]
     (small_own, small_got, k_own0, k_own1, e_own0, e_own1, r_own0, r_own1, *rest) = refs
-    (r_got0, r_got1, k_got0, k_got1, e_got0, e_got1, send, recv) = rest
+    (r_got0, r_got1, k_got0, k_got1, e_got0, e_got1, k_all, send, recv, store) = rest
     me = lax.axis_index("wa")
     other = 1 - me
     barrier = pltpu.get_barrier_semaphore()
@@ -95,7 +96,9 @@
     owns.append(small_own)
     gots = [r_got0, k_got0, e_got0, r_got1, k_got1, e_got1, small_got]
     copies = []
-    for at, (own, got) in enumerate(zip(owns, gots)):
+    pairs = list(zip(owns, gots))
+    for at in (6, 0, 2, 1, 3, 5, 4):
+        own, got = pairs[at]
         copies.append(
             pltpu.make_async_remote_copy(
                 src_ref=own,
@@ -107,15 +110,32 @@
             )
         )
         copies[-1].start()
-    for copy in copies:
-        copy.wait()
+    arrival = dict(zip((6, 0, 2, 1, 3, 5, 4), copies))
+    stores = []
+
+    def keep(at):
+        stores.append(pltpu.make_async_copy(outs[at], results[at], store.at[at]))
+        stores[-1].start()
 
     first_core = me == 0
+    square = (HALF, HALF)
+    unit = lax.broadcasted_iota(jnp.int32, square, 0) == lax.broadcasted_iota(jnp.int32, square, 1)
+    unit = jnp.where(unit, 1.0, 0.0).astype(BF)
+
+    def turn(out, columns, count, width=None):
+        for a in range(0, count, HALF):
+            b = min(a + HALF, count)
+            piece = nt_dot(unit[0 : b - a, 0 : b - a], columns(a, b)).astype(BF)
+            if width is None:
+                out[a:b, :] = piece
+            else:
+                out[a:b, 0:width] = piece
 
     def ordered(own, got):
         own, got = own.astype(F32), got.astype(F32)
         return jnp.where(first_core, own, got), jnp.where(first_core, got, own)
 
+    arrival[6].wait()
     small0, small1 = ordered(small_own[...], small_got[...])
 
     def column(row, n):
@@ -136,22 +156,36 @@
             half_gain[...] = gain[...] * 0.5
             half_bias[...] = column(base + row + 1, n) * 0.5
         n = taps[side]
+        first = 15 * side
+        for at in range(6, 15):
+            keep(first + at)
+        arrival[3 * side].wait()
         r0, r1 = ordered(owns[3 * side][0:half, :], gots[3 * side][0:half, :])
-        r = jnp.concatenate([r0, r1], axis=0)
-        wr[...] = r.T.astype(BF)
-        wrt[:, 0:d] = r.astype(BF)
+        wrt[:, 0:d] = jnp.concatenate([r0, r1], axis=0).astype(BF)
         wrt[:, d : d + AUG] = bias_columns(column(base + 2, inner))
+        keep(first)
+        turn(wr, lambda a, b: wrt[:, a:b], d)
+        keep(first + 5)
+        arrival[3 * side + 2].wait()
         e0, e1 = ordered(owns[3 * side + 2][0:half, :], gots[3 * side + 2][0:half, :])
-        e = jnp.concatenate([e0, e1], axis=0)
-        we[...] = e.astype(BF)
-        wet[:, 0:inner] = e.T.astype(BF)
+        we[...] = jnp.concatenate([e0, e1], axis=0).astype(BF)
+        keep(first + 3)
+        turn(wet, lambda a, b: we[:, a:b], d, inner)
         wet[:, inner : inner + AUG] = bias_columns(column(base + 8, d))
+        keep(first + 2)
+        arrival[3 * side + 1].wait()
         for j in range(n):
             k0, k1 = ordered(owns[3 * side + 1][j, 0:half, :], gots[3 * side + 1][j, 0:half, :])
-            k = jnp.concatenate([k0, k1], axis=0)
-            kb[:, j * inner : (j + 1) * inner] = k.astype(BF)
-            kt[:, j * inner : (j + 1) * inner] = k.T.astype(BF)
+            k = jnp.concatenate([k0, k1], axis=0).astype(BF)
+            for channels, place in tap_pieces(j, n, inner):
+                kb[:, place] = k[:, channels]
+                k_all[place, :] = k[channels, :]
+        keep(first + 4)
+        turn(kt, lambda a, b: k_all[0 : n * inner, a:b], inner, n * inner)
         kt[:, n * inner : n * inner + AUG] = bias_columns(column(base + 5, inner))
+        keep(first + 1)
+    for copy in stores:
+        copy.wait()
 
 
 def gather_weights(args, d, inner):
@@ -178,9 +212,11 @@
         functools.partial(weights_kernel, (d, inner, taps)),
         out_shape=[jax.ShapeDtypeStruct(*s) for s in shapes],
         in_specs=[vm] * 24,
-        out_specs=[vm] * 30,
-        scratch_shapes=[small, small, *kk, *ee, *ee, *ee, *kk, *ee]
-        + [pltpu.SemaphoreType.DMA((7,)), pltpu.SemaphoreType.DMA((7,))],
+        out_specs=[pl.BlockSpec(memory_space=pl.ANY)] * 30,
+        scratch_shapes=[pltpu.VMEM(*shape) for shape in shapes]
+        + [small, small, *kk, *ee, *ee, *ee, *kk, *ee]
+        + [pltpu.VMEM((taps[0] * inner, inner), BF)]
+        + [pltpu.SemaphoreType.DMA((7,)), pltpu.SemaphoreType.DMA((7,)), pltpu.SemaphoreType.DMA((30,))],
         compiler_params=params(0),
         name="gather_weights",
     )(*args)
@@ -208,29 +244,29 @@
     return [functools.partial(piece, at, min(at + HALF, columns)) for at in range(0, columns, HALF)]
 
 
-def norm_forward(src, lanes, channels, gain, bias, h_out, z_out, d_out, r_out, keep=None, fill=()):
+def norm_forward(src, lanes, channels, gain, bias, h_out, z_out, d_out, r_out, keep=None, fill=(), at=None, h_copy=None):
     width = lanes.stop - lanes.start
     between = pacing(fill, 3 * (channels // 16))
     total = [jnp.zeros((8, width), F32) for _ in range(4)]
     for c in range(0, channels, 16):
         between()
-        x = src[c : c + 16, lanes].astype(F32)
+        x = src[c : c + 16, at or lanes].astype(F32)
         if keep is not None:
-            keep[c : c + 16, lanes] = x
-        at = (c // 8) % 4
-        total[at] = total[at] + x[0:8]
-        total[at + 1] = total[at + 1] + x[8:16]
+            keep[c : c + 16, at or lanes] = x
+        k = (c // 8) % 4
+        total[k] = total[k] + x[0:8]
+        total[k + 1] = total[k + 1] + x[8:16]
     mean = jnp.sum((total[0] + total[1]) + (total[2] + total[3]), axis=0, keepdims=True) * (1.0 / channels)
     wide = jnp.broadcast_to(mean, (16, width))
     values = src if keep is None else keep
     total = [jnp.zeros((8, width), F32) for _ in range(4)]
     for c in range(0, channels, 16):
         between()
-        centre = values[c : c + 16, lanes] - wide
+        centre = values[c : c + 16, at or lanes] - wide
         square = centre * centre
-        at = (c // 8) % 4
-        total[at] = total[at] + square[0:8]
-        total[at + 1] = total[at + 1] + square[8:16]
+        k = (c // 8) % 4
+        total[k] = total[k] + square[0:8]
+        total[k + 1] = total[k + 1] + square[8:16]
     spread = jnp.sum((total[0] + total[1]) + (total[2] + total[3]), axis=0, keepdims=True) * (1.0 / channels)
     r = lax.rsqrt(spread + EPS)
     if r_out is not None:
@@ -241,17 +277,19 @@
     for c in range(0, channels, 16):
         between()
         rows = slice(c, c + 16)
-        z = values[rows, lanes] * rw - mw
+        z = values[rows, at or lanes] * rw - mw
         half = (z * lanes_of(gain[rows, :], width) + lanes_of(bias[rows, :], width)).astype(BF)
         sq = half * half
         t = jnp.tanh(half * (sq * BF(GELU_3) + BF(GELU_1)))
         up = one + t
         h_out[rows, lanes] = half * up
+        if h_copy is not None:
+            h_copy[rows, :] = half * up
         d_out[rows, lanes] = up * (point + half * (sq * BF(1.5 * GELU_3) + BF(0.5 * GELU_1)) * (one - t))
         z_out[rows, lanes] = z.astype(BF)
 
 
-def norm_backward(grad, lanes, channels, gain, z_in, d_in, r_in, gain_sum, bias_sum, keep, emit, fill=()):
+def norm_backward(grad, lanes, channels, gain, z_in, d_in, r_in, gain_sum, bias_sum, keep, emit, fill=(), at=None):
     width = lanes.stop - lanes.start
     between = pacing(fill, 2 * (channels // 16))
     one = [jnp.zeros((8, width), F32) for _ in range(2)]
@@ -261,24 +299,24 @@
     for c in range(0, channels, 16):
         between()
         rows = slice(c, c + 16)
-        da = grad[rows, lanes] * d_in[rows, lanes].astype(F32)
+        da = grad[rows, at or lanes] * d_in[rows, lanes].astype(F32)
         p = da * z_in[rows, lanes].astype(F32)
         bias_sum[rows, :] += fold(da)
         gain_sum[rows, :] += fold(p)
         wide = lanes_of(gain[rows, :], width)
         dz = da * wide
         q = p * wide
-        keep[rows, lanes] = (dz * rw).astype(BF)
-        for at in range(2):
-            one[at] = one[at] + dz[8 * at : 8 * at + 8]
-            two[at] = two[at] + q[8 * at : 8 * at + 8]
+        keep[rows, at or lanes] = (dz * rw).astype(BF)
+        for k in range(2):
+            one[k] = one[k] + dz[8 * k : 8 * k + 8]
+            two[k] = two[k] + q[8 * k : 8 * k + 8]
     scale = r * (1.0 / channels)
     m1 = jnp.broadcast_to(jnp.sum(one[0] + one[1], axis=0, keepdims=True) * scale, (16, width)).astype(BF)
     m2 = jnp.broadcast_to(jnp.sum(two[0] + two[1], axis=0, keepdims=True) * scale, (16, width)).astype(BF)
     for c in range(0, channels, 16):
         between()
         rows = slice(c, c + 16)
-        emit(rows, keep[rows, lanes] - (z_in[rows, lanes] * m2 + m1))
+        emit(rows, keep[rows, at or lanes] - (z_in[rows, lanes] * m2 + m1))
 
 
 def tap_mask(starts, ends, first, shift):
@@ -288,10 +326,23 @@
     return jnp.concatenate([one, one], axis=0).astype(BF)
 
 
+def tap_row(j, c, taps, inner):
+    aligned = inner // LANES * LANES
+    return j * aligned + c if c < aligned else taps * aligned + j * (inner - aligned) + c - aligned
+
+
+def tap_pieces(j, taps, inner):
+    aligned = inner // LANES * LANES
+    for a, b in ((0, aligned), (aligned, inner)):
+        at = tap_row(j, a, taps, inner)
+        yield slice(a, b), slice(at, at + b - a)
+
+
 def stack_taps(stack, shifts, before, main, after, starts, ends, first, inner):
     for j, shift in enumerate(shifts):
         if not shift:
-            stack[j * inner : (j + 1) * inner, :] = main[0:inner, :]
+            for channels, place in tap_pieces(j, len(shifts), inner):
+                stack[place, :] = main[channels, :]
             continue
         mask = tap_mask(starts, ends, first, shift)
         for c in range(0, inner, 16):
@@ -302,7 +353,8 @@
             else:
                 span = jnp.concatenate([main[rows, :], after[rows, :]], axis=1)
                 span = pltpu.roll(span, TILE + LANES - shift, 1)[:, :TILE]
-            stack[j * inner + c : j * inner + c + 16, :] = span * mask
+            at = tap_row(j, c, len(shifts), inner)
+            stack[at : at + 16, :] = span * mask
 
 
 def ones_rows(width):
@@ -338,21 +390,20 @@
 
 
 CHAINS = (slice(0, HALF), slice(HALF, TILE))
-
-
-def enc_in_kernel(x, wrt, g1, b1, g2, b2, h1, z1, d1, r1, h2, z2, d2, r2, xt, u):
+EVERY = slice(0, HALF)
+
+
+def enc_in_kernel(x, wrt, g1, b1, g2, b2, h1, z1, d1, r1, h2, z2, d2, r2, xt, u0, u1, h_wide0, h_wide1):
     d, inner = x.shape[0], wrt.shape[0]
     h1[d : d + AUG, :] = ones_rows(TILE)
     h2[inner : inner + AUG, :] = ones_rows(TILE)
-    one, two = CHAINS
-
-    def make_u(lanes):
-        u[:, lanes] = nn_dot(wrt[...], h1[:, lanes])
-
-    norm_forward(x, one, d, g1, b1, h1, z1, d1, r1, xt)
-    norm_forward(x, two, d, g1, b1, h1, z1, d1, r1, xt, [lambda: make_u(one)])
-    norm_forward(u, one, inner, g2, b2, h2, z2, d2, r2, None, [lambda: make_u(two)])
-    norm_forward(u, two, inner, g2, b2, h2, z2, d2, r2)
+    u, h_wide = (u0, u1), (h_wide0, h_wide1)
+    for k in range(2):
+        h_wide[k][d : d + AUG, :] = ones_rows(HALF)
+        norm_forward(x, CHAINS[k], d, g1, b1, h1, z1, d1, r1, xt, h_copy=h_wide[k])
+        u[k][...] = nn_dot(wrt[...], h_wide[k][...])
+    for k in range(2):
+        norm_forward(u[k], CHAINS[k], inner, g2, b2, h2, z2, d2, r2, at=EVERY)
 
 
 def choose_edge(window, block, edge, at_end):
@@ -383,10 +434,11 @@
 def enc_out_kernel(
     steps, starts, ends, before, main, after, head, tail, xt, kt, wet, wrt, g3, b3, g1, b1, g2, b2,
     h3, z3, d3, r3, x1, h1, z1, d1, r1, h2, z2, d2, r2, edge_o,
-    stack, win_b, win_a, v, y, u, got_l, got_r, own, got, send, recv,
+    stack, win_b, win_a, v0, v1, y0, y1, u0, u1, h_in0, h_in1, h_wide0, h_wide1, got_l, got_r, own, got, send, recv,
 ):
     step = pl.program_id(0)
-    d, inner = xt.shape[0], v.shape[0]
+    d, inner = xt.shape[0], v0.shape[0]
+    v, y, u, h_in, h_wide = (v0, v1), (y0, y1), (u0, u1), (h_in0, h_in1), (h_wide0, h_wide1)
     trade_edges(step, steps, head, tail, got_l, got_r, send, recv)
     choose_edge(win_b, before, got_l, step == steps - 1)
     choose_edge(win_a, after, got_r, step == steps - 2)
@@ -397,30 +449,41 @@
     h2[inner : inner + AUG, :] = ones_rows(TILE)
     one, two = CHAINS
 
-    def make_v(lanes):
-        v[:, lanes] = nn_dot(kt[...], stack[:, lanes])
-
-    def make_y(lanes):
-        y[:, lanes] = nn_dot(wet[...], h3[:, lanes]) + xt[:, lanes].astype(F32)
-
-    def make_u(lanes):
-        u[:, lanes] = nn_dot(wrt[...], h1[:, lanes])
-
-    def norm_last(lanes, fill):
-        norm_forward(v, lanes, inner, g3, b3, h3, z3, d3, r3, None, fill)
-
-    def norm_first(lanes, fill):
+    def make_v(k):
+        v[k][...] = nn_dot(kt[...], stack[:, CHAINS[k]])
+
+    def make_y(k):
+        y[k][...] = nn_dot(wet[...], h_in[k][...]) + xt[:, CHAINS[k]].astype(F32)
+
+    def make_u(k):
+        u[k][...] = nn_dot(wrt[...], h_wide[k][...])
+
+    def norm_last(k):
+        norm_forward(v[k], CHAINS[k], inner, g3, b3, h3, z3, d3, r3, at=EVERY, h_copy=h_in[k])
+
+    def norm_first(k):
         for c in range(0, d, 16):
-            x1[c : c + 16, lanes] = y[c : c + 16, lanes].astype(BF)
-        norm_forward(y, lanes, d, g1, b1, h1, z1, d1, r1, None, fill)
-
-    make_v(one)
-    norm_last(one, [lambda: make_v(two)])
-    norm_last(two, [lambda: make_y(one)])
-    norm_first(one, [lambda: make_y(two)])
-    norm_first(two, [lambda: make_u(one)])
-    norm_forward(u, one, inner, g2, b2, h2, z2, d2, r2, None, [lambda: make_u(two)])
-    norm_forward(u, two, inner, g2, b2, h2, z2, d2, r2)
+            x1[c : c + 16, CHAINS[k]] = y[k][c : c + 16, :].astype(BF)
+        norm_forward(y[k], CHAINS[k], d, g1, b1, h1, z1, d1, r1, at=EVERY, h_copy=h_wide[k])
+
+    def norm_mid(k):
+        norm_forward(u[k], CHAINS[k], inner, g2, b2, h2, z2, d2, r2, at=EVERY)
+
+    for k in range(2):
+        h_in[k][inner : inner + AUG, :] = ones_rows(HALF)
+        h_wide[k][d : d + AUG, :] = ones_rows(HALF)
+    make_v(0)
+    make_v(1)
+    norm_last(0)
+    make_y(0)
+    norm_last(1)
+    make_y(1)
+    norm_first(0)
+    make_u(0)
+    norm_first(1)
+    make_u(1)
+    norm_mid(0)
+    norm_mid(1)
 
     def give():
         return send_copy(own, got, send.at[2], recv.at[2], {"seq": neighbours()[1]})
@@ -437,12 +500,14 @@
 
 
 def dec_out_kernel(
-    steps, starts, ends, before, main, e_l, cot_t, x1, kt, we, wet, f3, b3, g3,
-    out, evr, dwe, dg3, db3,
-    stack, win_b, v, h3, z3, d3, r3, g, kept,
+    plan, starts, ends, before, main, e_l, cot_t, x1, kt, we, wet, f3, b3, g3,
+    out, evr, packed, dg3, db3,
+    dwe, stack, win_b, v0, v1, h3, z3, d3, r3, g0, g1, kept0, kept1, h_in0, h_in1,
 ):
+    steps = plan.steps
     step = pl.program_id(0)
-    inner = v.shape[0]
+    inner = v0.shape[0]
+    v, g, kept, h_in = (v0, v1), (g0, g1), (kept0, kept1), (h_in0, h_in1)
 
     @pl.when(step == 0)
     def _():
@@ -454,42 +519,48 @@
     stack_taps(stack, DECODER_SHIFTS, win_b, main, None, starts, ends, first_place(step, steps), inner)
     stack[len(DECODER_SHIFTS) * inner :, :] = ones_rows(TILE)
     h3[inner : inner + AUG, :] = ones_rows(TILE)
-    one, two = CHAINS
-
-    def make_v(lanes):
-        v[:, lanes] = nn_dot(kt[...], stack[:, lanes])
-
-    def make_g(lanes):
-        g[:, lanes] = nn_dot(we[...], cot_t[:, lanes])
-
-    def back(lanes, fill):
+
+    def make_out(k):
+        out[:, CHAINS[k]] = nn_dot(wet[...], h_in[k][...]) + x1[:, CHAINS[k]].astype(F32)
+
+    def back(k, fill):
         def emit(rows, value):
-            evr[rows, lanes] = value
-
-        norm_backward(g, lanes, inner, g3, z3, d3, r3, dg3, db3, kept, emit, fill)
-
-    def make_out(lanes):
-        out[:, lanes] = nn_dot(wet[...], h3[:, lanes]) + x1[:, lanes].astype(F32)
-
-    make_g(one)
-    make_g(two)
-    make_v(one)
-    norm_forward(v, one, inner, f3, b3, h3, z3, d3, r3, None, [lambda: make_v(two)])
-    norm_forward(v, two, inner, f3, b3, h3, z3, d3, r3)
+            evr[rows, CHAINS[k]] = value
+
+        norm_backward(g[k], CHAINS[k], inner, g3, z3, d3, r3, dg3, db3, kept[k], emit, fill, EVERY)
+
+    for k in range(2):
+        h_in[k][inner : inner + AUG, :] = ones_rows(HALF)
+        g[k][...] = nn_dot(we[...], cot_t[:, CHAINS[k]])
+    for k in range(2):
+        v[k][...] = nn_dot(kt[...], stack[:, CHAINS[k]])
+    for k in range(2):
+        norm_forward(v[k], CHAINS[k], inner, f3, b3, h3, z3, d3, r3, at=EVERY, h_copy=h_in[k])
     products = add_product(dwe, h3, cot_t)
-    back(one, [lambda: make_out(one), *products[:2]])
-    back(two, [lambda: make_out(two), *products[2:]])
+    back(0, [lambda: make_out(0), *products[:2]])
+    back(1, [lambda: make_out(1), *products[2:]])
+
+    @pl.when(step == steps - 1)
+    def _():
+        pack_gradients(packed, plan, ((dwe, dwe.shape[1]),), ())
 
 
 def dec_back_kernel(
     plan, starts, ends, main, after, head, kb, wr, we, g2, g1, g3,
-    h2, z2, d2, r2, h1, z1, d1, r1, cot_t, h3, z3, d3, r3, dwe_d,
-    ey, evr, packed, dg2, db2, dg1, db1, dg3, db3,
-    dk, dwrt, dwe, stack, win_a, g, big, eur, kept, got, send, recv,
+    h2, z2, d2, r2, h1, z1, d1, r1, cot_t, h3, z3, d3, r3, given,
+    ey, evr, packed, first, dg2, db2, dg1, db1, dg3, db3,
+    dk, dwrt, dwe, stack, win_a, ga0, ga1, gb0, gb1, big0, big1, eur, eur0, eur1, ey0, ey1,
+    kept0, kept1, keeps0, keeps1, got, send, recv, *traffic,
 ):
     steps = plan.steps
+    sum_over = Summing(plan.first, given, first, traffic)
+    k = sum_over.steps
+    due = [0, 2] + [5 + 6 * i // max(1, k - 1) for i in range(k)]
+    hook = hooks(steps, [(place, functools.partial(sum_over.reduce_stage, at)) for at, place in enumerate(due)])
     step = pl.program_id(0)
-    d, inner = cot_t.shape[0], g.shape[0]
+    d, inner = cot_t.shape[0], ga0.shape[0]
+    ga, gb, big, eurs, eys = (ga0, ga1), (gb0, gb1), (big0, big1), (eur0, eur1), (ey0, ey1)
+    kept, keeps = (kept0, kept1), (keeps0, keeps1)
 
     @pl.when(step == 0)
     def _():
@@ -501,75 +572,79 @@
 
     @pl.when(step == 0)
     def _():
-        greet([{"seq": left}, {"seq": right}])
+        greet([{"seq": left}, {"seq": right}, *sum_over.partners()])
         to_left.start()
 
     @pl.when(step == steps - 1)
     def _():
         to_left.wait()
 
+    hook(0)
     choose_edge(win_a, after, got, step == steps - 1)
     back = tuple(-s for s in DECODER_SHIFTS)
     stack_taps(stack, back, None, main, win_a, starts, ends, first_place(step, steps), inner)
-    one, two = CHAINS
-
-    def make_g2(lanes):
-        g[:, lanes] = nn_dot(kb[...], stack[:, lanes])
-
-    def make_g1(lanes):
-        big[:, lanes] = nn_dot(wr[...], eur[:, lanes])
-
-    def make_g3(lanes):
-        g[:, lanes] = nn_dot(we[...], ey[:, lanes])
-
-    def back2(lanes, fill):
+
+    def back2(k, fill):
         def emit(rows, value):
-            eur[rows, lanes] = value
-
-        norm_backward(g, lanes, inner, g2, z2, d2, r2, dg2, db2, kept, emit, fill)
-
-    def back1(lanes, fill):
+            eur[rows, CHAINS[k]] = value
+            eurs[k][rows, :] = value
+
+        norm_backward(ga[k], CHAINS[k], inner, g2, z2, d2, r2, dg2, db2, keeps[k], emit, fill, EVERY)
+
+    def back1(k, fill):
         def emit(rows, value):
-            ey[rows, lanes] = value + cot_t[rows, lanes]
-
-        norm_backward(big, lanes, d, g1, z1, d1, r1, dg1, db1, kept, emit, fill)
-
-    def back3(lanes, fill):
+            total = value + cot_t[rows, CHAINS[k]]
+            ey[rows, CHAINS[k]] = total
+            eys[k][rows, :] = total
+
+        norm_backward(big[k], CHAINS[k], d, g1, z1, d1, r1, dg1, db1, kept[k], emit, fill, EVERY)
+
+    def back3(k, fill):
         def emit(rows, value):
-            evr[rows, lanes] = value
-
-        norm_backward(g, lanes, inner, g3, z3, d3, r3, dg3, db3, kept, emit, fill)
-
-    make_g2(one)
+            evr[rows, CHAINS[k]] = value
+
+        norm_backward(gb[k], CHAINS[k], inner, g3, z3, d3, r3, dg3, db3, keeps[k], emit, fill, EVERY)
+
+    for k in range(2):
+        ga[k][...] = nn_dot(kb[...], stack[:, CHAINS[k]])
     by_k = add_product(dk, h2, stack)
-    back2(one, [lambda: make_g2(two)])
-    back2(two, [lambda: make_g1(one)])
+    back2(0, by_k[:2])
+    big[0][...] = nn_dot(wr[...], eur0[...])
+    back2(1, by_k[2:])
+    big[1][...] = nn_dot(wr[...], eur1[...])
+    hook(1)
     by_r = add_product(dwrt, eur, h1)
-    back1(one, [lambda: make_g1(two), *by_k[:3]])
-    back1(two, [lambda: make_g3(one), *by_k[3:], *by_r[:2]])
-    make_g3(two)
+    back1(0, by_r[:2])
+    gb[0][...] = nn_dot(we[...], ey0[...])
+    back1(1, by_r[2:])
+    gb[1][...] = nn_dot(we[...], ey1[...])
     by_e = add_product(dwe, h3, ey)
-    back3(one, [*by_r[2:], *by_e[:1]])
-    back3(two, by_e[1:])
+    back3(0, by_e[:2])
+    back3(1, by_e[2:])
 
     @pl.when(step == steps - 1)
     def _():
-        pack_gradients(packed, plan, ((dwe_d, d), (dk, dk.shape[1]), (dwrt, d + AUG), (dwe, d)), ())
+        pack_gradients(packed, plan, ((dk, dk.shape[1]), (dwrt, d + AUG), (dwe, d)), ())
+
+    hook(2)
 
 
 def enc_back_kernel(
     plan, starts, ends, before, main, after, head, tail, kb, wr, g2, g1,
-    h2, z2, d2, r2, h1, z1, d1, r1, ey, given, *rest,
+    h2, z2, d2, r2, h1, z1, d1, r1, ey, given, first_share, *rest,
 ):
     vecs, rest = rest[:8], rest[8:]
     (
-        grad, packed, summed,
+        grad, packed, summed, first_whole,
         dk, dwrt, dg2, db2, dg1, db1,
-        stack, win_b, win_a, g, big, eur, kept, got_l, got_r, send, recv,
-    ), traffic = rest[:20], rest[20:]
+        stack, win_b, win_a, ga0, ga1, big0, big1, eur, eur0, eur1, kept0, kept1, keeps0, keeps1,
+        got_l, got_r, send, recv, result, first_up,
+    ), traffic = rest[:30], rest[30:]
     steps = plan.steps
     step = pl.program_id(0)
-    d, inner = ey.shape[0], g.shape[0]
+    d, inner = ey.shape[0], ga0.shape[0]
+    ga, big, eurs = (ga0, ga1), (big0, big1), (eur0, eur1)
+    kept, keeps = (kept0, kept1), (keeps0, keeps1)
 
     @pl.when(step == 0)
     def _():
@@ -579,54 +654,53 @@
     sum_over = Summing(plan.early, given, summed, traffic)
     trade_edges(step, steps, head, tail, got_l, got_r, send, recv, sum_over.partners())
 
-    stage_count = sum_over.steps + 2
-    due = [0, 2] + [6 + 6 * i // max(1, stage_count - 3) for i in range(stage_count - 2)]
-
-    def hook(at):
-        for stage, place in enumerate(due):
-            where = (place // 2, place % 2) if place < 2 * steps else (steps - 1, 2)
-            if where[1] == at:
-
-                @pl.when(step == where[0])
-                def _(stage=stage):
-                    sum_over.reduce_stage(stage)
+    k = sum_over.steps
+    due = [0, 2] + [6 + 6 * i // max(1, k - 1) for i in range(k)]
+    actions = [(place, functools.partial(sum_over.reduce_stage, at)) for at, place in enumerate(due)]
+    first = Summing(plan.first, None, result, (None,) * 6 + (first_up,))
+
+    def begin():
+        first.take_share(first_share)
+        first.spread_stage(0)
+
+    actions.append((1, begin))
+    actions += [(3 + 8 * at // k, functools.partial(first.spread_stage, at + 1)) for at in range(k)]
+    hook = hooks(steps, actions)
 
     hook(0)
     choose_edge(win_b, before, got_l, step == steps - 1)
     choose_edge(win_a, after, got_r, step == steps - 2)
     back = tuple(-s for s in ENCODER_SHIFTS)
     stack_taps(stack, back, win_b, main, win_a, starts, ends, first_place(later_tile(step, steps), steps), inner)
-    one, two = CHAINS
-
-    def make_g2(lanes):
-        g[:, lanes] = nn_dot(kb[...], stack[:, lanes])
-
-    def make_g1(lanes):
-        big[:, lanes] = nn_dot(wr[...], eur[:, lanes])
-
-    def back2(lanes, fill):
+
+    def back2(k, fill):
         def emit(rows, value):
-            eur[rows, lanes] = value
-
-        norm_backward(g, lanes, inner, g2, z2, d2, r2, dg2, db2, kept, emit, fill)
-
-    def back1(lanes, fill):
+            eur[rows, CHAINS[k]] = value
+            eurs[k][rows, :] = value
+
+        norm_backward(ga[k], CHAINS[k], inner, g2, z2, d2, r2, dg2, db2, keeps[k], emit, fill, EVERY)
+
+    def back1(k, fill):
         def emit(rows, value):
-            grad[rows, lanes] = value + ey[rows, lanes]
-
-        norm_backward(big, lanes, d, g1, z1, d1, r1, dg1, db1, kept, emit, fill)
-
-    make_g2(one)
+            grad[rows, CHAINS[k]] = value + ey[rows, CHAINS[k]]
+
+        norm_backward(big[k], CHAINS[k], d, g1, z1, d1, r1, dg1, db1, kept[k], emit, fill, EVERY)
+
+    for k in range(2):
+        ga[k][...] = nn_dot(kb[...], stack[:, CHAINS[k]])
     by_k = add_product(dk, h2, stack)
-    back2(one, [lambda: make_g2(two)])
-    back2(two, [lambda: make_g1(one), *by_k[:1]])
+    back2(0, by_k[:2])
+    big[0][...] = nn_dot(wr[...], eur0[...])
+    back2(1, by_k[2:4])
+    big[1][...] = nn_dot(wr[...], eur1[...])
     hook(1)
     by_r = add_product(dwrt, eur, h1)
-    back1(one, [lambda: make_g1(two), *by_k[1:5]])
-    back1(two, [*by_k[5:], *by_r])
+    back1(0, by_k[4:])
+    back1(1, by_r)
 
     @pl.when(step == steps - 1)
     def _():
+        in_chunks(plan.first.pieces, lambda at, count: copy_pieces(first_whole, result, at, count))
         sums = (dg1, db1, dg2, db2, *vecs)
         pack_gradients(packed, plan, ((dk, dk.shape[1]), (dwrt, d + AUG)), sums)
 
@@ -662,7 +736,8 @@
 class Plan:
     def __init__(self, d, inner, steps, n):
         self.d, self.inner, self.steps, self.n = d, inner, steps, n
-        early = (("d_we", d), ("d_k", DECODER_TAPS * inner), ("d_wr", d + AUG), ("e_we", d))
+        self.first = Part((("d_we", d),), False, 2, n)
+        early = (("d_k", DECODER_TAPS * inner), ("d_wr", d + AUG), ("e_we", d))
         self.early = Part(early, False, 2, n)
         self.late = Part((("e_k", ENCODER_TAPS * inner), ("e_wr", d + AUG)), True, 4, n)
 
@@ -725,6 +800,21 @@
     dst[pl.ds(at, count)] = src[pl.ds(at, count)]
 
 
+def hooks(steps, actions):
+    step = pl.program_id(0)
+
+    def hook(at):
+        for place, action in actions:
+            where = (place // 2, place % 2) if place < 2 * steps else (steps - 1, 2)
+            if where[1] == at:
+
+                @pl.when(step == where[0])
+                def _(action=action):
+                    action()
+
+    return hook
+
+
 class Summing:
     def __init__(self, part, given, out, traffic):
         self.part, self.given, self.out = part, given, out
@@ -871,7 +961,7 @@
         late.spread_stage(at)
 
 
-def finish_kernel(plan, grad_low, early, late, grad, *outs):
+def finish_kernel(plan, grad_low, first, early, late, grad, *outs):
     d, inner = plan.d, plan.inner
     half = inner // 2
     grad[...] = grad_low[...].astype(F32)
@@ -881,10 +971,12 @@
         me = lax.axis_index("wa")
 
         def matrix(name):
-            part, ref = (plan.early, early) if name in plan.early.starts else (plan.late, late)
-            first, used = part.starts[name]
+            for part, ref in ((plan.first, first), (plan.early, early), (plan.late, late)):
+                if name in part.starts:
+                    break
+            begin, used = part.starts[name]
             parts = []
-            for b in range(first, first + blocks_of(used)):
+            for b in range(begin, begin + blocks_of(used)):
                 value = ref[b * ROWS_OF : (b + 1) * ROWS_OF].reshape(ROWS_OF * 16, LANES)
                 parts.append(value.astype(F32))
             return jnp.concatenate(parts, axis=1)
@@ -914,9 +1006,10 @@
             write(exp_b, [my_half(value[half : half + 1, 0:d], d // 2)])
             value = matrix(tag + "_k")
             for j in range(taps):
-                ker[j] = value[0:half, j * inner : (j + 1) * inner]
+                ker[j] = jnp.concatenate([value[0:half, place] for _, place in tap_pieces(j, taps, inner)], axis=1)
             centre = (ENCODER_SHIFTS if side == 0 else DECODER_SHIFTS).index(0)
-            write(ker_b, [my_half(value[half : half + 1, centre * inner : (centre + 1) * inner], half)])
+            sums = [value[half : half + 1, place] for _, place in tap_pieces(centre, taps, inner)]
+            write(ker_b, [my_half(jnp.concatenate(sums, axis=1), half)])
             value = matrix(tag + "_wr")[0:half]
             red_w[...] = value[:, 0:d]
             write(red_b, [value[:, d:].T[0:1]])
@@ -983,7 +1076,7 @@
         out_shape=shapes,
         in_specs=[plain.cols(d)] + [spec(a) for a in ins],
         out_specs=specs,
-        scratch_shapes=[vmem((d, TILE), F32), vmem((inner, TILE), F32)],
+        scratch_shapes=[vmem((d, TILE), F32)] + [vmem((inner, HALF), F32)] * 2 + [vmem((d1, HALF), BF)] * 2,
         compiler_params=params(),
         name="encoder_in",
     )(x, *ins)
@@ -1002,10 +1095,12 @@
             vmem((ENCODER_TAPS * inner + AUG, TILE), BF),
             vmem((inner, LANES), BF),
             vmem((inner, LANES), BF),
-            vmem((inner, TILE), F32),
-            vmem((d, TILE), F32),
-            vmem((inner, TILE), F32),
         ]
+        + [vmem((inner, HALF), F32)] * 2
+        + [vmem((d, HALF), F32)] * 2
+        + [vmem((inner, HALF), F32)] * 2
+        + [vmem((i1, HALF), BF)] * 2
+        + [vmem((d1, HALF), BF)] * 2
         + [vmem((i1, LANES), BF)] * 4
         + [sem((3,)), sem((3,))],
         compiler_params=params(1),
@@ -1013,10 +1108,10 @@
     )(starts, ends, h2e, h2e, h2e, h2e, h2e, x, *ins)
 
     small, large = fixed((inner, LANES)), fixed((d, LANES))
-    sums = [fixed((i1, d)), small, small]
+    sums = [fixed((2, plan.first.pieces, 16, LANES), BF), small, small]
     ins = [kt_d, we_d, wet_d, f3_d, b3_d, g3_d]
-    out, evr_d, dwe_d, dg3_d, db3_d = pl.pallas_call(
-        functools.partial(dec_out_kernel, steps),
+    out, evr_d, packed_first, dg3_d, db3_d = pl.pallas_call(
+        functools.partial(dec_out_kernel, plan),
         grid=(steps,),
         out_shape=[wide(d, F32), wide(inner)] + sums,
         in_specs=[plain.cols(1), plain.cols(1), plain.before(i1), plain.cols(i1), spec(edge_d)]
@@ -1024,68 +1119,73 @@
         + [spec(a) for a in ins],
         out_specs=[plain.cols(d), plain.cols(inner)] + [whole(s.shape) for s in sums],
         scratch_shapes=[
+            vmem((i1, d), F32),
             vmem((DECODER_TAPS * inner + AUG, TILE), BF),
             vmem((inner, LANES), BF),
-            vmem((inner, TILE), F32),
+            vmem((inner, HALF), F32),
+            vmem((inner, HALF), F32),
             vmem((i1, TILE), BF),
             vmem((inner, TILE), BF),
             vmem((inner, TILE), BF),
             vmem((8, TILE), F32),
-            vmem((inner, TILE), F32),
-            vmem((inner, TILE), BF),
-        ],
+        ]
+        + [vmem((inner, HALF), F32)] * 2
+        + [vmem((inner, HALF), BF)] * 2
+        + [vmem((i1, HALF), BF)] * 2,
         compiler_params=params(),
         name="decoder_out",
     )(starts, ends, h2d, h2d, edge_d, cot, x1, *ins)
 
     shapes, specs = outs_of(plain, [(d, BF), (inner, BF)])
     early = fixed((2, plan.early.pieces, 16, LANES), BF)
+    first = fixed((plan.first.pieces, 16, LANES), BF)
     sums = [small, small, large, large, small, small]
     ins = [kb_d, wr_d, we_e, g2_d, g1_d, g3_e]
     stash = [h2d, z2d, d2d, r2d, h1d, z1d, d1d, r1d, cot, h3e, z3e, d3e, r3e]
-    ey, evr_e, packed, dg2_d, db2_d, dg1_d, db1_d, dg3_e, db3_e = pl.pallas_call(
+    ey, evr_e, packed, first_share, dg2_d, db2_d, dg1_d, db1_d, dg3_e, db3_e = pl.pallas_call(
         functools.partial(dec_back_kernel, plan),
         grid=(steps,),
-        out_shape=shapes + [early] + sums,
+        out_shape=shapes + [early, first] + sums,
         in_specs=[plain.cols(1), plain.cols(1), plain.cols(inner), plain.after(inner), head(inner)]
         + [spec(a) for a in ins]
         + [plain.cols(a.shape[0]) for a in stash]
-        + [spec(dwe_d)],
-        out_specs=specs + [whole(early.shape)] + [whole(s.shape) for s in sums],
+        + [spec(packed_first)],
+        out_specs=specs + [whole(early.shape), whole(first.shape)] + [whole(s.shape) for s in sums],
         scratch_shapes=[
             vmem((i1, DECODER_TAPS * inner), F32),
             vmem((inner, d1), F32),
             vmem((i1, d), F32),
             vmem((DECODER_TAPS * inner, TILE), BF),
             vmem((inner, LANES), BF),
-            vmem((inner, TILE), F32),
-            vmem((d, TILE), F32),
-            vmem((inner, TILE), BF),
-            vmem((d, TILE), BF),
-            vmem((inner, LANES), BF),
-            sem((1,)),
-            sem((1,)),
-        ],
+        ]
+        + [vmem((inner, HALF), F32)] * 4
+        + [vmem((d, HALF), F32)] * 2
+        + [vmem((inner, TILE), BF)]
+        + [vmem((inner, HALF), BF)] * 2
+        + [vmem((d, HALF), BF)] * 4
+        + [vmem((inner, HALF), BF)] * 2
+        + [vmem((inner, LANES), BF), sem((1,)), sem((1,))]
+        + Summing.scratch(plan.first),
         compiler_params=params(2),
         name="decoder_back",
-    )(starts, ends, evr_d, evr_d, evr_d, *ins, *stash, dwe_d)
+    )(starts, ends, evr_d, evr_d, evr_d, *ins, *stash, packed_first)
 
     late = fixed((2, plan.late.pieces, 16, LANES), BF)
     early_sum = fixed((plan.early.pieces, 16, LANES), BF)
     ins = [kb_e, wr_e, g2_e, g1_e]
     stash = [h2e, z2e, d2e, r2e, h1e, z1e, d1e, r1e, ey]
     vecs = [dg3_e, db3_e, dg1_d, db1_d, dg2_d, db2_d, dg3_d, db3_d]
-    grad_low, packed_late, summed = pl.pallas_call(
+    grad_low, packed_late, summed, first_whole = pl.pallas_call(
         functools.partial(enc_back_kernel, plan),
         grid=(steps,),
-        out_shape=[wide(d), late, early_sum],
+        out_shape=[wide(d), late, early_sum, first],
         in_specs=[later.cols(1), later.cols(1), later.before(inner), later.cols(inner), later.after(inner)]
         + [head(inner), tail(inner)]
         + [spec(a) for a in ins]
         + [later.cols(a.shape[0]) for a in stash]
-        + [whole(early.shape)]
+        + [whole(early.shape), whole(first.shape)]
         + [spec(a) for a in vecs],
-        out_specs=[later.cols(d), whole(late.shape), whole(early_sum.shape)],
+        out_specs=[later.cols(d), whole(late.shape), whole(early_sum.shape), whole(first.shape)],
         scratch_shapes=[
             vmem((i1, ENCODER_TAPS * inner), F32),
             vmem((inner, d1), F32),
@@ -1096,19 +1196,20 @@
             vmem((ENCODER_TAPS * inner, TILE), BF),
             vmem((inner, LANES), BF),
             vmem((inner, LANES), BF),
-            vmem((inner, TILE), F32),
-            vmem((d, TILE), F32),
-            vmem((inner, TILE), BF),
-            vmem((d, TILE), BF),
-            vmem((inner, LANES), BF),
-            vmem((inner, LANES), BF),
-            sem((2,)),
-            sem((2,)),
         ]
+        + [vmem((inner, HALF), F32)] * 2
+        + [vmem((d, HALF), F32)] * 2
+        + [vmem((inner, TILE), BF)]
+        + [vmem((inner, HALF), BF)] * 2
+        + [vmem((d, HALF), BF)] * 2
+        + [vmem((inner, HALF), BF)] * 2
+        + [vmem((inner, LANES), BF)] * 2
+        + [sem((2,)), sem((2,)), vmem(first.shape, BF)]
+        + Summing.spread_scratch(plan.first)
         + Summing.scratch(plan.early),
         compiler_params=params(3),
         name="encoder_back",
-    )(starts, ends, evr_e, evr_e, evr_e, evr_e, evr_e, *ins, *stash, packed, *vecs)
+    )(starts, ends, evr_e, evr_e, evr_e, evr_e, evr_e, *ins, *stash, packed, first_share, *vecs)
 
     vm = pl.BlockSpec(memory_space=pltpu.VMEM)
     early_whole, late_whole = pl.pallas_call(
@@ -1127,11 +1228,11 @@
         functools.partial(finish_kernel, plan),
         grid=(steps,),
         out_shape=[wide(d, F32)] + [fixed(w.shape) for w in weights],
-        in_specs=[plain.cols(d), whole(early_whole.shape), whole(late_whole.shape)],
+        in_specs=[plain.cols(d), whole(first_whole.shape), whole(early_whole.shape), whole(late_whole.shape)],
         out_specs=[plain.cols(d)] + [whole(w.shape) for w in weights],
         compiler_params=params(),
         name="finish",
-    )(grad_low, early_whole, late_whole)
+    )(grad_low, first_whole, early_whole, late_whole)
     shares = [w.T if at % 12 == 2 else w for at, w in enumerate(shares)]
     return (out.T[None], grad.T[None], *shares)
 

time: 243 us -> 228 us (0.938)
  Pallas kernels: 241 us -> 227 us
    pallas_call x1, Pallas kernels: 17.7 us -> 11.3 us  [gather_weights(): pl.pallas_call(functools.partial(weights_kernel, (d, inner, taps)), out_s...]
    pallas_call x1, Pallas kernels: 40.9 us -> 38.4 us  [local(): pl.pallas_call(functools.partial(enc_out_kernel, steps), grid=(steps,), o...]
where the time goes in v3:
time: 228 us
  Pallas kernels  227 us (100%)
    pallas_call x1, Pallas kernels, local(): pl.pallas_call(functools.partial(sum_kernel, plan), out_shape=[early_sum,...  52.5 us
    pallas_call x1, Pallas kernels, local(): pl.pallas_call(functools.partial(enc_back_kernel, plan), grid=(steps,), o...  40.7 us
    pallas_call x1, Pallas kernels, local(): pl.pallas_call(functools.partial(enc_out_kernel, steps), grid=(steps,), o...  38.4 us
    pallas_call x1, Pallas kernels, local(): pl.pallas_call(functools.partial(dec_back_kernel, plan), grid=(steps,), o...  35.2 us
    pallas_call x1, Pallas kernels, local(): pl.pallas_call(functools.partial(dec_out_kernel, plan), grid=(steps,), ou...  22.8 us
    pallas_call x1, Pallas kernels, local(): pl.pallas_call(enc_in_kernel, grid=(steps,), out_shape=shapes, in_specs=[...  15.4 us
    pallas_call x1, Pallas kernels, gather_weights(): pl.pallas_call(functools.partial(weights_kernel, (d, inner, taps)), out_s...  11.3 us
    pallas_call x1, Pallas kernels, local(): pl.pallas_call(functools.partial(finish_kernel, plan), grid=(steps,), out...  10.9 us

profile of v3, /device:TPU:0, one launch (start us, length us, event | category | flops | bytes accessed | tf_op | source)
XLA Modules:
  0.0 228.0 jit_solution(10333105384777200652)
XLA Ops:
  0.7 11.3 %gather_weights.1 = (bf16[400,816]{1,0:T(8,128)(2,1)}, bf16[400,2016]{1,0:T(8,128)(2,1)}, bf16[800,416]{1,0:T(8,128)(2,1)}, bf16[400,800]{1,0:T(8,128)(2,1)}, bf...) custom-call(bf16[400]{0:T(512)(128)(2,1)} %refs_0_.1, ...), custom_call_target="tpu_custom_call" | custom-call | tf_op jit(solution)/shard_map/gather_weights/pallas_call | solution.py:211
  12.0 15.4 %encoder_in.1 = (bf16[816,3072]{1,0:T(8,128)(2,1)}, bf16[800,3072]{1,0:T(8,128)(2,1)}, bf16[800,3072]{1,0:T(8,128)(2,1)}, f32[8,3072]{1,0:T(8,128)}, bf16[416,30...) custom-call(bf16[800,3072]{1,0:T(8,128)(2,1)} %bitcast.16, ...), custom_call_target="tpu_custom_call" | custom-call | tf_op jit(solution)/shard_map/encoder_in/pallas_call | solution.py:1073
  27.4 38.4 %encoder_out.1 = (bf16[416,3072]{1,0:T(8,128)(2,1)}, bf16[400,3072]{1,0:T(8,128)(2,1)}, bf16[400,3072]{1,0:T(8,128)(2,1)}, f32[8,3072]{1,0:T(8,128)}, bf16[800,3...) custom-call(s32[1,3072]{1,0:T(1,128)} %starts.7, ...), custom_call_target="tpu_custom_call" | custom-call | tf_op jit(solution)/shard_map/encoder_out/pallas_call | solution.py:1086
  65.8 22.8 %decoder_out.1 = (f32[800,3072]{1,0:T(8,128)}, bf16[400,3072]{1,0:T(8,128)(2,1)}, bf16[2,96,16,128]{3,2,1,0:T(8,128)(2,1)}, f32[400,128]{1,0:T(8,128)}, f32[400,128]{1,0:T(8,128)}) custom-call(s32[1,3072]{1,0:T(1,128)} %starts.7, s32[1,3072]{1,0:T(1,128)} %ends.7, bf16[416,3072]{1,0:T(8,128)(2,1)} %get-tuple-element.139.before.main.h2, ...), custom_call_target="tpu_custom_call" | custom-call | tf_op jit(solution)/shard_map/decoder_out/pallas_call | solution.py:1113
  88.6 35.2 %decoder_back.1 = (bf16[800,3072]{1,0:T(8,128)(2,1)}, bf16[400,3072]{1,0:T(8,128)(2,1)}, bf16[2,320,16,128]{3,2,1,0:T(8,128)(2,1)}, bf16[96,16,128]{2,1,0:T(8,12...) custom-call(s32[1,3072]{1,0:T(1,128)} %starts.7, ...), custom_call_target="tpu_custom_call" | custom-call | tf_op jit(solution)/shard_map/decoder_back/pallas_call | solution.py:1145
  123.8 40.7 %encoder_back.1 = (bf16[800,3072]{1,0:T(8,128)(2,1)}, bf16[2,320,16,128]{3,2,1,0:T(8,128)(2,1)}, bf16[320,16,128]{2,1,0:T(8,128)(2,1)}, bf16[96,16,128]{2,1,0:T(8,128)(2,1)}) custom-call(s32[1,3072]{1,0:T(1,128)} %starts.7, s32[1,3072]{1,0:T(1,128)} %ends.7, bf16[400,3072]{1,0:T(8,128)(2,1)} %get-tuple-element.168.before.main.after.head.tail, ...), custom_call_target="tpu_custom_call" | custom-call | tf_op jit(solution)/shard_map/encoder_back/pallas_call | solution.py:1178
  164.4 52.5 %sum_gradients.1 = (bf16[320,16,128]{2,1,0:T(8,128)(2,1)}, bf16[320,16,128]{2,1,0:T(8,128)(2,1)}) custom-call(bf16[2,320,16,128]{3,2,1,0:T(8,128)(2,1)} %get-tuple-element.193.late_given, bf16[320,16,128]{2,1,0:T(8,128)(2,1)} %get-tuple-element.194.early_share), custom_call_target="tpu_custom_call" | custom-call | tf_op jit(solution)/shard_map/sum_gradients/pallas_call | solution.py:1215
  216.9 10.9 %finish.1 = (f32[800,3072]{1,0:T(8,128)}, f32[400]{0:T(512)}, f32[400]{0:T(512)}, f32[200,800]{1,0:T(8,128)}, f32[200]{0:T(256)}, /*index=5*/f32[200]{0:T(256)},...) custom-call(bf16[800,3072]{1,0:T(8,128)(2,1)} %get-tuple-element.191, ...), custom_call_target="tpu_custom_call" | custom-call | tf_op jit(solution)/shard_map/finish/pallas_call | solution.py:1227

commit v4 on v3

--- a/solution.py
+++ b/solution.py
@@ -46,6 +46,13 @@
 
 def nn_dot(left, right):
     return jnp.dot(left, right, preferred_element_type=F32)
+
+
+def product(out, left, right):
+    rows = out.shape[0]
+    middle = (rows // 2 + 15) // 16 * 16
+    for a, b in ((0, middle), (middle, rows)):
+        out[a:b, :] = nn_dot(left[a:b, :], right)
 
 
 def lanes_of(column, width):
@@ -450,7 +457,7 @@
     one, two = CHAINS
 
     def make_v(k):
-        v[k][...] = nn_dot(kt[...], stack[:, CHAINS[k]])
+        product(v[k], kt, stack[:, CHAINS[k]])
 
     def make_y(k):
         y[k][...] = nn_dot(wet[...], h_in[k][...]) + xt[:, CHAINS[k]].astype(F32)
@@ -533,7 +540,7 @@
         h_in[k][inner : inner + AUG, :] = ones_rows(HALF)
         g[k][...] = nn_dot(we[...], cot_t[:, CHAINS[k]])
     for k in range(2):
-        v[k][...] = nn_dot(kt[...], stack[:, CHAINS[k]])
+        product(v[k], kt, stack[:, CHAINS[k]])
     for k in range(2):
         norm_forward(v[k], CHAINS[k], inner, f3, b3, h3, z3, d3, r3, at=EVERY, h_copy=h_in[k])
     products = add_product(dwe, h3, cot_t)
@@ -555,7 +562,7 @@
     steps = plan.steps
     sum_over = Summing(plan.first, given, first, traffic)
     k = sum_over.steps
-    due = [0, 2] + [5 + 6 * i // max(1, k - 1) for i in range(k)]
+    due = [0, 1] + [2 + (i * (steps - 3)) // max(1, k - 1) for i in range(k)]
     hook = hooks(steps, [(place, functools.partial(sum_over.reduce_stage, at)) for at, place in enumerate(due)])
     step = pl.program_id(0)
     d, inner = cot_t.shape[0], ga0.shape[0]
@@ -579,7 +586,7 @@
     def _():
         to_left.wait()
 
-    hook(0)
+    hook(False)
     choose_edge(win_a, after, got, step == steps - 1)
     back = tuple(-s for s in DECODER_SHIFTS)
     stack_taps(stack, back, None, main, win_a, starts, ends, first_place(step, steps), inner)
@@ -606,13 +613,12 @@
         norm_backward(gb[k], CHAINS[k], inner, g3, z3, d3, r3, dg3, db3, keeps[k], emit, fill, EVERY)
 
     for k in range(2):
-        ga[k][...] = nn_dot(kb[...], stack[:, CHAINS[k]])
+        product(ga[k], kb, stack[:, CHAINS[k]])
     by_k = add_product(dk, h2, stack)
     back2(0, by_k[:2])
     big[0][...] = nn_dot(wr[...], eur0[...])
     back2(1, by_k[2:])
     big[1][...] = nn_dot(wr[...], eur1[...])
-    hook(1)
     by_r = add_product(dwrt, eur, h1)
     back1(0, by_r[:2])
     gb[0][...] = nn_dot(we[...], ey0[...])
@@ -626,7 +632,7 @@
     def _():
         pack_gradients(packed, plan, ((dk, dk.shape[1]), (dwrt, d + AUG), (dwe, d)), ())
 
-    hook(2)
+    hook(True)
 
 
 def enc_back_kernel(
@@ -655,7 +661,7 @@
     trade_edges(step, steps, head, tail, got_l, got_r, send, recv, sum_over.partners())
 
     k = sum_over.steps
-    due = [0, 2] + [6 + 6 * i // max(1, k - 1) for i in range(k)]
+    due = [0, 1] + [3 + (i * (steps - 3)) // max(1, k - 1) for i in range(k)]
     actions = [(place, functools.partial(sum_over.reduce_stage, at)) for at, place in enumerate(due)]
     first = Summing(plan.first, None, result, (None,) * 6 + (first_up,))
 
@@ -663,11 +669,11 @@
         first.take_share(first_share)
         first.spread_stage(0)
 
-    actions.append((1, begin))
-    actions += [(3 + 8 * at // k, functools.partial(first.spread_stage, at + 1)) for at in range(k)]
+    actions.append((0, begin))
+    actions += [(1 + (steps - 2) * (at + 1) // k, functools.partial(first.spread_stage, at + 1)) for at in range(k)]
     hook = hooks(steps, actions)
 
-    hook(0)
+    hook(False)
     choose_edge(win_b, before, got_l, step == steps - 1)
     choose_edge(win_a, after, got_r, step == steps - 2)
     back = tuple(-s for s in ENCODER_SHIFTS)
@@ -687,13 +693,12 @@
         norm_backward(big[k], CHAINS[k], d, g1, z1, d1, r1, dg1, db1, kept[k], emit, fill, EVERY)
 
     for k in range(2):
-        ga[k][...] = nn_dot(kb[...], stack[:, CHAINS[k]])
+        product(ga[k], kb, stack[:, CHAINS[k]])
     by_k = add_product(dk, h2, stack)
     back2(0, by_k[:2])
     big[0][...] = nn_dot(wr[...], eur0[...])
     back2(1, by_k[2:4])
     big[1][...] = nn_dot(wr[...], eur1[...])
-    hook(1)
     by_r = add_product(dwrt, eur, h1)
     back1(0, by_k[4:])
     back1(1, by_r)
@@ -704,9 +709,10 @@
         sums = (dg1, db1, dg2, db2, *vecs)
         pack_gradients(packed, plan, ((dk, dk.shape[1]), (dwrt, d + AUG)), sums)
 
-    hook(2)
-
-
+    hook(True)
+
+
+LARGE = (2, 6, 10, 14, 18, 22)
 ROWS_OF = 13
 
 
@@ -728,9 +734,11 @@
         self.per = -(-self.filled // (streams * n)) * n
         self.pieces = streams * self.per
         self.n = n
-        self.bits = []
-        while 1 << len(self.bits) < n:
-            self.bits.append(1 << len(self.bits))
+        self.rounds, base = [], 1
+        while base < n:
+            radix = 4 if n // base == 4 else 2
+            self.rounds.append((base, radix))
+            base *= radix
 
 
 class Plan:
@@ -803,12 +811,11 @@
 def hooks(steps, actions):
     step = pl.program_id(0)
 
-    def hook(at):
+    def hook(end):
         for place, action in actions:
-            where = (place // 2, place % 2) if place < 2 * steps else (steps - 1, 2)
-            if where[1] == at:
-
-                @pl.when(step == where[0])
+            if (place >= steps) == end:
+
+                @pl.when(step == min(place, steps - 1))
                 def _(action=action):
                     action()
 
@@ -822,18 +829,20 @@
         self.up = up[0] if up else None
         self.me = lax.axis_index("wa")
         self.seq = lax.axis_index("seq")
-        self.steps = len(part.bits)
+        self.steps = len(part.rounds)
         self.orders = []
         for s in range(part.streams):
             order = list(range(self.steps))
-            if s % 2 and self.steps > 1:
+            if s % 2 and self.steps > 2:
                 order[0], order[1] = order[1], order[0]
+            if s % 4 > 1 and self.steps > 2:
+                order.insert(1, order.pop())
             self.orders.append(order)
 
     @staticmethod
     def scratch(part):
         sem = pltpu.SemaphoreType.DMA
-        steps = max(1, len(part.bits))
+        steps = max(1, len(part.rounds))
         pieces = (part.pieces, 16, LANES)
         return [
             pltpu.VMEM(pieces, BF),
@@ -841,30 +850,36 @@
             pltpu.VMEM(pieces, BF),
             pltpu.VMEM(pieces, BF),
             sem((2,)),
-            sem((2, steps, part.streams)),
+            sem((2, steps, part.streams, 3)),
         ]
 
     @staticmethod
     def spread_scratch(part):
-        return [pltpu.SemaphoreType.DMA((2, max(1, len(part.bits)), part.streams))]
-
-    def high(self, which):
-        return lax.rem(lax.div(self.seq, self.part.bits[which]), 2)
-
-    def partner(self, which):
-        bit = self.part.bits[which]
-        return {"seq": self.seq + bit - 2 * bit * self.high(which)}
+        return [pltpu.SemaphoreType.DMA((2, max(1, len(part.rounds)), part.streams, 3))]
+
+    def digit(self, which, by=0):
+        base, radix = self.part.rounds[which]
+        return lax.rem(lax.div(self.seq, base) + by, radix)
+
+    def others(self, which):
+        return range(1, self.part.rounds[which][1])
+
+    def peer(self, which, by):
+        base = self.part.rounds[which][0]
+        return {"seq": self.seq + (self.digit(which, by) - self.digit(which)) * base}
 
     def partners(self):
-        return [{"wa": 1 - self.me}] + [self.partner(k) for k in range(self.steps)]
+        peers = [self.peer(which, by) for which in range(self.steps) for by in self.others(which)]
+        return [{"wa": 1 - self.me}, *peers]
 
     def range_at(self, s, k):
         start, size, land = s * self.part.per, self.part.per, s * self.part.per
         for i in range(k):
-            size //= 2
-            start = start + self.high(self.orders[s][i]) * size
+            radix = self.part.rounds[self.orders[s][i]][1]
+            size //= radix
+            start = start + self.digit(self.orders[s][i]) * size
             if i < k - 1:
-                land += size
+                land += (radix - 1) * size
         return start, size, land
 
     def core_copy(self):
@@ -872,54 +887,59 @@
             self.given.at[1 - self.me], self.got, self.core.at[0], self.core.at[1], {"wa": 1 - self.me}
         )
 
-    def down_copy(self, s, k):
-        start, size, _ = self.range_at(s, k)
-        _, half, land = self.range_at(s, k + 1)
+    def down_copy(self, s, k, by):
+        start, _, _ = self.range_at(s, k)
+        _, size, land = self.range_at(s, k + 1)
         which = self.orders[s][k]
-        give = start + (1 - self.high(which)) * half
         return send_copy(
-            self.leave.at[pl.ds(give, half)],
-            self.landed.at[pl.ds(land, half)],
-            self.down.at[0, k, s],
-            self.down.at[1, k, s],
-            self.partner(which),
+            self.leave.at[pl.ds(start + self.digit(which, by) * size, size)],
+            self.landed.at[pl.ds(land + (by - 1) * size, size)],
+            self.down.at[0, k, s, by - 1],
+            self.down.at[1, k, s, by - 1],
+            self.peer(which, by),
         )
 
-    def up_copy(self, s, k):
+    def up_copy(self, s, k, by):
         start, size, _ = self.range_at(s, k + 1)
         ref = self.out.at[pl.ds(start, size)]
-        return send_copy(ref, ref, self.up.at[0, k, s], self.up.at[1, k, s], self.partner(self.orders[s][k]))
+        which = self.orders[s][k]
+        return send_copy(ref, ref, self.up.at[0, k, s, by - 1], self.up.at[1, k, s, by - 1], self.peer(which, by))
 
     def add(self, s, k):
         start, size, land = self.range_at(s, k)
-        last = k == self.steps
 
         def summed(at, count):
             if k == 0:
                 own = self.given[self.me, pl.ds(start + at, count)].astype(F32)
                 return own + self.got[pl.ds(start + at, count)].astype(F32)
-            return self.total[pl.ds(start + at, count)] + self.landed[pl.ds(land + at, count)].astype(F32)
-
-        if last:
+            total = self.total[pl.ds(start + at, count)]
+            for by in self.others(self.orders[s][k - 1]):
+                total = total + self.landed[pl.ds(land + (by - 1) * size + at, count)].astype(F32)
+            return total
+
+        if k == self.steps:
 
             def finish(at, count):
                 self.out[pl.ds(start + at, count)] = summed(at, count).astype(BF)
 
             in_chunks(size, finish)
             return
-        half = size // 2
-        high = self.high(self.orders[s][k])
-        give, keep = (1 - high) * half, high * half
-
-        def to_leave(at, count):
-            self.leave[pl.ds(start + give + at, count)] = summed(give + at, count).astype(BF)
+        which = self.orders[s][k]
+        part = size // self.part.rounds[which][1]
+        for by in self.others(which):
+            give = self.digit(which, by) * part
+
+            def to_leave(at, count, give=give):
+                self.leave[pl.ds(start + give + at, count)] = summed(give + at, count).astype(BF)
+
+            in_chunks(part, to_leave)
+            self.down_copy(s, k, by).start()
+        own = self.digit(which) * part
 
         def to_keep(at, count):
-            self.total[pl.ds(start + keep + at, count)] = summed(keep + at, count)
-
-        in_chunks(half, to_leave)
-        self.down_copy(s, k).start()
-        in_chunks(half, to_keep)
+            self.total[pl.ds(start + own + at, count)] = summed(own + at, count)
+
+        in_chunks(part, to_keep)
 
     def reduce_stage(self, at):
         if at == 0:
@@ -929,15 +949,18 @@
             self.core_copy().wait()
         for s in range(self.part.streams):
             if at > 1:
-                self.down_copy(s, at - 2).wait()
+                for by in self.others(self.orders[s][at - 2]):
+                    self.down_copy(s, at - 2, by).wait()
             self.add(s, at - 1)
 
     def spread_stage(self, at):
         for s in range(self.part.streams):
             if at > 0:
-                self.up_copy(s, self.steps - at).wait()
+                for by in self.others(self.orders[s][self.steps - at]):
+                    self.up_copy(s, self.steps - at, by).wait()
             if at < self.steps:
-                self.up_copy(s, self.steps - at - 1).start()
+                for by in self.others(self.orders[s][self.steps - at - 1]):
+                    self.up_copy(s, self.steps - at - 1, by).start()
 
     def take_share(self, source):
         for s in range(self.part.streams):
@@ -961,7 +984,12 @@
         late.spread_stage(at)
 
 
-def finish_kernel(plan, grad_low, first, early, late, grad, *outs):
+def finish_kernel(plan, grad_low, first, early, late, grad, *rest):
+    results, large, stored = list(rest[:24]), rest[24:30], rest[30]
+    outs, copies = list(results), []
+    for at, place in enumerate(LARGE):
+        outs[place] = large[at]
+        copies.append(pltpu.make_async_copy(large[at], results[place], stored.at[at]))
     d, inner = plan.d, plan.inner
     half = inner // 2
     grad[...] = grad_low[...].astype(F32)
@@ -1013,6 +1041,13 @@
             value = matrix(tag + "_wr")[0:half]
             red_w[...] = value[:, 0:d]
             write(red_b, [value[:, d:].T[0:1]])
+            for copy in copies[3 * side : 3 * side + 3]:
+                copy.start()
+
+    @pl.when(pl.program_id(0) == plan.steps - 1)
+    def _():
+        for copy in copies:
+            copy.wait()
 
 
 def local(n, stream, doc_start, doc_end, cotangent, *weights):
@@ -1229,7 +1264,9 @@
         grid=(steps,),
         out_shape=[wide(d, F32)] + [fixed(w.shape) for w in weights],
         in_specs=[plain.cols(d), whole(first_whole.shape), whole(early_whole.shape), whole(late_whole.shape)],
-        out_specs=[plain.cols(d)] + [whole(w.shape) for w in weights],
+        out_specs=[plain.cols(d)]
+        + [pl.BlockSpec(memory_space=pl.ANY) if at in LARGE else whole(w.shape) for at, w in enumerate(weights)],
+        scratch_shapes=[vmem(weights[at].shape, F32) for at in LARGE] + [sem((len(LARGE),))],
         compiler_params=params(),
         name="finish",
     )(grad_low, first_whole, early_whole, late_whole)

time: 228 us -> 217 us (0.952)
  Pallas kernels: 227 us -> 216 us
    pallas_call x1, Pallas kernels: 52.5 us -> 48.8 us  [local(): pl.pallas_call(functools.partial(sum_kernel, plan), out_shape=[early_sum,...]
where the time goes in v4:
time: 217 us
  Pallas kernels  216 us (100%)
    pallas_call x1, Pallas kernels, local(): pl.pallas_call(functools.partial(sum_kernel, plan), out_shape=[early_sum,...  48.8 us
    pallas_call x1, Pallas kernels, local(): pl.pallas_call(functools.partial(enc_back_kernel, plan), grid=(steps,), o...  38.9 us
    pallas_call x1, Pallas kernels, local(): pl.pallas_call(functools.partial(enc_out_kernel, steps), grid=(steps,), o...  36.6 us
    pallas_call x1, Pallas kernels, local(): pl.pallas_call(functools.partial(dec_back_kernel, plan), grid=(steps,), o...  33.1 us
    pallas_call x1, Pallas kernels, local(): pl.pallas_call(functools.partial(dec_out_kernel, plan), grid=(steps,), ou...  21.1 us
    pallas_call x1, Pallas kernels, local(): pl.pallas_call(enc_in_kernel, grid=(steps,), out_shape=shapes, in_specs=[...  15.4 us
    pallas_call x1, Pallas kernels, gather_weights(): pl.pallas_call(functools.partial(weights_kernel, (d, inner, taps)), out_s...  11.3 us
    pallas_call x1, Pallas kernels, local(): pl.pallas_call(functools.partial(finish_kernel, plan), grid=(steps,), out...  10.9 us

profile of v4, /device:TPU:0, one launch (start us, length us, event | category | flops | bytes accessed | tf_op | source)
XLA Modules:
  0.0 216.9 jit_solution(14494815603424943153)
XLA Ops:
  0.7 11.3 %gather_weights.1 = (bf16[400,816]{1,0:T(8,128)(2,1)}, bf16[400,2016]{1,0:T(8,128)(2,1)}, bf16[800,416]{1,0:T(8,128)(2,1)}, bf16[400,800]{1,0:T(8,128)(2,1)}, bf...) custom-call(bf16[400]{0:T(512)(128)(2,1)} %refs_0_.1, ...), custom_call_target="tpu_custom_call" | custom-call | tf_op jit(solution)/shard_map/gather_weights/pallas_call | solution.py:218
  12.0 15.4 %encoder_in.1 = (bf16[816,3072]{1,0:T(8,128)(2,1)}, bf16[800,3072]{1,0:T(8,128)(2,1)}, bf16[800,3072]{1,0:T(8,128)(2,1)}, f32[8,3072]{1,0:T(8,128)}, bf16[416,30...) custom-call(bf16[800,3072]{1,0:T(8,128)(2,1)} %bitcast.16, ...), custom_call_target="tpu_custom_call" | custom-call | tf_op jit(solution)/shard_map/encoder_in/pallas_call | solution.py:1108
  27.4 36.6 %encoder_out.1 = (bf16[416,3072]{1,0:T(8,128)(2,1)}, bf16[400,3072]{1,0:T(8,128)(2,1)}, bf16[400,3072]{1,0:T(8,128)(2,1)}, f32[8,3072]{1,0:T(8,128)}, bf16[800,3...) custom-call(s32[1,3072]{1,0:T(1,128)} %starts.7, ...), custom_call_target="tpu_custom_call" | custom-call | tf_op jit(solution)/shard_map/encoder_out/pallas_call | solution.py:1121
  64.0 21.1 %decoder_out.1 = (f32[800,3072]{1,0:T(8,128)}, bf16[400,3072]{1,0:T(8,128)(2,1)}, bf16[2,96,16,128]{3,2,1,0:T(8,128)(2,1)}, f32[400,128]{1,0:T(8,128)}, f32[400,128]{1,0:T(8,128)}) custom-call(s32[1,3072]{1,0:T(1,128)} %starts.7, s32[1,3072]{1,0:T(1,128)} %ends.7, bf16[416,3072]{1,0:T(8,128)(2,1)} %get-tuple-element.139.before.main.h2, ...), custom_call_target="tpu_custom_call" | custom-call | tf_op jit(solution)/shard_map/decoder_out/pallas_call | solution.py:1148
  85.0 33.1 %decoder_back.1 = (bf16[800,3072]{1,0:T(8,128)(2,1)}, bf16[400,3072]{1,0:T(8,128)(2,1)}, bf16[2,320,16,128]{3,2,1,0:T(8,128)(2,1)}, bf16[96,16,128]{2,1,0:T(8,12...) custom-call(s32[1,3072]{1,0:T(1,128)} %starts.7, ...), custom_call_target="tpu_custom_call" | custom-call | tf_op jit(solution)/shard_map/decoder_back/pallas_call | solution.py:1180
  118.2 38.9 %encoder_back.1 = (bf16[800,3072]{1,0:T(8,128)(2,1)}, bf16[2,320,16,128]{3,2,1,0:T(8,128)(2,1)}, bf16[320,16,128]{2,1,0:T(8,128)(2,1)}, bf16[96,16,128]{2,1,0:T(8,128)(2,1)}) custom-call(s32[1,3072]{1,0:T(1,128)} %starts.7, s32[1,3072]{1,0:T(1,128)} %ends.7, bf16[400,3072]{1,0:T(8,128)(2,1)} %get-tuple-element.168.before.main.after.head.tail, ...), custom_call_target="tpu_custom_call" | custom-call | tf_op jit(solution)/shard_map/encoder_back/pallas_call | solution.py:1213
  157.0 48.8 %sum_gradients.1 = (bf16[320,16,128]{2,1,0:T(8,128)(2,1)}, bf16[320,16,128]{2,1,0:T(8,128)(2,1)}) custom-call(bf16[2,320,16,128]{3,2,1,0:T(8,128)(2,1)} %get-tuple-element.193.late_given, bf16[320,16,128]{2,1,0:T(8,128)(2,1)} %get-tuple-element.194.early_share), custom_call_target="tpu_custom_call" | custom-call | tf_op jit(solution)/shard_map/sum_gradients/pallas_call | solution.py:1250
  205.9 10.9 %finish.1 = (f32[800,3072]{1,0:T(8,128)}, f32[400]{0:T(512)}, f32[400]{0:T(512)}, f32[200,800]{1,0:T(8,128)}, f32[200]{0:T(256)}, /*index=5*/f32[200]{0:T(256)},...) custom-call(bf16[800,3072]{1,0:T(8,128)(2,1)} %get-tuple-element.191, ...), custom_call_target="tpu_custom_call" | custom-call | tf_op jit(solution)/shard_map/finish/pallas_call | solution.py:1262

commit v5 on v4

--- a/solution.py
+++ b/solution.py
@@ -48,11 +48,12 @@
     return jnp.dot(left, right, preferred_element_type=F32)
 
 
-def product(out, left, right):
+def product(out, left, right, extra=None):
     rows = out.shape[0]
     middle = (rows // 2 + 15) // 16 * 16
     for a, b in ((0, middle), (middle, rows)):
-        out[a:b, :] = nn_dot(left[a:b, :], right)
+        value = nn_dot(left[a:b, :], right)
+        out[a:b, :] = value if extra is None else value + extra[a:b, :].astype(F32)
 
 
 def lanes_of(column, width):
@@ -408,7 +409,7 @@
     for k in range(2):
         h_wide[k][d : d + AUG, :] = ones_rows(HALF)
         norm_forward(x, CHAINS[k], d, g1, b1, h1, z1, d1, r1, xt, h_copy=h_wide[k])
-        u[k][...] = nn_dot(wrt[...], h_wide[k][...])
+        product(u[k], wrt, h_wide[k][...])
     for k in range(2):
         norm_forward(u[k], CHAINS[k], inner, g2, b2, h2, z2, d2, r2, at=EVERY)
 
@@ -460,10 +461,10 @@
         product(v[k], kt, stack[:, CHAINS[k]])
 
     def make_y(k):
-        y[k][...] = nn_dot(wet[...], h_in[k][...]) + xt[:, CHAINS[k]].astype(F32)
+        product(y[k], wet, h_in[k][...], xt[:, CHAINS[k]])
 
     def make_u(k):
-        u[k][...] = nn_dot(wrt[...], h_wide[k][...])
+        product(u[k], wrt, h_wide[k][...])
 
     def norm_last(k):
         norm_forward(v[k], CHAINS[k], inner, g3, b3, h3, z3, d3, r3, at=EVERY, h_copy=h_in[k])
@@ -644,8 +645,10 @@
         grad, packed, summed, first_whole,
         dk, dwrt, dg2, db2, dg1, db1,
         stack, win_b, win_a, ga0, ga1, big0, big1, eur, eur0, eur1, kept0, kept1, keeps0, keeps1,
-        got_l, got_r, send, recv, result, first_up,
-    ), traffic = rest[:30], rest[30:]
+        got_l, got_r, send, recv, result, first_up, first_sem, vec_sem,
+    ), rest = rest[:32], rest[32:]
+    held, traffic = rest[:8], rest[8:]
+    loads = [pltpu.make_async_copy(vecs[at], held[at], vec_sem.at[at]) for at in range(8)]
     steps = plan.steps
     step = pl.program_id(0)
     d, inner = ey.shape[0], ga0.shape[0]
@@ -654,6 +657,8 @@
 
     @pl.when(step == 0)
     def _():
+        for load in loads:
+            load.start()
         for ref in (dk, dwrt, dg2, db2, dg1, db1):
             ref[...] = jnp.zeros_like(ref)
 
@@ -663,7 +668,7 @@
     k = sum_over.steps
     due = [0, 1] + [3 + (i * (steps - 3)) // max(1, k - 1) for i in range(k)]
     actions = [(place, functools.partial(sum_over.reduce_stage, at)) for at, place in enumerate(due)]
-    first = Summing(plan.first, None, result, (None,) * 6 + (first_up,))
+    first = Summing(plan.first, None, result, (None,) * 8 + (first_up, first_sem))
 
     def begin():
         first.take_share(first_share)
@@ -706,7 +711,9 @@
     @pl.when(step == steps - 1)
     def _():
         in_chunks(plan.first.pieces, lambda at, count: copy_pieces(first_whole, result, at, count))
-        sums = (dg1, db1, dg2, db2, *vecs)
+        for load in loads:
+            load.wait()
+        sums = (dg1, db1, dg2, db2, *held)
         pack_gradients(packed, plan, ((dk, dk.shape[1]), (dwrt, d + AUG)), sums)
 
     hook(True)
@@ -825,8 +832,8 @@
 class Summing:
     def __init__(self, part, given, out, traffic):
         self.part, self.given, self.out = part, given, out
-        self.got, self.total, self.leave, self.landed, self.core, self.down, *up = traffic
-        self.up = up[0] if up else None
+        self.got, self.total, self.leave, self.landed, self.core, self.down, self.own, self.own_sem, *up = traffic
+        self.up, self.share_sem = up if up else (None, None)
         self.me = lax.axis_index("wa")
         self.seq = lax.axis_index("seq")
         self.steps = len(part.rounds)
@@ -851,11 +858,16 @@
             pltpu.VMEM(pieces, BF),
             sem((2,)),
             sem((2, steps, part.streams, 3)),
+            pltpu.VMEM(pieces, BF),
+            sem((1,)),
         ]
 
     @staticmethod
     def spread_scratch(part):
-        return [pltpu.SemaphoreType.DMA((2, max(1, len(part.rounds)), part.streams, 3))]
+        return [
+            pltpu.SemaphoreType.DMA((2, max(1, len(part.rounds)), part.streams, 3)),
+            pltpu.SemaphoreType.DMA((part.streams,)),
+        ]
 
     def digit(self, which, by=0):
         base, radix = self.part.rounds[which]
@@ -886,6 +898,9 @@
         return send_copy(
             self.given.at[1 - self.me], self.got, self.core.at[0], self.core.at[1], {"wa": 1 - self.me}
         )
+
+    def own_copy(self):
+        return pltpu.make_async_copy(self.given.at[self.me], self.own, self.own_sem.at[0])
 
     def down_copy(self, s, k, by):
         start, _, _ = self.range_at(s, k)
@@ -910,7 +925,7 @@
 
         def summed(at, count):
             if k == 0:
-                own = self.given[self.me, pl.ds(start + at, count)].astype(F32)
+                own = self.own[pl.ds(start + at, count)].astype(F32)
                 return own + self.got[pl.ds(start + at, count)].astype(F32)
             total = self.total[pl.ds(start + at, count)]
             for by in self.others(self.orders[s][k - 1]):
@@ -944,9 +959,11 @@
     def reduce_stage(self, at):
         if at == 0:
             self.core_copy().start()
+            self.own_copy().start()
             return
         if at == 1:
             self.core_copy().wait()
+            self.own_copy().wait()
         for s in range(self.part.streams):
             if at > 1:
                 for by in self.others(self.orders[s][at - 2]):
@@ -963,14 +980,19 @@
                     self.up_copy(s, self.steps - at - 1, by).start()
 
     def take_share(self, source):
+        copies = []
         for s in range(self.part.streams):
             start, size, _ = self.range_at(s, self.steps)
-            in_chunks(size, lambda at, count, start=start: copy_pieces(self.out, source, start + at, count))
+            where = pl.ds(start, size)
+            copies.append(pltpu.make_async_copy(source.at[where], self.out.at[where], self.share_sem.at[s]))
+            copies[-1].start()
+        for copy in copies:
+            copy.wait()
 
 
 def sum_kernel(plan, late_given, early_share, early_out, late_out, *traffic):
-    late = Summing(plan.late, late_given, late_out, traffic[:7])
-    early = Summing(plan.early, None, early_out, (None,) * 6 + traffic[7:])
+    late = Summing(plan.late, late_given, late_out, traffic[:10])
+    early = Summing(plan.early, None, early_out, (None,) * 8 + traffic[10:])
     steps = late.steps
     greet(late.partners())
     late.reduce_stage(0)
@@ -1099,6 +1121,7 @@
     norm_in = [(i1, BF), (inner, BF), (inner, BF), (8, F32)]
     sem = pltpu.SemaphoreType.DMA
     vmem = pltpu.VMEM
+    anywhere = pl.BlockSpec(memory_space=pl.ANY)
 
     def outs_of(order, items):
         return [wide(c, t) for c, t in items], [order.cols(c) for c, _ in items]
@@ -1184,7 +1207,7 @@
         in_specs=[plain.cols(1), plain.cols(1), plain.cols(inner), plain.after(inner), head(inner)]
         + [spec(a) for a in ins]
         + [plain.cols(a.shape[0]) for a in stash]
-        + [spec(packed_first)],
+        + [anywhere],
         out_specs=specs + [whole(early.shape), whole(first.shape)] + [whole(s.shape) for s in sums],
         scratch_shapes=[
             vmem((i1, DECODER_TAPS * inner), F32),
@@ -1218,8 +1241,7 @@
         + [head(inner), tail(inner)]
         + [spec(a) for a in ins]
         + [later.cols(a.shape[0]) for a in stash]
-        + [whole(early.shape), whole(first.shape)]
-        + [spec(a) for a in vecs],
+        + [anywhere] * (2 + len(vecs)),
         out_specs=[later.cols(d), whole(late.shape), whole(early_sum.shape), whole(first.shape)],
         scratch_shapes=[
             vmem((i1, ENCODER_TAPS * inner), F32),
@@ -1241,6 +1263,8 @@
         + [vmem((inner, LANES), BF)] * 2
         + [sem((2,)), sem((2,)), vmem(first.shape, BF)]
         + Summing.spread_scratch(plan.first)
+        + [sem((8,))]
+        + [vmem(a.shape, F32) for a in vecs]
         + Summing.scratch(plan.early),
         compiler_params=params(3),
         name="encoder_back",
@@ -1250,7 +1274,7 @@
     early_whole, late_whole = pl.pallas_call(
         functools.partial(sum_kernel, plan),
         out_shape=[early_sum, fixed((plan.late.pieces, 16, LANES), BF)],
-        in_specs=[vm, vm],
+        in_specs=[anywhere, anywhere],
         out_specs=[vm, vm],
         scratch_shapes=Summing.scratch(plan.late)
         + Summing.spread_scratch(plan.late)

time: 217 us -> 215 us (level)
  no operation moved by 1% of the time
where the time goes in v5:
time: 215 us
  Pallas kernels  214 us (100%)
    pallas_call x1, Pallas kernels, local(): pl.pallas_call(functools.partial(sum_kernel, plan), out_shape=[early_sum,...  48.3 us
    pallas_call x1, Pallas kernels, local(): pl.pallas_call(functools.partial(enc_back_kernel, plan), grid=(steps,), o...  38.3 us
    pallas_call x1, Pallas kernels, local(): pl.pallas_call(functools.partial(enc_out_kernel, steps), grid=(steps,), o...  35.8 us
    pallas_call x1, Pallas kernels, local(): pl.pallas_call(functools.partial(dec_back_kernel, plan), grid=(steps,), o...  33 us
    pallas_call x1, Pallas kernels, local(): pl.pallas_call(functools.partial(dec_out_kernel, plan), grid=(steps,), ou...  21.1 us
    pallas_call x1, Pallas kernels, local(): pl.pallas_call(enc_in_kernel, grid=(steps,), out_shape=shapes, in_specs=[...  15.3 us
    pallas_call x1, Pallas kernels, gather_weights(): pl.pallas_call(functools.partial(weights_kernel, (d, inner, taps)), out_s...  11.3 us
    pallas_call x1, Pallas kernels, local(): pl.pallas_call(functools.partial(finish_kernel, plan), grid=(steps,), out...  10.9 us

profile of v5, /device:TPU:0, one launch (start us, length us, event | category | flops | bytes accessed | tf_op | source)
XLA Modules:
  0.0 214.9 jit_solution(6358419239582941172)
XLA Ops:
  0.7 11.3 %gather_weights.1 = (bf16[400,816]{1,0:T(8,128)(2,1)}, bf16[400,2016]{1,0:T(8,128)(2,1)}, bf16[800,416]{1,0:T(8,128)(2,1)}, bf16[400,800]{1,0:T(8,128)(2,1)}, bf...) custom-call(bf16[400]{0:T(512)(128)(2,1)} %refs_0_.1, ...), custom_call_target="tpu_custom_call" | custom-call | tf_op jit(solution)/shard_map/gather_weights/pallas_call | solution.py:219
  12.0 15.3 %encoder_in.1 = (bf16[816,3072]{1,0:T(8,128)(2,1)}, bf16[800,3072]{1,0:T(8,128)(2,1)}, bf16[800,3072]{1,0:T(8,128)(2,1)}, f32[8,3072]{1,0:T(8,128)}, bf16[416,30...) custom-call(bf16[800,3072]{1,0:T(8,128)(2,1)} %bitcast.16, ...), custom_call_target="tpu_custom_call" | custom-call | tf_op jit(solution)/shard_map/encoder_in/pallas_call | solution.py:1131
  27.3 35.8 %encoder_out.1 = (bf16[416,3072]{1,0:T(8,128)(2,1)}, bf16[400,3072]{1,0:T(8,128)(2,1)}, bf16[400,3072]{1,0:T(8,128)(2,1)}, f32[8,3072]{1,0:T(8,128)}, bf16[800,3...) custom-call(s32[1,3072]{1,0:T(1,128)} %starts.7, ...), custom_call_target="tpu_custom_call" | custom-call | tf_op jit(solution)/shard_map/encoder_out/pallas_call | solution.py:1144
  63.2 21.1 %decoder_out.1 = (f32[800,3072]{1,0:T(8,128)}, bf16[400,3072]{1,0:T(8,128)(2,1)}, bf16[2,96,16,128]{3,2,1,0:T(8,128)(2,1)}, f32[400,128]{1,0:T(8,128)}, f32[400,128]{1,0:T(8,128)}) custom-call(s32[1,3072]{1,0:T(1,128)} %starts.7, s32[1,3072]{1,0:T(1,128)} %ends.7, bf16[416,3072]{1,0:T(8,128)(2,1)} %get-tuple-element.139.before.main.h2, ...), custom_call_target="tpu_custom_call" | custom-call | tf_op jit(solution)/shard_map/decoder_out/pallas_call | solution.py:1171
  84.2 33.0 %decoder_back.1 = (bf16[800,3072]{1,0:T(8,128)(2,1)}, bf16[400,3072]{1,0:T(8,128)(2,1)}, bf16[2,320,16,128]{3,2,1,0:T(8,128)(2,1)}, bf16[96,16,128]{2,1,0:T(8,12...) custom-call(s32[1,3072]{1,0:T(1,128)} %starts.7, ...), custom_call_target="tpu_custom_call" | custom-call | tf_op jit(solution)/shard_map/decoder_back/pallas_call | solution.py:1203
  117.2 38.3 %encoder_back.1 = (bf16[800,3072]{1,0:T(8,128)(2,1)}, bf16[2,320,16,128]{3,2,1,0:T(8,128)(2,1)}, bf16[320,16,128]{2,1,0:T(8,128)(2,1)}, bf16[96,16,128]{2,1,0:T(8,128)(2,1)}) custom-call(s32[1,3072]{1,0:T(1,128)} %starts.7, s32[1,3072]{1,0:T(1,128)} %ends.7, bf16[400,3072]{1,0:T(8,128)(2,1)} %get-tuple-element.168.before.main.after.head.tail, ...), custom_call_target="tpu_custom_call" | custom-call | tf_op jit(solution)/shard_map/encoder_back/pallas_call | solution.py:1236
  155.6 48.3 %sum_gradients.1 = (bf16[320,16,128]{2,1,0:T(8,128)(2,1)}, bf16[320,16,128]{2,1,0:T(8,128)(2,1)}) custom-call(bf16[2,320,16,128]{3,2,1,0:T(8,128)(2,1)} %get-tuple-element.193.late_given, bf16[320,16,128]{2,1,0:T(8,128)(2,1)} %get-tuple-element.194.early_share), custom_call_target="tpu_custom_call" | custom-call | tf_op jit(solution)/shard_map/sum_gradients/pallas_call | solution.py:1274
  203.8 10.9 %finish.1 = (f32[800,3072]{1,0:T(8,128)}, f32[400]{0:T(512)}, f32[400]{0:T(512)}, f32[200,800]{1,0:T(8,128)}, f32[200]{0:T(256)}, /*index=5*/f32[200]{0:T(256)},...) custom-call(bf16[800,3072]{1,0:T(8,128)(2,1)} %get-tuple-element.191, ...), custom_call_target="tpu_custom_call" | custom-call | tf_op jit(solution)/shard_map/finish/pallas_call | solution.py:1286

commit v6 on v5

--- a/solution.py
+++ b/solution.py
@@ -290,10 +290,11 @@
         sq = half * half
         t = jnp.tanh(half * (sq * BF(GELU_3) + BF(GELU_1)))
         up = one + t
-        h_out[rows, lanes] = half * up
+        h = half * up
+        h_out[rows, lanes] = h
         if h_copy is not None:
-            h_copy[rows, :] = half * up
-        d_out[rows, lanes] = up * (point + half * (sq * BF(1.5 * GELU_3) + BF(0.5 * GELU_1)) * (one - t))
+            h_copy[rows, :] = h
+        d_out[rows, lanes] = point * up + h * ((one - t) * (sq * BF(1.5 * GELU_3) + BF(0.5 * GELU_1)))
         z_out[rows, lanes] = z.astype(BF)
 
 

time: 215 us -> 216 us (level)
  no operation moved by 1% of the time
where the time goes in v6:
time: 216 us; the launch traced here: 215 us
  Pallas kernels  214 us (99%)
    pallas_call x1, Pallas kernels, local(): pl.pallas_call(functools.partial(sum_kernel, plan), out_shape=[early_sum,...  48.3 us
    pallas_call x1, Pallas kernels, local(): pl.pallas_call(functools.partial(enc_back_kernel, plan), grid=(steps,), o...  38.4 us
    pallas_call x1, Pallas kernels, local(): pl.pallas_call(functools.partial(enc_out_kernel, steps), grid=(steps,), o...  36.3 us
    pallas_call x1, Pallas kernels, local(): pl.pallas_call(functools.partial(dec_back_kernel, plan), grid=(steps,), o...  32.9 us
    pallas_call x1, Pallas kernels, local(): pl.pallas_call(functools.partial(dec_out_kernel, plan), grid=(steps,), ou...  21.2 us
    pallas_call x1, Pallas kernels, local(): pl.pallas_call(enc_in_kernel, grid=(steps,), out_shape=shapes, in_specs=[...  15.2 us
    pallas_call x1, Pallas kernels, gather_weights(): pl.pallas_call(functools.partial(weights_kernel, (d, inner, taps)), out_s...  11.3 us
    pallas_call x1, Pallas kernels, local(): pl.pallas_call(functools.partial(finish_kernel, plan), grid=(steps,), out...  10.9 us

profile of v6, /device:TPU:0, one launch (start us, length us, event | category | flops | bytes accessed | tf_op | source)
XLA Modules:
  0.0 215.4 jit_solution(11931599902659455304)
XLA Ops:
  0.7 11.3 %gather_weights.1 = (bf16[400,816]{1,0:T(8,128)(2,1)}, bf16[400,2016]{1,0:T(8,128)(2,1)}, bf16[800,416]{1,0:T(8,128)(2,1)}, bf16[400,800]{1,0:T(8,128)(2,1)}, bf...) custom-call(bf16[400]{0:T(512)(128)(2,1)} %refs_0_.1, ...), custom_call_target="tpu_custom_call" | custom-call | tf_op jit(solution)/shard_map/gather_weights/pallas_call | solution.py:219
  12.0 15.2 %encoder_in.1 = (bf16[816,3072]{1,0:T(8,128)(2,1)}, bf16[800,3072]{1,0:T(8,128)(2,1)}, bf16[800,3072]{1,0:T(8,128)(2,1)}, f32[8,3072]{1,0:T(8,128)}, bf16[416,30...) custom-call(bf16[800,3072]{1,0:T(8,128)(2,1)} %bitcast.16, ...), custom_call_target="tpu_custom_call" | custom-call | tf_op jit(solution)/shard_map/encoder_in/pallas_call | solution.py:1132
  27.2 36.3 %encoder_out.1 = (bf16[416,3072]{1,0:T(8,128)(2,1)}, bf16[400,3072]{1,0:T(8,128)(2,1)}, bf16[400,3072]{1,0:T(8,128)(2,1)}, f32[8,3072]{1,0:T(8,128)}, bf16[800,3...) custom-call(s32[1,3072]{1,0:T(1,128)} %starts.7, ...), custom_call_target="tpu_custom_call" | custom-call | tf_op jit(solution)/shard_map/encoder_out/pallas_call | solution.py:1145
  63.5 21.2 %decoder_out.1 = (f32[800,3072]{1,0:T(8,128)}, bf16[400,3072]{1,0:T(8,128)(2,1)}, bf16[2,96,16,128]{3,2,1,0:T(8,128)(2,1)}, f32[400,128]{1,0:T(8,128)}, f32[400,128]{1,0:T(8,128)}) custom-call(s32[1,3072]{1,0:T(1,128)} %starts.7, s32[1,3072]{1,0:T(1,128)} %ends.7, bf16[416,3072]{1,0:T(8,128)(2,1)} %get-tuple-element.139.before.main.h2, ...), custom_call_target="tpu_custom_call" | custom-call | tf_op jit(solution)/shard_map/decoder_out/pallas_call | solution.py:1172
  84.7 32.9 %decoder_back.1 = (bf16[800,3072]{1,0:T(8,128)(2,1)}, bf16[400,3072]{1,0:T(8,128)(2,1)}, bf16[2,320,16,128]{3,2,1,0:T(8,128)(2,1)}, bf16[96,16,128]{2,1,0:T(8,12...) custom-call(s32[1,3072]{1,0:T(1,128)} %starts.7, ...), custom_call_target="tpu_custom_call" | custom-call | tf_op jit(solution)/shard_map/decoder_back/pallas_call | solution.py:1204
  117.7 38.4 %encoder_back.1 = (bf16[800,3072]{1,0:T(8,128)(2,1)}, bf16[2,320,16,128]{3,2,1,0:T(8,128)(2,1)}, bf16[320,16,128]{2,1,0:T(8,128)(2,1)}, bf16[96,16,128]{2,1,0:T(8,128)(2,1)}) custom-call(s32[1,3072]{1,0:T(1,128)} %starts.7, s32[1,3072]{1,0:T(1,128)} %ends.7, bf16[400,3072]{1,0:T(8,128)(2,1)} %get-tuple-element.168.before.main.after.head.tail, ...), custom_call_target="tpu_custom_call" | custom-call | tf_op jit(solution)/shard_map/encoder_back/pallas_call | solution.py:1237
  156.0 48.3 %sum_gradients.1 = (bf16[320,16,128]{2,1,0:T(8,128)(2,1)}, bf16[320,16,128]{2,1,0:T(8,128)(2,1)}) custom-call(bf16[2,320,16,128]{3,2,1,0:T(8,128)(2,1)} %get-tuple-element.193.late_given, bf16[320,16,128]{2,1,0:T(8,128)(2,1)} %get-tuple-element.194.early_share), custom_call_target="tpu_custom_call" | custom-call | tf_op jit(solution)/shard_map/sum_gradients/pallas_call | solution.py:1275
  204.3 10.9 %finish.1 = (f32[800,3072]{1,0:T(8,128)}, f32[400]{0:T(512)}, f32[400]{0:T(512)}, f32[200,800]{1,0:T(8,128)}, f32[200]{0:T(256)}, /*index=5*/f32[200]{0:T(256)},...) custom-call(bf16[800,3072]{1,0:T(8,128)(2,1)} %get-tuple-element.191, ...), custom_call_target="tpu_custom_call" | custom-call | tf_op jit(solution)/shard_map/finish/pallas_call | solution.py:1287
